TPU v7x, 32 devices: a whole 2x2x4 slice. The times are simulated.
32 devices in a mesh: groups: 2 (over y), rows: 4 (over z), tm: 4 (over x, core).
Axes of the slice: x: 2, y: 2, z: 4, core: 2. Of those that a mesh axis runs over, the one named last changes fastest.
Arguments:
- video: bfloat16 [2, 16, 8, 96, 128], P('groups', 'tm', 'rows'), parts along dimension 0, may hold values from -6 to 6
- gamma_first: float32 [96], replicated, may hold values from 0.25 to 1.75
- kernel_first: bfloat16 [96, 2592], replicated, may hold values from -0.125 to 0.125
- bias_first: float32 [96], replicated, may hold values from -3 to 3
- gamma_second: float32 [96], replicated, may hold values from 0.25 to 1.75
- kernel_second: bfloat16 [96, 2592], replicated, may hold values from -0.125 to 0.125
- bias_second: float32 [96], replicated, may hold values from -3 to 3
Outputs:
- encoded: bfloat16 [2, 16, 8, 96, 128], P('groups', 'tm', 'rows'), parts along dimension 0
There are 2 independent parts, one for each index of `groups`. A program takes and returns all parts, laid end to end along the dimension named above; an argument that names none is the same for every part. Nothing has to cross between parts.
All inputs are finite; a program needn't handle non-finite values.
Results may differ from a plain program's by a relative error of at most 0.0036.
Values may be sent and summed in bfloat16 or wider, within the bound.
No kernel may reach another device: no remote copies, remote signals or barrier semaphores. Data moves between devices by JAX's collectives and lax.ppermute only.
A program may use at most 64 MiB of HBM per device.

v0:
```python
import jax
import jax.numpy as jnp
from jax import lax
from jax.sharding import PartitionSpec as P

epsilon = 1e-06


def passed_along(block, axis, distance):
    devices = range(lax.axis_size(axis))
    route = [(i - distance, i) for i in devices if i - distance in devices]
    return lax.ppermute(block, axis, route)


def padded_2(cells, sides, width):
    for axis, dim in sides:
        count = lax.axis_size(axis)
        ends = count - 1
        head = lax.slice_in_dim(cells, 0, width, axis=dim)
        tail = lax.slice_in_dim(cells, cells.shape[dim] - width, cells.shape[dim], axis=dim)
        cells = jnp.concatenate(
            [
                lax.ppermute(tail, axis, [(i, (i + 1) % count) for i in range(ends)]),
                cells,
                lax.ppermute(head, axis, [((i + 1) % count, i) for i in range(ends)]),
            ],
            axis=dim,
        )
    return cells


def norm_silu(values, gain):
    meansq = jnp.mean(values * values, axis=3, keepdims=True)
    scaled = values * lax.rsqrt(meansq + epsilon) * gain[:, None]
    return jax.nn.silu(scaled)


def conv_valid(extended, kernel, offset):
    chans = extended.shape[3]
    width = extended.shape[4]
    out_frames = extended.shape[1] - 2
    out_rows = extended.shape[2] - 2
    padded = jnp.pad(extended, ((0, 0), (0, 0), (0, 0), (0, 0), (1, 1)))
    summed = jnp.zeros((extended.shape[0], out_frames, out_rows, chans, width), jnp.float32)
    for frame_off in range(3):
        for row_off in range(3):
            section = padded[:, frame_off : frame_off + out_frames, row_off : row_off + out_rows]
            stacked = jnp.concatenate(
                [section[..., 0:width], section[..., 1 : width + 1], section[..., 2 : width + 2]],
                axis=3,
            )
            start = (frame_off * 3 + row_off) * 3 * chans
            columns = kernel[:, start : start + 3 * chans]
            summed = summed + jnp.einsum(
                "oc,bfrcw->bfrow", columns, stacked, preferred_element_type=jnp.float32
            )
    return summed + offset[:, None]


def local(video, gamma_first, kernel_first, bias_first, gamma_second, kernel_second, bias_second):
    frames = video.shape[1]
    tile_rows = video.shape[2]
    prior = passed_along(video, "tm", 1)
    joined = jnp.concatenate([prior, video], axis=1)
    margin = padded_2(joined, (("rows", 2),), 2)
    first = norm_silu(margin.astype(jnp.float32), gamma_first).astype(jnp.bfloat16)
    hidden = conv_valid(first, kernel_first, bias_first)
    second = norm_silu(hidden, gamma_second).astype(jnp.bfloat16)
    frame_pos = jnp.arange(frames + 2, dtype=jnp.int32) - 2 + lax.axis_index("tm") * frames
    row_pos = jnp.arange(tile_rows + 2, dtype=jnp.int32) - 1 + lax.axis_index("rows") * tile_rows
    row_limit = tile_rows * lax.axis_size("rows")
    inside = (frame_pos >= 0)[:, None] & ((row_pos >= 0) & (row_pos < row_limit))[None, :]
    second = jnp.where(inside[None, :, :, None, None], second, jnp.zeros_like(second))
    result = conv_valid(second, kernel_second, bias_second)
    return (video.astype(jnp.float32) + result).astype(jnp.bfloat16)


def solution(mesh):
    in_specs = (P("groups", "tm", "rows", None, None), P(), P(), P(), P(), P(), P())
    out_specs = P("groups", "tm", "rows", None, None)
    return jax.shard_map(local, mesh=mesh, in_specs=in_specs, out_specs=out_specs, check_vma=False)
```

profile of v0, /device:TPU:1, one launch (start us, length us, event | category | flops | bytes accessed | tf_op | source)
XLA Modules:
  0.0 39.6 jit_solution(17630420195884164558)
XLA Ops:
  0.0 0.0 copy-start.2
  0.0 4.6 %collective-permute-start = (bf16[1,4,2,96,128]{4,3,2,1,0:T(8,128)(2,1)}, bf16[1,4,2,96,128]{4,3,2,1,0:T(8,128)(2,1)S(1)}, u32[]{:S(2)}, u32[]{:S(2)}) collective-permute-start(bf16[1,4,2,96,128]{4,3,2,1,0:T(8,128)(2,1)} %param.7), channel_id=1, source_target_pairs={{0,1},{1,2},{2,3},{4,5},{5,6},{6,7},{8,9},{9,10},{10,11},{12,13},{... | collective-permute-start | bytes 589832 | tf_op jit(solution)/shard_map/ppermute | solution.py:12
  4.6 2.9 %collective-permute-done = bf16[1,4,2,96,128]{4,3,2,1,0:T(8,128)(2,1)S(1)} collective-permute-done((bf16[1,4,2,96,128]{4,3,2,1,0:T(8,128)(2,1)}, bf16[1,4,2,96,128]{4,3,2,1,0:T(8,128)(2,1)S(1)}, u32[]{:S(2)}, u32[]{:S(2)}) %collective-permute-start) | collective-permute-done | bytes 196640 | tf_op jit(solution)/shard_map/ppermute | solution.py:12
  7.6 1.0 %constant_dynamic-update-slice_fusion = bf16[1,8,2,96,128]{4,3,2,1,0:T(8,128)(2,1)S(1)} fusion(bf16[1,8,2,96,128]{4,3,2,1,0:T(8,128)(2,1)S(1)} %constant_dynamic-update-slice_fusion.1, bf16[1,4,2,96,128]{4,3,2,1,0:T(8,128)(2,1)} %param.7), kind=kLoop, calls=%fused_computation.216 | loop fusion | bytes 393216 | tf_op jit(solution)/shard_map/concatenate | solution.py:64
  8.5 3.2 %collective-permute-start.1 = (bf16[1,8,2,96,128]{4,3,2,1,0:T(8,128)(2,1)S(1)}, bf16[1,8,2,96,128]{4,3,2,1,0:T(8,128)(2,1)S(1)}, u32[]{:S(2)}, u32[]{:S(2)}) collective-permute-start(bf16[1,8,2,96,128]{4,3,2,1,0:T(8,128)(2,1)S(1)} %constant_dynamic-update-slice_fusion), channel_id=1, source_target_pairs={{0,4},{4,8},{8,12},{1,5},{5,9},{9,13},{2,6},{6,10},{10,14},{3,7},{... | collective-permute-start | bytes 1179656 | tf_op jit(solution)/shard_map/ppermute | solution.py:23
  11.8 1.3 %collective-permute-start.2 = (bf16[1,8,2,96,128]{4,3,2,1,0:T(8,128)(2,1)S(1)}, bf16[1,8,2,96,128]{4,3,2,1,0:T(8,128)(2,1)S(1)}, u32[]{:S(2)}, u32[]{:S(2)}) collective-permute-start(bf16[1,8,2,96,128]{4,3,2,1,0:T(8,128)(2,1)S(1)} %constant_dynamic-update-slice_fusion), channel_id=1, source_target_pairs={{4,0},{8,4},{12,8},{5,1},{9,5},{13,9},{6,2},{10,6},{14,10},{7,3},{... | collective-permute-start | bytes 1179656 | tf_op jit(solution)/shard_map/ppermute | solution.py:25
  13.1 0.1 broadcast_and_fusion
  13.2 5.0 %collective-permute-done.1 = bf16[1,8,2,96,128]{4,3,2,1,0:T(8,128)(2,1)S(1)} collective-permute-done((bf16[1,8,2,96,128]{4,3,2,1,0:T(8,128)(2,1)S(1)}, bf16[1,8,2,96,128]{4,3,2,1,0:T(8,128)(2,1)S(1)}, u32[]{:S(2)}, u32[]{:S(2)}) %collective-permute-start.1) | collective-permute-done | bytes 393248 | tf_op jit(solution)/shard_map/ppermute | solution.py:23
  18.2 4.1 %collective-permute-done.2 = bf16[1,8,2,96,128]{4,3,2,1,0:T(8,128)(2,1)S(1)} collective-permute-done((bf16[1,8,2,96,128]{4,3,2,1,0:T(8,128)(2,1)S(1)}, bf16[1,8,2,96,128]{4,3,2,1,0:T(8,128)(2,1)S(1)}, u32[]{:S(2)}, u32[]{:S(2)}) %collective-permute-start.2) | collective-permute-done | bytes 393248 | tf_op jit(solution)/shard_map/ppermute | solution.py:25
  22.3 0.3 fusion
  22.6 0.0 copy-done.2
  22.6 0.8 %fusion.7 = bf16[1,8,6,96,128]{4,3,2,1,0:T(8,128)(2,1)S(1)} fusion(f32[96]{0:T(128)S(1)} %copy-done.2, f32[8,6,128]{2,1,0:T(8,128)S(1)} %add_rsqrt_fusion, bf16[1,8,2,96,128]{4,3,2,1,0:T(8,128)(2,1)S(1)} %collective-permute-done.2, bf16[1,8,2,96,128]{4,3,2,1,0:T(8,128)(2,1)S(1)} %constant_dynamic-update-slice_fusion, ...), kind=kLoop, calls=%fused_computation.45 | loop fusion | flops 5898240 | bytes 2384256 | tf_op jit(solution)/shard_map/convert_element_type | solution.py:66
  23.4 3.0 %pad_slice_fusion.1 = (bf16[1,6,4,96,128]{4,3,2,1,0:T(8,128)(2,1)S(1)}, bf16[1,6,4,96,128]{4,3,2,1,0:T(8,128)(2,1)S(1)}, bf16[1,6,4,96,128]{4,3,2,1,0:T(8,128)(2...) fusion(bf16[1,8,6,96,128]{4,3,2,1,0:T(8,128)(2,1)S(1)} %fusion.7), kind=kLoop, calls=%fused_computation.1 | loop fusion | bytes 13565952 | tf_op jit(solution)/shard_map/slice | solution.py:49
  26.4 0.0 copy-start.3
  26.4 0.8 %fusion.164 = (bf16[1,6,4,96,128]{4,3,2,1,0:T(8,128)(2,1)S(1)}, bf16[1,6,4,96,128]{4,3,2,1,0:T(8,128)(2,1)S(1)}, bf16[1,6,4,96,128]{4,3,2,1,0:T(8,128)(2,1)S(1)}...) fusion(bf16[1,8,6,96,128]{4,3,2,1,0:T(8,128)(2,1)S(1)} %fusion.7), kind=kLoop, calls=%fused_computation.239 | loop fusion | bytes 10027008 | tf_op jit(solution)/shard_map/slice | solution.py:49
  27.2 0.2 copy-done.3
  27.4 0.6 %fusion.13 = f32[6,4,128,96]{2,3,1,0:T(8,128)S(1)} fusion(bf16[1,6,4,96,128]{4,3,2,1,0:T(8,128)(2,1)S(1)} %get-tuple-element.8, bf16[1,6,4,96,128]{4,3,2,1,0:T(8,128)(2,1)S(1)} %get-tuple-element.29, bf16[1,6,4,96,128]{4,3,2,1,0:T(8,128)(2,1)S(1)} %get-tuple-element.7, bf16[96,2592]{1,0:T(8,128)(2,1)S(1)} %copy-done.3), kind=kOutput, calls=%fused_computation.53 | convolution fusion | flops 175177728 | bytes 3022848 | tf_op jit(solution)/shard_map/oc,bfrcw->bfrow/dot_general | solution.py:54
  28.1 0.6 %fusion.61 = f32[6,4,128,96]{2,3,1,0:T(8,128)S(1)} fusion(f32[6,4,128,96]{2,3,1,0:T(8,128)S(1)} %fusion.13, bf16[1,6,4,96,128]{4,3,2,1,0:T(8,128)(2,1)S(1)} %get-tuple-element.6, bf16[1,6,4,96,128]{4,3,2,1,0:T(8,128)(2,1)S(1)} %get-tuple-element.30, bf16[1,6,4,96,128]{4,3,2,1,0:T(8,128)(2,1)S(1)} %get-tuple-element.31, bf16[96,2592]{1,0:T(8,128)(2,1)S(1)} %copy-done.3), kind=kOutput, calls=%fused_computation.108 | convolution fusion | flops 175472640 | bytes 4202496 | tf_op jit(solution)/shard_map/oc,bfrcw->bfrow/dot_general | solution.py:54
  28.6 0.6 %fusion.60 = f32[6,4,128,96]{2,3,1,0:T(8,128)S(1)} fusion(f32[6,4,128,96]{2,3,1,0:T(8,128)S(1)} %fusion.61, bf16[1,6,4,96,128]{4,3,2,1,0:T(8,128)(2,1)S(1)} %get-tuple-element.10, bf16[1,6,4,96,128]{4,3,2,1,0:T(8,128)(2,1)S(1)} %get-tuple-element.28, bf16[1,6,4,96,128]{4,3,2,1,0:T(8,128)(2,1)S(1)} %get-tuple-element.9, bf16[96,2592]{1,0:T(8,128)(2,1)S(1)} %copy-done.3), kind=kOutput, calls=%fused_computation.107 | convolution fusion | flops 175472640 | bytes 4202496 | tf_op jit(solution)/shard_map/oc,bfrcw->bfrow/dot_general | solution.py:54
  29.3 0.6 %fusion.59 = f32[6,4,128,96]{2,3,1,0:T(8,128)S(1)} fusion(f32[6,4,128,96]{2,3,1,0:T(8,128)S(1)} %fusion.60, bf16[1,6,4,96,128]{4,3,2,1,0:T(8,128)(2,1)S(1)} %get-tuple-element.12, bf16[1,6,4,96,128]{4,3,2,1,0:T(8,128)(2,1)S(1)} %get-tuple-element.27, bf16[1,6,4,96,128]{4,3,2,1,0:T(8,128)(2,1)S(1)} %get-tuple-element.11, bf16[96,2592]{1,0:T(8,128)(2,1)S(1)} %copy-done.3), kind=kOutput, calls=%fused_computation.106 | convolution fusion | flops 175472640 | bytes 4202496 | tf_op jit(solution)/shard_map/oc,bfrcw->bfrow/dot_general | solution.py:54
  29.9 0.6 %fusion.58 = f32[6,4,128,96]{2,3,1,0:T(8,128)S(1)} fusion(f32[6,4,128,96]{2,3,1,0:T(8,128)S(1)} %fusion.59, bf16[1,6,4,96,128]{4,3,2,1,0:T(8,128)(2,1)S(1)} %get-tuple-element.14, bf16[1,6,4,96,128]{4,3,2,1,0:T(8,128)(2,1)S(1)} %get-tuple-element.26, bf16[1,6,4,96,128]{4,3,2,1,0:T(8,128)(2,1)S(1)} %get-tuple-element.13, bf16[96,2592]{1,0:T(8,128)(2,1)S(1)} %copy-done.3), kind=kOutput, calls=%fused_computation.105 | convolution fusion | flops 175472640 | bytes 4202496 | tf_op jit(solution)/shard_map/oc,bfrcw->bfrow/dot_general | solution.py:54
  30.5 0.6 %fusion.57 = f32[6,4,128,96]{2,3,1,0:T(8,128)S(1)} fusion(f32[6,4,128,96]{2,3,1,0:T(8,128)S(1)} %fusion.58, bf16[1,6,4,96,128]{4,3,2,1,0:T(8,128)(2,1)S(1)} %get-tuple-element.16, bf16[1,6,4,96,128]{4,3,2,1,0:T(8,128)(2,1)S(1)} %get-tuple-element.25, bf16[1,6,4,96,128]{4,3,2,1,0:T(8,128)(2,1)S(1)} %get-tuple-element.15, bf16[96,2592]{1,0:T(8,128)(2,1)S(1)} %copy-done.3), kind=kOutput, calls=%fused_computation.104 | convolution fusion | flops 175472640 | bytes 4202496 | tf_op jit(solution)/shard_map/oc,bfrcw->bfrow/dot_general | solution.py:54
  31.1 0.6 %fusion.56 = f32[6,4,128,96]{2,3,1,0:T(8,128)S(1)} fusion(f32[6,4,128,96]{2,3,1,0:T(8,128)S(1)} %fusion.57, bf16[1,6,4,96,128]{4,3,2,1,0:T(8,128)(2,1)S(1)} %get-tuple-element.18, bf16[1,6,4,96,128]{4,3,2,1,0:T(8,128)(2,1)S(1)} %get-tuple-element.24, bf16[1,6,4,96,128]{4,3,2,1,0:T(8,128)(2,1)S(1)} %get-tuple-element.17, bf16[96,2592]{1,0:T(8,128)(2,1)S(1)} %copy-done.3), kind=kOutput, calls=%fused_computation.103 | convolution fusion | flops 175472640 | bytes 4202496 | tf_op jit(solution)/shard_map/oc,bfrcw->bfrow/dot_general | solution.py:54
  31.7 0.0 copy-start.5
  31.7 0.6 %fusion.55 = f32[6,4,128,96]{2,3,1,0:T(8,128)S(1)} fusion(f32[6,4,128,96]{2,3,1,0:T(8,128)S(1)} %fusion.56, bf16[1,6,4,96,128]{4,3,2,1,0:T(8,128)(2,1)S(1)} %get-tuple-element.20, bf16[1,6,4,96,128]{4,3,2,1,0:T(8,128)(2,1)S(1)} %get-tuple-element.23, bf16[1,6,4,96,128]{4,3,2,1,0:T(8,128)(2,1)S(1)} %get-tuple-element.19, bf16[96,2592]{1,0:T(8,128)(2,1)S(1)} %copy-done.3), kind=kOutput, calls=%fused_computation.102 | convolution fusion | flops 175472640 | bytes 4202496 | tf_op jit(solution)/shard_map/oc,bfrcw->bfrow/dot_general | solution.py:54
  32.3 0.0 copy-done.5
  32.4 0.0 copy-start.1
  32.4 0.6 %multiply_reduce_fusion = (f32[6,4,128]{2,1,0:T(4,128)S(1)}, f32[1,6,4,128,96]{3,4,2,1,0:T(8,128)S(1)}) fusion(f32[96]{0:T(128)S(1)} %copy-done.5, f32[6,4,128,96]{2,3,1,0:T(8,128)S(1)} %fusion.55, bf16[1,6,4,96,128]{4,3,2,1,0:T(8,128)(2,1)S(1)} %get-tuple-element.21, bf16[1,6,4,96,128]{4,3,2,1,0:T(8,128)(2,1)S(1)} %get-tuple-element.22, ...), kind=kOutput, calls=%fused_computation.128 | convolution fusion | flops 176354304 | bytes 4215296 | tf_op jit(solution)/shard_map/oc,bfrcw->bfrow/dot_general | solution.py:54
  33.0 0.0 copy-done.1
  33.0 0.4 %fusion.109 = bf16[1,6,4,96,128]{4,3,2,1,0:T(8,128)(2,1)S(1)} fusion(f32[96]{0:T(128)S(1)} %copy-done.1, f32[1,6,4,128,96]{3,4,2,1,0:T(8,128)S(1)} %get-tuple-element.60, f32[6,4,128]{2,1,0:T(4,128)S(1)} %add_rsqrt_fusion.1, pred[6,4]{1,0:T(8,128)(4,1)S(1)} %broadcast_and_fusion), kind=kLoop, calls=%fused_computation.177 | loop fusion | flops 2359296 | bytes 1782168 | tf_op jit(solution)/shard_map/jit(_where)/select_n | solution.py:73
  33.5 1.0 %pad_slice_fusion.19 = (bf16[1,4,2,96,128]{4,3,2,1,0:T(8,128)(2,1)S(1)}, bf16[1,4,2,96,128]{4,3,2,1,0:T(8,128)(2,1)S(1)}, bf16[1,4,2,96,128]{4,3,2,1,0:T(8,128)(...) fusion(bf16[1,6,4,96,128]{4,3,2,1,0:T(8,128)(2,1)S(1)} %fusion.109), kind=kLoop, calls=%fused_computation.19 | loop fusion | bytes 4718592 | tf_op jit(solution)/shard_map/slice | solution.py:49
  34.4 0.0 copy-start.4
  34.4 0.3 fusion.165
  34.7 0.7 %copy-done.4 = bf16[96,2592]{1,0:T(8,128)(2,1)S(1)} copy-done((bf16[96,2592]{1,0:T(8,128)(2,1)S(1)}, bf16[96,2592]{1,0:T(8,128)(2,1)}, u32[]{:S(2)}) %copy-start.4) | copy-done | bytes 497688
  35.5 0.3 fusion.72
  35.8 0.3 convolution_add_fusion.7
  36.1 0.3 convolution_add_fusion.6
  36.4 0.3 convolution_add_fusion.5
  36.8 0.3 convolution_add_fusion.4
  37.0 0.3 convolution_add_fusion.3
  37.4 0.3 convolution_add_fusion.2
  37.7 0.0 copy-start
  37.7 0.0 copy-start.6
  37.7 0.3 convolution_add_fusion.1
  38.1 0.6 %copy-done = bf16[1,4,2,96,128]{4,3,2,1,0:T(8,128)(2,1)S(1)} copy-done((bf16[1,4,2,96,128]{4,3,2,1,0:T(8,128)(2,1)S(1)}, bf16[1,4,2,96,128]{4,3,2,1,0:T(8,128)(2,1)}, u32[]{:S(2)}) %copy-start) | copy-done | bytes 196632
  38.6 0.0 copy-done.6
  38.6 1.0 %fusion.71 = bf16[1,4,2,96,128]{4,3,2,1,0:T(8,128)(2,1)} fusion(f32[4,2,128,96]{2,3,1,0:T(8,128)S(1)} %convolution_add_fusion.1, bf16[1,4,2,96,128]{4,3,2,1,0:T(8,128)(2,1)S(1)} %get-tuple-element.48, bf16[1,4,2,96,128]{4,3,2,1,0:T(8,128)(2,1)S(1)} %get-tuple-element.49, bf16[1,4,2,96,128]{4,3,2,1,0:T(8,128)(2,1)S(1)} %get-tuple-element.32, ...), kind=kOutput, calls=%fused_computation.130 | convolution fusion | flops 58884096 | bytes 1450496 | tf_op jit(solution)/shard_map/oc,bfrcw->bfrow/dot_general | solution.py:54
  (5 shorter events, 0.1 us)
Async XLA Ops:
  0.0 22.6 %copy-start.2 = (f32[96]{0:T(128)S(1)}, f32[96]{0:T(128)}, u32[]{:S(2)}) copy-start(f32[96]{0:T(128)} %param.8) | copy-start | bytes 1156
  0.0 7.5 %collective-permute-start = (bf16[1,4,2,96,128]{4,3,2,1,0:T(8,128)(2,1)}, bf16[1,4,2,96,128]{4,3,2,1,0:T(8,128)(2,1)S(1)}, u32[]{:S(2)}, u32[]{:S(2)}) collective-permute-start(bf16[1,4,2,96,128]{4,3,2,1,0:T(8,128)(2,1)} %param.7), channel_id=1, source_target_pairs={{0,1},{1,2},{2,3},{4,5},{5,6},{6,7},{8,9},{9,10},{10,11},{12,13},{... | collective-permute-start | bytes 589832 | tf_op jit(solution)/shard_map/ppermute | solution.py:12
  8.5 9.7 %collective-permute-start.1 = (bf16[1,8,2,96,128]{4,3,2,1,0:T(8,128)(2,1)S(1)}, bf16[1,8,2,96,128]{4,3,2,1,0:T(8,128)(2,1)S(1)}, u32[]{:S(2)}, u32[]{:S(2)}) collective-permute-start(bf16[1,8,2,96,128]{4,3,2,1,0:T(8,128)(2,1)S(1)} %constant_dynamic-update-slice_fusion), channel_id=1, source_target_pairs={{0,4},{4,8},{8,12},{1,5},{5,9},{9,13},{2,6},{6,10},{10,14},{3,7},{... | collective-permute-start | bytes 1179656 | tf_op jit(solution)/shard_map/ppermute | solution.py:23
  11.8 10.6 %collective-permute-start.2 = (bf16[1,8,2,96,128]{4,3,2,1,0:T(8,128)(2,1)S(1)}, bf16[1,8,2,96,128]{4,3,2,1,0:T(8,128)(2,1)S(1)}, u32[]{:S(2)}, u32[]{:S(2)}) collective-permute-start(bf16[1,8,2,96,128]{4,3,2,1,0:T(8,128)(2,1)S(1)} %constant_dynamic-update-slice_fusion), channel_id=1, source_target_pairs={{4,0},{8,4},{12,8},{5,1},{9,5},{13,9},{6,2},{10,6},{14,10},{7,3},{... | collective-permute-start | bytes 1179656 | tf_op jit(solution)/shard_map/ppermute | solution.py:25
  26.4 1.0 %copy-start.3 = (bf16[96,2592]{1,0:T(8,128)(2,1)S(1)}, bf16[96,2592]{1,0:T(8,128)(2,1)}, u32[]{:S(2)}) copy-start(bf16[96,2592]{1,0:T(8,128)(2,1)} %param.9) | copy-start | bytes 1492996
  31.7 0.7 %copy-start.5 = (f32[96]{0:T(128)S(1)}, f32[96]{0:T(128)}, u32[]{:S(2)}) copy-start(f32[96]{0:T(128)} %param.10) | copy-start | bytes 1156
  32.4 0.7 %copy-start.1 = (f32[96]{0:T(128)S(1)}, f32[96]{0:T(128)}, u32[]{:S(2)}) copy-start(f32[96]{0:T(128)} %param.11) | copy-start | bytes 1156
  34.4 1.0 %copy-start.4 = (bf16[96,2592]{1,0:T(8,128)(2,1)S(1)}, bf16[96,2592]{1,0:T(8,128)(2,1)}, u32[]{:S(2)}) copy-start(bf16[96,2592]{1,0:T(8,128)(2,1)} %param.12) | copy-start | bytes 1492996
  37.7 0.9 %copy-start = (bf16[1,4,2,96,128]{4,3,2,1,0:T(8,128)(2,1)S(1)}, bf16[1,4,2,96,128]{4,3,2,1,0:T(8,128)(2,1)}, u32[]{:S(2)}) copy-start(bf16[1,4,2,96,128]{4,3,2,1,0:T(8,128)(2,1)} %param.7) | copy-start | bytes 589828
  37.7 0.9 %copy-start.6 = (f32[96]{0:T(128)S(1)}, f32[96]{0:T(128)}, u32[]{:S(2)}) copy-start(f32[96]{0:T(128)} %param.13) | copy-start | bytes 1156
where the time goes:
time: 39.9 us; the launch traced here: 39.6 us
  waiting for transfers between devices  12.1 us (30%)
  starting transfers between devices  9.15 us (23%)
  matrix products  8.95 us (22%)
  local copies, waits for them, and re-layouts  7.62 us (19%)
  other arithmetic  1.58 us (4%)
    dot_general x18, matrix products, conv_valid(): jnp.einsum('oc,bfrcw->bfrow', columns, stacked, preferred_element_type=jn...  8.95 us
    ppermute x1, waiting for transfers between devices, padded_2(): lax.ppermute(tail, axis, [(i, (i + 1) % count) for i in range(ends)])  5.04 us
    ppermute x1, starting transfers between devices, passed_along(): return lax.ppermute(block, axis, route)  4.63 us
    ppermute x1, waiting for transfers between devices, padded_2(): lax.ppermute(head, axis, [((i + 1) % count, i) for i in range(ends)])  4.12 us
    slice x2, local copies, waits for them, and re-layouts, conv_valid(): section[..., 0:width]  3.97 us
    ppermute x1, starting transfers between devices, padded_2(): lax.ppermute(tail, axis, [(i, (i + 1) % count) for i in range(ends)])  3.22 us
    ppermute x1, waiting for transfers between devices, passed_along(): return lax.ppermute(block, axis, route)  2.9 us
    unnamed x15, local copies, waits for them, and re-layouts  1.61 us
  transfers between devices with their start and end apart: 3, of which 3 were waited for; matrix products, arithmetic and copies ran while one was open for 0% of the time, Pallas kernels for 0%

commit v1 on v0

v1 whole, which is shorter than its diff:
```python
import functools

import jax
import jax.numpy as jnp
from jax import lax
from jax.experimental import pallas as pl
from jax.experimental.pallas import tpu as pltpu
from jax.sharding import PartitionSpec as P

epsilon = 1e-06
VMEM = pl.BlockSpec(memory_space=pltpu.VMEM)
SMEM = pl.BlockSpec(memory_space=pltpu.SMEM)


def column(vector_ref):
    row = vector_ref[...].reshape(1, -1)
    count = row.shape[1]
    down = lax.broadcasted_iota(jnp.int32, (count, count), 0)
    across = lax.broadcasted_iota(jnp.int32, (count, count), 1)
    return jnp.sum(jnp.where(down == across, row, 0.0), axis=1, keepdims=True)


def norm_silu(values, gain):
    meansq = jnp.mean(values * values, axis=-2, keepdims=True)
    half = values * lax.rsqrt(meansq + epsilon) * (0.5 * gain)
    return half + half * jnp.tanh(half)


def restacked(weights, frame_offs):
    chans = weights.shape[0]
    return jnp.concatenate(
        [
            jnp.concatenate(
                [
                    weights[:, (m * 3 + k) * chans : (m * 3 + k + 1) * chans]
                    for m in range(3 * frame_offs[0], 3 * frame_offs[1])
                ],
                axis=1,
            )
            for k in range(3)
        ],
        axis=0,
    )


def conv_two_rows(weights, cells, frame, count, row):
    chans, width = cells.shape[2:]
    depth = 3 * count * chans
    windows = jnp.concatenate(
        [
            cells[frame : frame + count, row : row + 3].reshape(depth, width),
            cells[frame : frame + count, row + 1 : row + 4].reshape(depth, width),
        ],
        axis=1,
    )
    stacked = jnp.dot(weights, windows, preferred_element_type=jnp.float32)
    lane = lax.broadcasted_iota(jnp.int32, (chans, width), 1)
    sums = []
    for side in range(2):
        part = stacked[:, side * width : (side + 1) * width]
        left = jnp.where(lane == 0, 0.0, pltpu.roll(part[:chans], 1, 1))
        right = jnp.where(lane == width - 1, 0.0, pltpu.roll(part[2 * chans :], width - 1, 1))
        sums.append(part[chans : 2 * chans] + left + right)
    return sums


def fill_active(active, blocks, gain):
    row = 0
    for block in blocks:
        for frame in range(block.shape[1]):
            for inner in range(block.shape[2]):
                values = block[0, frame, inner].astype(jnp.float32)
                active[frame, row + inner] = norm_silu(values, gain).astype(jnp.bfloat16)
        row += block.shape[2]


def own_kernel(
    edge, video, above, below, gamma_first, kernel_first, bias_first, gamma_second, kernel_second,
    partial, second, first_0, first_01, first_all, second_all, active,
):
    weights = kernel_first[...]
    stacked_all = restacked(weights, (0, 3))
    first_all[...] = stacked_all
    first_0[...] = restacked(weights, (0, 1))
    first_01[...] = restacked(weights, (0, 2))
    second_all[...] = restacked(kernel_second[...], (0, 3))
    stacked_2 = restacked(weights, (2, 3))
    stacked_12 = restacked(weights, (1, 3))
    fill_active(active, (above, video, below), column(gamma_first))
    bias = column(bias_first)
    gain = column(gamma_second)
    frames = video.shape[1]
    for frame in range(frames):
        for row in (0, 2):
            if frame == 0:
                sums = conv_two_rows(stacked_2, active, 0, 1, row)
            elif frame == 1:
                sums = conv_two_rows(stacked_12, active, 0, 2, row)
            else:
                sums = conv_two_rows(first_all[...], active, frame - 2, 3, row)
            for side in range(2):
                hidden = sums[side] + bias
                if frame < 2:
                    partial[frame, row + side] = hidden
                else:
                    value = norm_silu(hidden, gain)
                    if row + side == 0:
                        value = value * edge[0]
                    if row + side == 3:
                        value = value * edge[1]
                    second[frame - 2, row + side] = value.astype(jnp.bfloat16)


def last_kernel(
    edge, video, prior, above, below, partial, late, first_0, first_01, first_all, second_all,
    gamma_first, bias_first, gamma_second, bias_second, encoded, active, second,
):
    fill_active(active, (above, prior, below), column(gamma_first))
    bias = column(bias_first)
    gain = column(gamma_second)
    frames = video.shape[1]
    second[4 : frames + 2] = late[...]
    for frame in range(4):
        for row in (0, 2):
            if frame < 2:
                sums = conv_two_rows(first_all[...], active, frames - 4 + frame, 3, row)
            elif frame == 2:
                sums = conv_two_rows(first_01[...], active, frames - 2, 2, row)
            else:
                sums = conv_two_rows(first_0[...], active, frames - 1, 1, row)
            for side in range(2):
                if frame < 2:
                    value = norm_silu(sums[side] + bias, gain) * edge[2]
                else:
                    value = norm_silu(sums[side] + partial[frame - 2, row + side], gain)
                if row + side == 0:
                    value = value * edge[0]
                if row + side == 3:
                    value = value * edge[1]
                second[frame, row + side] = value.astype(jnp.bfloat16)
    offset = column(bias_second)
    for frame in range(frames):
        sums = conv_two_rows(second_all[...], second, frame, 3, 0)
        for side in range(2):
            value = video[0, frame, side].astype(jnp.float32) + (sums[side] + offset)
            encoded[0, frame, side] = value.astype(jnp.bfloat16)


def from_neighbour(block, frame_step, row_step):
    frame_parts, row_parts = lax.axis_size("tm"), lax.axis_size("rows")
    route = []
    for row in range(row_parts):
        for part in range(frame_parts):
            row_to, part_to = row + row_step, part + frame_step
            if 0 <= row_to < row_parts and 0 <= part_to < frame_parts:
                route.append((row * frame_parts + part, row_to * frame_parts + part_to))
    return lax.ppermute(block, ("rows", "tm"), route)


def local(video, gamma_first, kernel_first, bias_first, gamma_second, kernel_second, bias_second):
    _, frames, rows, chans, width = video.shape
    above = from_neighbour(video, 0, 1)
    below = from_neighbour(video, 0, -1)
    prior_above = from_neighbour(video, 1, 1)
    prior_below = from_neighbour(video, 1, -1)
    prior = from_neighbour(video, 1, 0)
    row_part = lax.axis_index("rows")
    edge = jnp.stack(
        [row_part > 0, row_part < lax.axis_size("rows") - 1, lax.axis_index("tm") > 0]
    ).astype(jnp.float32)
    bf16, f32 = jnp.bfloat16, jnp.float32
    shape = jax.ShapeDtypeStruct
    params = pltpu.CompilerParams(vmem_limit_bytes=24 * 2**20)
    partial, late, first_0, first_01, first_all, second_all = pl.pallas_call(
        own_kernel,
        out_shape=(
            shape((2, rows + 2, chans, width), f32),
            shape((frames - 2, rows + 2, chans, width), bf16),
            shape((3 * chans, 3 * chans), bf16),
            shape((3 * chans, 6 * chans), bf16),
            shape((3 * chans, 9 * chans), bf16),
            shape((3 * chans, 9 * chans), bf16),
        ),
        in_specs=[SMEM] + [VMEM] * 8,
        out_specs=[VMEM] * 6,
        scratch_shapes=[pltpu.VMEM((frames, rows + 4, chans, width), bf16)],
        compiler_params=params,
        cost_estimate=pl.CostEstimate(flops=2 * 10**9, bytes_accessed=4 * 10**6, transcendentals=10**6),
    )(edge, video, above, below, gamma_first, kernel_first, bias_first, gamma_second, kernel_second)
    return pl.pallas_call(
        last_kernel,
        out_shape=shape(video.shape, bf16),
        in_specs=[SMEM] + [VMEM] * 14,
        out_specs=VMEM,
        scratch_shapes=[
            pltpu.VMEM((frames, rows + 4, chans, width), bf16),
            pltpu.VMEM((frames + 2, rows + 2, chans, width), bf16),
        ],
        compiler_params=params,
        cost_estimate=pl.CostEstimate(flops=2 * 10**9, bytes_accessed=4 * 10**6, transcendentals=10**6),
    )(
        edge, video, prior, prior_above, prior_below, partial, late, first_0, first_01, first_all, second_all,
        gamma_first, bias_first, gamma_second, bias_second,
    )


def solution(mesh):
    in_specs = (P("groups", "tm", "rows", None, None), P(), P(), P(), P(), P(), P())
    out_specs = P("groups", "tm", "rows", None, None)
    return jax.shard_map(local, mesh=mesh, in_specs=in_specs, out_specs=out_specs, check_vma=False)
```

time: 39.9 us -> 26.3 us (0.66)
  waiting for transfers between devices: 12.1 us -> 1.38 us
  matrix products: 8.95 us -> 0 us
  Pallas kernels: 0 us -> 5.61 us
  starting transfers between devices: 9.15 us -> 14.6 us
  local copies, waits for them, and re-layouts: 7.62 us -> 4.24 us
  other arithmetic: 1.58 us -> 0.08 us
    ppermute x3 -> x5, waiting for transfers between devices: 12.1 us -> 1.38 us  [from_neighbour(): return lax.ppermute(block, ('rows', 'tm'), route)]
    dot_general x18 -> x0, matrix products: 8.95 us -> none  [conv_valid(): jnp.einsum('oc,bfrcw->bfrow', columns, stacked, preferred_element_type=jn...]
    pallas_call x0 -> x2, Pallas kernels: none -> 5.61 us  [the longest x1 3.45 us: local(): pl.pallas_call(last_kernel, out_shape=shape(video.shape, bf16), in_specs=...]
    ppermute x3 -> x5, starting transfers between devices: 9.15 us -> 14.6 us  [from_neighbour(): return lax.ppermute(block, ('rows', 'tm'), route)]
    slice x4 -> x0, local copies, waits for them, and re-layouts: 5.06 us -> none  [the longest x2 3.97 us: conv_valid(): section[..., 0:width]]
    unnamed x15 -> x14, local copies, waits for them, and re-layouts: 1.61 us -> 4.24 us
    concatenate x1 -> x0, local copies, waits for them, and re-layouts: 0.96 us -> none  [local(): joined = jnp.concatenate([prior, video], axis=1)]
    convert_element_type x1, other arithmetic: 0.77 us -> 0.08 us  [local(): edge = jnp.stack([row_part > 0, row_part < lax.axis_size('rows') - 1, lax...]
  transfers between devices with their start and end apart: 3 -> 5, of which waited for: 3 -> 1; matrix products, arithmetic and copies ran while one was open for 0% -> 0% of each run, Pallas kernels for 0% -> 8%
where the time goes in v1:
time: 26.3 us; the launch traced here: 26 us
  starting transfers between devices  14.6 us (56%)
  Pallas kernels  5.61 us (21%)
  local copies, waits for them, and re-layouts  4.24 us (16%)
  waiting for transfers between devices  1.38 us (5%)
    ppermute x5, starting transfers between devices, from_neighbour(): return lax.ppermute(block, ('rows', 'tm'), route)  14.6 us
    unnamed x14, local copies, waits for them, and re-layouts  4.24 us
    pallas_call x1, Pallas kernels, local(): pl.pallas_call(last_kernel, out_shape=shape(video.shape, bf16), in_specs=...  3.45 us
    pallas_call x1, Pallas kernels, local(): pl.pallas_call(own_kernel, out_shape=(shape((2, rows + 2, chans, width),...  2.16 us
    ppermute x5, waiting for transfers between devices, from_neighbour(): return lax.ppermute(block, ('rows', 'tm'), route)  1.38 us
  transfers between devices with their start and end apart: 5, of which 1 were waited for; matrix products, arithmetic and copies ran while one was open for 0% of the time, Pallas kernels for 8%

profile of v1, /device:TPU:1, one launch (start us, length us, event | category | flops | bytes accessed | tf_op | source)
XLA Modules:
  0.0 26.0 jit_solution(14827642179916123471)
XLA Ops:
  0.0 4.0 %collective-permute-start.3 = (bf16[1,4,2,96,128]{4,3,2,1,0:T(8,128)(2,1)}, bf16[1,4,2,96,128]{4,3,2,1,0:T(8,128)(2,1)S(1)}, u32[]{:S(2)}, u32[]{:S(2)}) collective-permute-start(bf16[1,4,2,96,128]{4,3,2,1,0:T(8,128)(2,1)} %video.3), channel_id=1, source_target_pairs={{0,4},{1,5},{2,6},{3,7},{4,8},{5,9},{6,10},{7,11},{8,12},{9,13},{1... | collective-permute-start | bytes 589832 | tf_op jit(solution)/shard_map/ppermute | solution.py:157
  4.0 1.3 %collective-permute-start.4 = (bf16[1,4,2,96,128]{4,3,2,1,0:T(8,128)(2,1)}, bf16[1,4,2,96,128]{4,3,2,1,0:T(8,128)(2,1)S(1)}, u32[]{:S(2)}, u32[]{:S(2)}) collective-permute-start(bf16[1,4,2,96,128]{4,3,2,1,0:T(8,128)(2,1)} %video.3), channel_id=1, source_target_pairs={{4,0},{5,1},{6,2},{7,3},{8,4},{9,5},{10,6},{11,7},{12,8},{13,9},{1... | collective-permute-start | bytes 589832 | tf_op jit(solution)/shard_map/ppermute | solution.py:157
  5.3 4.0 %collective-permute-start = (bf16[1,4,2,96,128]{4,3,2,1,0:T(8,128)(2,1)}, bf16[1,4,2,96,128]{4,3,2,1,0:T(8,128)(2,1)S(1)}, u32[]{:S(2)}, u32[]{:S(2)}) collective-permute-start(bf16[1,4,2,96,128]{4,3,2,1,0:T(8,128)(2,1)} %video.3), channel_id=1, source_target_pairs={{0,1},{1,2},{2,3},{4,5},{5,6},{6,7},{8,9},{9,10},{10,11},{12,13},{... | collective-permute-start | bytes 589832 | tf_op jit(solution)/shard_map/ppermute | solution.py:157
  9.3 4.0 %collective-permute-start.1 = (bf16[1,4,2,96,128]{4,3,2,1,0:T(8,128)(2,1)}, bf16[1,4,2,96,128]{4,3,2,1,0:T(8,128)(2,1)S(1)}, u32[]{:S(2)}, u32[]{:S(2)}) collective-permute-start(bf16[1,4,2,96,128]{4,3,2,1,0:T(8,128)(2,1)} %video.3), channel_id=1, source_target_pairs={{0,5},{1,6},{2,7},{4,9},{5,10},{6,11},{8,13},{9,14},{10,15},{16,21... | collective-permute-start | bytes 589832 | tf_op jit(solution)/shard_map/ppermute | solution.py:157
  13.3 1.3 %collective-permute-start.2 = (bf16[1,4,2,96,128]{4,3,2,1,0:T(8,128)(2,1)}, bf16[1,4,2,96,128]{4,3,2,1,0:T(8,128)(2,1)S(1)}, u32[]{:S(2)}, u32[]{:S(2)}) collective-permute-start(bf16[1,4,2,96,128]{4,3,2,1,0:T(8,128)(2,1)} %video.3), channel_id=1, source_target_pairs={{4,1},{5,2},{6,3},{8,5},{9,6},{10,7},{12,9},{13,10},{14,11},{20,17... | collective-permute-start | bytes 589832 | tf_op jit(solution)/shard_map/ppermute | solution.py:157
  14.6 0.0 copy-start.3
  14.6 0.0 copy-start.4
  14.7 0.0 copy-start.5
  14.7 0.1 add_convert_fusion.edge
  14.7 0.0 collective-permute-done.3.above
  14.7 0.0 collective-permute-done.4.below
  14.8 0.5 %copy-done.3 = f32[96]{0:T(128)S(1)} copy-done((f32[96]{0:T(128)S(1)}, f32[96]{0:T(128)}, u32[]{:S(2)}) %copy-start.3) | copy-done | bytes 408
  15.3 0.0 copy-done.4
  15.3 0.0 copy-done.5
  15.3 0.0 copy-start
  15.3 1.0 %copy-done = bf16[96,2592]{1,0:T(8,128)(2,1)S(1)} copy-done((bf16[96,2592]{1,0:T(8,128)(2,1)S(1)}, bf16[96,2592]{1,0:T(8,128)(2,1)}, u32[]{:S(2)}) %copy-start) | copy-done | bytes 497688
  16.4 0.0 copy-start.1
  16.4 1.0 %copy-done.1 = bf16[96,2592]{1,0:T(8,128)(2,1)S(1)} copy-done((bf16[96,2592]{1,0:T(8,128)(2,1)S(1)}, bf16[96,2592]{1,0:T(8,128)(2,1)}, u32[]{:S(2)}) %copy-start.1) | copy-done | bytes 497688
  17.4 0.0 copy-start.2
  17.4 0.9 %copy-done.2 = bf16[1,4,2,96,128]{4,3,2,1,0:T(8,128)(2,1)S(1)} copy-done((bf16[1,4,2,96,128]{4,3,2,1,0:T(8,128)(2,1)S(1)}, bf16[1,4,2,96,128]{4,3,2,1,0:T(8,128)(2,1)}, u32[]{:S(2)}) %copy-start.2) | copy-done | bytes 196632
  18.3 2.2 %shard_map.73 = (f32[2,4,96,128]{3,2,1,0:T(8,128)S(1)}, bf16[2,4,96,128]{3,2,1,0:T(8,128)(2,1)S(1)}, bf16[288,288]{1,0:T(8,128)(2,1)S(1)}, bf16[288,576]{1,0:T(8...) custom-call(f32[3]{0:T(128)S(1)} %add_convert_fusion.edge, ...), custom_call_target="tpu_custom_call" | custom-call | flops 2000000000 | bytes 4000000 | tf_op jit(solution)/shard_map/pallas_call | solution.py:174
  20.5 0.0 collective-permute-done.prior
  20.5 0.0 collective-permute-done.1.above
  20.5 1.4 %collective-permute-done.2.below = bf16[1,4,2,96,128]{4,3,2,1,0:T(8,128)(2,1)S(1)} collective-permute-done((bf16[1,4,2,96,128]{4,3,2,1,0:T(8,128)(2,1)}, bf16[1,4,2,96,128]{4,3,2,1,0:T(8,128)(2,1)S(1)}, u32[]{:S(2)}, u32[]{:S(2)}) %collective-permute-start.2) | collective-permute-done | bytes 196640 | tf_op jit(solution)/shard_map/ppermute | solution.py:157
  21.9 0.0 copy-start.6
  21.9 0.7 %copy-done.6 = f32[96]{0:T(128)S(1)} copy-done((f32[96]{0:T(128)S(1)}, f32[96]{0:T(128)}, u32[]{:S(2)}) %copy-start.6) | copy-done | bytes 408
  22.5 3.5 %shard_map.74 = bf16[1,4,2,96,128]{4,3,2,1,0:T(8,128)(2,1)} custom-call(f32[3]{0:T(128)S(1)} %add_convert_fusion.edge, bf16[1,4,2,96,128]{4,3,2,1,0:T(8,128)(2,1)S(1)} %copy-done.2, bf16[1,4,2,96,128]{4,3,2,1,0:T(8,128)(2,1)S(1)} %collective-permute-done.prior, bf16[1,4,2,96,128]{4,3,2,1,0:T(8,128)(2,1)S(1)} %collective-permute-done.1.above, ...), custom_call_target="tpu_custom_call" | custom-call | flops 2000000000 | bytes 4000000 | tf_op jit(solution)/shard_map/pallas_call | solution.py:190
Async XLA Ops:
  0.0 14.7 %collective-permute-start.3 = (bf16[1,4,2,96,128]{4,3,2,1,0:T(8,128)(2,1)}, bf16[1,4,2,96,128]{4,3,2,1,0:T(8,128)(2,1)S(1)}, u32[]{:S(2)}, u32[]{:S(2)}) collective-permute-start(bf16[1,4,2,96,128]{4,3,2,1,0:T(8,128)(2,1)} %video.3), channel_id=1, source_target_pairs={{0,4},{1,5},{2,6},{3,7},{4,8},{5,9},{6,10},{7,11},{8,12},{9,13},{1... | collective-permute-start | bytes 589832 | tf_op jit(solution)/shard_map/ppermute | solution.py:157
  4.0 10.7 %collective-permute-start.4 = (bf16[1,4,2,96,128]{4,3,2,1,0:T(8,128)(2,1)}, bf16[1,4,2,96,128]{4,3,2,1,0:T(8,128)(2,1)S(1)}, u32[]{:S(2)}, u32[]{:S(2)}) collective-permute-start(bf16[1,4,2,96,128]{4,3,2,1,0:T(8,128)(2,1)} %video.3), channel_id=1, source_target_pairs={{4,0},{5,1},{6,2},{7,3},{8,4},{9,5},{10,6},{11,7},{12,8},{13,9},{1... | collective-permute-start | bytes 589832 | tf_op jit(solution)/shard_map/ppermute | solution.py:157
  5.3 15.2 %collective-permute-start = (bf16[1,4,2,96,128]{4,3,2,1,0:T(8,128)(2,1)}, bf16[1,4,2,96,128]{4,3,2,1,0:T(8,128)(2,1)S(1)}, u32[]{:S(2)}, u32[]{:S(2)}) collective-permute-start(bf16[1,4,2,96,128]{4,3,2,1,0:T(8,128)(2,1)} %video.3), channel_id=1, source_target_pairs={{0,1},{1,2},{2,3},{4,5},{5,6},{6,7},{8,9},{9,10},{10,11},{12,13},{... | collective-permute-start | bytes 589832 | tf_op jit(solution)/shard_map/ppermute | solution.py:157
  9.3 11.2 %collective-permute-start.1 = (bf16[1,4,2,96,128]{4,3,2,1,0:T(8,128)(2,1)}, bf16[1,4,2,96,128]{4,3,2,1,0:T(8,128)(2,1)S(1)}, u32[]{:S(2)}, u32[]{:S(2)}) collective-permute-start(bf16[1,4,2,96,128]{4,3,2,1,0:T(8,128)(2,1)} %video.3), channel_id=1, source_target_pairs={{0,5},{1,6},{2,7},{4,9},{5,10},{6,11},{8,13},{9,14},{10,15},{16,21... | collective-permute-start | bytes 589832 | tf_op jit(solution)/shard_map/ppermute | solution.py:157
  13.3 8.6 %collective-permute-start.2 = (bf16[1,4,2,96,128]{4,3,2,1,0:T(8,128)(2,1)}, bf16[1,4,2,96,128]{4,3,2,1,0:T(8,128)(2,1)S(1)}, u32[]{:S(2)}, u32[]{:S(2)}) collective-permute-start(bf16[1,4,2,96,128]{4,3,2,1,0:T(8,128)(2,1)} %video.3), channel_id=1, source_target_pairs={{4,1},{5,2},{6,3},{8,5},{9,6},{10,7},{12,9},{13,10},{14,11},{20,17... | collective-permute-start | bytes 589832 | tf_op jit(solution)/shard_map/ppermute | solution.py:157
  14.6 0.7 %copy-start.3 = (f32[96]{0:T(128)S(1)}, f32[96]{0:T(128)}, u32[]{:S(2)}) copy-start(f32[96]{0:T(128)} %gamma_first.3) | copy-start | bytes 1156
  14.6 0.7 %copy-start.4 = (f32[96]{0:T(128)S(1)}, f32[96]{0:T(128)}, u32[]{:S(2)}) copy-start(f32[96]{0:T(128)} %bias_first.3) | copy-start | bytes 1156
  14.7 0.7 %copy-start.5 = (f32[96]{0:T(128)S(1)}, f32[96]{0:T(128)}, u32[]{:S(2)}) copy-start(f32[96]{0:T(128)} %gamma_second.3) | copy-start | bytes 1156
  15.3 1.0 %copy-start = (bf16[96,2592]{1,0:T(8,128)(2,1)S(1)}, bf16[96,2592]{1,0:T(8,128)(2,1)}, u32[]{:S(2)}) copy-start(bf16[96,2592]{1,0:T(8,128)(2,1)} %kernel_first.1) | copy-start | bytes 1492996
  16.4 1.0 %copy-start.1 = (bf16[96,2592]{1,0:T(8,128)(2,1)S(1)}, bf16[96,2592]{1,0:T(8,128)(2,1)}, u32[]{:S(2)}) copy-start(bf16[96,2592]{1,0:T(8,128)(2,1)} %kernel_second.1) | copy-start | bytes 1492996
  17.4 0.9 %copy-start.2 = (bf16[1,4,2,96,128]{4,3,2,1,0:T(8,128)(2,1)S(1)}, bf16[1,4,2,96,128]{4,3,2,1,0:T(8,128)(2,1)}, u32[]{:S(2)}) copy-start(bf16[1,4,2,96,128]{4,3,2,1,0:T(8,128)(2,1)} %video.3) | copy-start | bytes 589828
  21.9 0.7 %copy-start.6 = (f32[96]{0:T(128)S(1)}, f32[96]{0:T(128)}, u32[]{:S(2)}) copy-start(f32[96]{0:T(128)} %bias_second.1) | copy-start | bytes 1156

commit v2 on v0

v2 whole, which is shorter than its diff:
```python
import jax
import jax.numpy as jnp
from jax import lax
from jax.experimental import pallas as pl
from jax.experimental.pallas import tpu as pltpu
from jax.sharding import PartitionSpec as P

epsilon = 1e-06
VMEM = pl.BlockSpec(memory_space=pltpu.VMEM)


def column(vector_ref):
    row = vector_ref[...].reshape(1, -1)
    count = row.shape[1]
    down = lax.broadcasted_iota(jnp.int32, (count, count), 0)
    across = lax.broadcasted_iota(jnp.int32, (count, count), 1)
    return jnp.sum(jnp.where(down == across, row, 0.0), axis=1, keepdims=True)


def norm_silu(values, gain):
    meansq = jnp.mean(values * values, axis=-2, keepdims=True)
    half = values * lax.rsqrt(meansq + epsilon) * (0.5 * gain)
    return half + half * jnp.tanh(half)


def activate(block, out, gain):
    for frame in range(block.shape[1]):
        for row in range(block.shape[2]):
            values = block[0, frame, row].astype(jnp.float32)
            out[frame, row] = norm_silu(values, gain).astype(jnp.bfloat16)


def restack(weights, out, padded):
    chans = weights.shape[0]
    blank = jnp.zeros((chans, chans), weights.dtype)
    for k in range(3):
        pieces = []
        for i in range(3):
            for j in range(3):
                start = ((i * 3 + j) * 3 + k) * chans
                pieces.append(weights[:, start : start + chans])
            if padded:
                pieces.append(blank)
        out[k * chans : (k + 1) * chans, :] = jnp.concatenate(pieces, axis=1)


def conv_two_rows(weights, rows, frame, count, padded):
    halves = []
    for side in range(2):
        pieces = []
        for offset in range(frame, frame + count):
            for cells, row in rows[side : side + 3] + (rows[side + 1 : side + 2] if padded else []):
                pieces.append(cells[offset, row])
        halves.append(jnp.concatenate(pieces, axis=0))
    stacked = jnp.dot(weights, jnp.concatenate(halves, axis=1), preferred_element_type=jnp.float32)
    chans, width = pieces[0].shape
    lane = lax.broadcasted_iota(jnp.int32, (chans, width), 1)
    sums = []
    for side in range(2):
        part = stacked[:, side * width : (side + 1) * width]
        left = jnp.where(lane == 0, 0.0, pltpu.roll(part[:chans], 1, 1))
        right = jnp.where(lane == width - 1, 0.0, pltpu.roll(part[2 * chans :], width - 1, 1))
        sums.append(part[chans : 2 * chans] + left + right)
    return sums


def row_pairs(top, bottom):
    return [(top, 0), (top, 1), (bottom, 0), (bottom, 1)]


def either_way(flag, near, own, body):
    @pl.when(~flag)
    def _():
        body(row_pairs(near, own))

    @pl.when(flag)
    def _():
        body(row_pairs(own, near))


def own_kernel(video, gamma_first, bias_first, gamma_second, bias_second, own, columns):
    for index, vector in enumerate((gamma_first, bias_first, gamma_second, bias_second)):
        columns[index] = jnp.broadcast_to(column(vector), columns.shape[1:])
    activate(video, own, columns[0])


def even_partner_below():
    return lax.rem(lax.axis_index("rows"), 2) == 0


def edge_kernel(valid):
    row_part = lax.axis_index("rows")
    one_below = even_partner_below()
    has_above = row_part > 0
    has_below = row_part < lax.axis_size("rows") - 1
    inside = (
        has_above | one_below,
        has_below | ~one_below,
        has_above | ~one_below,
        has_below | one_below,
        lax.axis_index("tm") > 0,
    )
    for index, flag in enumerate(inside):
        valid[index] = jnp.broadcast_to(jnp.where(flag, 1.0, 0.0), valid.shape[1:])


def present_frames(rows, first, columns, valid, base, partial, late):
    bias, gain = columns[1], columns[2]
    depth = first.shape[1] // 3
    frames = late.shape[0] + 2
    for frame in range(frames):
        count = min(frame + 1, 3)
        sums = conv_two_rows(first[:, (3 - count) * depth :], rows, frame + 1 - count, count, True)
        for side in range(2):
            hidden = sums[side] + bias
            if frame < 2:
                partial[frame, side] = hidden
            else:
                late[frame - 2, side] = (norm_silu(hidden, gain) * valid[base + side, 0:1]).astype(jnp.bfloat16)


def earlier_frames(rows, first, columns, valid, base, partial, early):
    bias, gain = columns[1], columns[2]
    depth = first.shape[1] // 3
    frames = rows[0][0].shape[0]
    for frame in range(4):
        count = min(3, 4 - frame)
        sums = conv_two_rows(first[:, : count * depth], rows, frames - 4 + frame, count, True)
        for side in range(2):
            if frame < 2:
                value = norm_silu(sums[side] + bias, gain) * valid[4, 0:1]
            else:
                value = norm_silu(sums[side] + partial[frame - 2, side], gain)
            early[frame, side] = (value * valid[base + side, 0:1]).astype(jnp.bfloat16)


def one_kernel(
    valid, one, own, kernel_first, kernel_second, columns,
    first, second, partial, late, active,
):
    one_below = even_partner_below()
    activate(one, active, columns[0])
    restack(kernel_first[...], first, True)
    restack(kernel_second[...], second, False)
    either_way(
        one_below, active, own, lambda rows: present_frames(rows, first, columns, valid, 0, partial, late)
    )


def two_kernel(
    valid, two, prior, prior_one, own, first, columns, partial_one,
    inner, partial, late, early, active, active_prior,
):
    one_below = even_partner_below()
    activate(two, active, columns[0])
    either_way(
        ~one_below, active, own, lambda rows: present_frames(rows, first, columns, valid, 2, partial, late)
    )
    activate(prior, inner, columns[0])
    activate(prior_one, active_prior, columns[0])
    either_way(
        one_below, active_prior, inner,
        lambda rows: earlier_frames(rows, first, columns, valid, 0, partial_one, early),
    )


def last_kernel(
    valid, video, prior_two, inner, first, second, columns, early_one, late_one, partial_two, late_two,
    encoded, active, near_one, near_two,
):
    one_below = even_partner_below()
    activate(prior_two, active, columns[0])
    near_one[0:4] = early_one[...]
    near_one[4:] = late_one[...]
    near_two[4:] = late_two[...]
    either_way(
        ~one_below, active, inner,
        lambda rows: earlier_frames(rows, first, columns, valid, 2, partial_two, near_two),
    )
    offset = columns[3]

    def finish(rows):
        for frame in range(video.shape[1]):
            sums = conv_two_rows(second[...], rows, frame, 3, False)
            for side in range(2):
                value = video[0, frame, side].astype(jnp.float32) + (sums[side] + offset)
                encoded[0, frame, side] = value.astype(jnp.bfloat16)

    either_way(one_below, near_one, near_two, finish)


def routed(block, goal):
    frame_parts, row_parts = lax.axis_size("tm"), lax.axis_size("rows")
    route = []
    for row in range(row_parts):
        for part in range(frame_parts):
            row_to, part_to = goal(row, part)
            if 0 <= row_to < row_parts and 0 <= part_to < frame_parts:
                route.append((row * frame_parts + part, row_to * frame_parts + part_to))
    return lax.ppermute(block, ("rows", "tm"), route)


def later(row, part):
    return row, part + 1


def even_pair(row, part):
    return row + 1 - 2 * (row % 2), part


def odd_pair(row, part):
    return row - 1 + 2 * (row % 2), part


def exchange(video):
    prior = routed(video, later)
    two = routed(video, odd_pair)
    one = routed(video, even_pair)
    prior_two = routed(prior, odd_pair)
    prior_one = routed(prior, even_pair)
    return one, two, prior, prior_one, prior_two


def local(video, gamma_first, kernel_first, bias_first, gamma_second, kernel_second, bias_second):
    _, frames, rows, chans, width = video.shape
    one, two, prior, prior_one, prior_two = exchange(video)
    bf16, f32 = jnp.bfloat16, jnp.float32
    shape = jax.ShapeDtypeStruct
    params = pltpu.CompilerParams(vmem_limit_bytes=24 * 2**20)

    def cost(millions):
        return pl.CostEstimate(flops=millions * 10**6, bytes_accessed=10**6, transcendentals=10**5)

    block = shape((frames, rows, chans, width), bf16)
    pair = shape((2, 2, chans, width), f32)
    late = shape((frames - 2, 2, chans, width), bf16)
    early = shape((4, 2, chans, width), bf16)
    in_vmem = pltpu.VMEM(block.shape, bf16)
    valid = pl.pallas_call(
        edge_kernel,
        out_shape=shape((5, 8, width), f32),
        out_specs=VMEM,
        compiler_params=params,
        cost_estimate=cost(2000),
    )()
    own, columns = pl.pallas_call(
        own_kernel,
        out_shape=(block, shape((4, chans, width), f32)),
        in_specs=[VMEM] * 5,
        out_specs=[VMEM] * 2,
        compiler_params=params,
        cost_estimate=cost(1000),
    )(video, gamma_first, bias_first, gamma_second, bias_second)
    first, second, partial_one, late_one = pl.pallas_call(
        one_kernel,
        out_shape=(shape((3 * chans, 12 * chans), bf16), shape((3 * chans, 9 * chans), bf16), pair, late),
        in_specs=[VMEM] * 6,
        out_specs=[VMEM] * 4,
        scratch_shapes=[in_vmem],
        compiler_params=params,
        cost_estimate=cost(1000),
    )(valid, one, own, kernel_first, kernel_second, columns)
    inner, partial_two, late_two, early_one = pl.pallas_call(
        two_kernel,
        out_shape=(block, pair, late, early),
        in_specs=[VMEM] * 8,
        out_specs=[VMEM] * 4,
        scratch_shapes=[in_vmem, in_vmem],
        compiler_params=params,
        cost_estimate=cost(1000),
    )(valid, two, prior, prior_one, own, first, columns, partial_one)
    return pl.pallas_call(
        last_kernel,
        out_shape=shape(video.shape, bf16),
        in_specs=[VMEM] * 11,
        out_specs=VMEM,
        scratch_shapes=[in_vmem] + [pltpu.VMEM((frames + 2, 2, chans, width), bf16)] * 2,
        compiler_params=params,
        cost_estimate=cost(1000),
    )(valid, video, prior_two, inner, first, second, columns, early_one, late_one, partial_two, late_two)


def solution(mesh):
    in_specs = (P("groups", "tm", "rows", None, None), P(), P(), P(), P(), P(), P())
    out_specs = P("groups", "tm", "rows", None, None)
    return jax.shard_map(local, mesh=mesh, in_specs=in_specs, out_specs=out_specs, check_vma=False)
```

time: 39.9 us -> 20.5 us (0.51)
  the two profiles are of different devices: /device:TPU:1 before, /device:TPU:0 now
where the time goes in v2:
time: 20.5 us; the launch traced here: 20.4 us
  starting transfers between devices  10.9 us (53%)
  Pallas kernels  6.46 us (32%)
  waiting for transfers between devices  2.71 us (13%)
    ppermute x5, starting transfers between devices, routed(): return lax.ppermute(block, ('rows', 'tm'), route)  10.9 us
    ppermute x5, waiting for transfers between devices, routed(): return lax.ppermute(block, ('rows', 'tm'), route)  2.71 us
    pallas_call x1, Pallas kernels, local(): pl.pallas_call(last_kernel, out_shape=shape(video.shape, bf16), in_specs=...  2.64 us
    pallas_call x1, Pallas kernels, local(): pl.pallas_call(two_kernel, out_shape=(block, pair, late, early), in_specs...  2.27 us
    pallas_call x1, Pallas kernels, local(): pl.pallas_call(one_kernel, out_shape=(shape((3 * chans, 12 * chans), bf16...  1.4 us
  transfers between devices with their start and end apart: 5, of which 1 were waited for; matrix products, arithmetic and copies ran while one was open for 0% of the time, Pallas kernels for 19%

profile of v2, /device:TPU:0, one launch (start us, length us, event | category | flops | bytes accessed | tf_op | source)
XLA Modules:
  0.0 20.4 jit_solution(11051789095683442227)
XLA Ops:
  0.0 0.0 copy-start.2
  0.0 0.0 copy-start.4
  0.0 0.0 copy-start.5
  0.0 0.0 copy-start.6
  0.0 0.0 copy-start.3
  0.0 2.5 %collective-permute-start = (bf16[1,4,2,96,128]{4,3,2,1,0:T(8,128)(2,1)}, bf16[1,4,2,96,128]{4,3,2,1,0:T(8,128)(2,1)S(1)}, u32[]{:S(2)}, u32[]{:S(2)}) collective-permute-start(bf16[1,4,2,96,128]{4,3,2,1,0:T(8,128)(2,1)} %video.3), channel_id=1, source_target_pairs={{0,1},{1,2},{2,3},{4,5},{5,6},{6,7},{8,9},{9,10},{10,11},{12,13},{... | collective-permute-start | bytes 589832 | tf_op jit(solution)/shard_map/ppermute | solution.py:200
  2.5 2.5 %collective-permute-start.4 = (bf16[1,4,2,96,128]{4,3,2,1,0:T(8,128)(2,1)}, bf16[1,4,2,96,128]{4,3,2,1,0:T(8,128)(2,1)S(1)}, u32[]{:S(2)}, u32[]{:S(2)}) collective-permute-start(bf16[1,4,2,96,128]{4,3,2,1,0:T(8,128)(2,1)} %video.3), channel_id=1, source_target_pairs={{0,4},{1,5},{2,6},{3,7},{4,0},{5,1},{6,2},{7,3},{8,12},{9,13},{10,... | collective-permute-start | bytes 589832 | tf_op jit(solution)/shard_map/ppermute | solution.py:200
  5.0 0.7 %collective-permute-start.2 = (bf16[1,4,2,96,128]{4,3,2,1,0:T(8,128)(2,1)}, bf16[1,4,2,96,128]{4,3,2,1,0:T(8,128)(2,1)S(1)}, u32[]{:S(2)}, u32[]{:S(2)}) collective-permute-start(bf16[1,4,2,96,128]{4,3,2,1,0:T(8,128)(2,1)} %video.3), channel_id=1, source_target_pairs={{4,8},{5,9},{6,10},{7,11},{8,4},{9,5},{10,6},{11,7},{20,24},{21,25... | collective-permute-start | bytes 589832 | tf_op jit(solution)/shard_map/ppermute | solution.py:200
  5.7 0.0 collective-permute-done.prior
  5.7 4.5 %collective-permute-start.3 = (bf16[1,4,2,96,128]{4,3,2,1,0:T(8,128)(2,1)S(1)}, bf16[1,4,2,96,128]{4,3,2,1,0:T(8,128)(2,1)S(1)}, u32[]{:S(2)}, u32[]{:S(2)}) collective-permute-start(bf16[1,4,2,96,128]{4,3,2,1,0:T(8,128)(2,1)S(1)} %collective-permute-done.prior), channel_id=1, source_target_pairs={{0,4},{1,5},{2,6},{3,7},{4,0},{5,1},{6,2},{7,3},{8,12},{9,13},{10,... | collective-permute-start | bytes 589832 | tf_op jit(solution)/shard_map/ppermute | solution.py:200
  10.1 0.0 copy-start
  10.1 0.0 copy-start.1
  10.2 0.8 %collective-permute-start.1 = (bf16[1,4,2,96,128]{4,3,2,1,0:T(8,128)(2,1)S(1)}, bf16[1,4,2,96,128]{4,3,2,1,0:T(8,128)(2,1)S(1)}, u32[]{:S(2)}, u32[]{:S(2)}) collective-permute-start(bf16[1,4,2,96,128]{4,3,2,1,0:T(8,128)(2,1)S(1)} %collective-permute-done.prior), channel_id=1, source_target_pairs={{4,8},{5,9},{6,10},{7,11},{8,4},{9,5},{10,6},{11,7},{20,24},{21,25... | collective-permute-start | bytes 589832 | tf_op jit(solution)/shard_map/ppermute | solution.py:200
  11.0 0.0 copy-done.2
  11.0 0.0 copy-done.4
  11.0 0.0 copy-done.5
  11.0 0.0 copy-done.6
  11.0 0.0 copy-done.3
  11.0 0.2 shard_map.74
  11.2 0.0 collective-permute-done.4.one
  11.2 0.0 copy-done
  11.2 0.1 copy-done.1
  11.3 1.4 %shard_map.75 = (bf16[288,1152]{1,0:T(8,128)(2,1)S(1)}, bf16[288,864]{1,0:T(8,128)(2,1)S(1)}, f32[2,2,96,128]{3,2,1,0:T(8,128)S(1)}, bf16[2,2,96,128]{3,2,1,0:T(8,128)(2,1)S(1)}) custom-call(f32[5,8,128]{2,1,0:T(8,128)S(1)} %shard_map.73.valid, bf16[1,4,2,96,128]{4,3,2,1,0:T(8,128)(2,1)S(1)} %collective-permute-done.4.one, ...), custom_call_target="tpu_custom_call" | custom-call | flops 1000000000 | bytes 1000000 | tf_op jit(solution)/shard_map/pallas_call | solution.py:254
  12.7 0.0 collective-permute-done.2.two
  12.8 2.7 %collective-permute-done.3.prior_one = bf16[1,4,2,96,128]{4,3,2,1,0:T(8,128)(2,1)S(1)} collective-permute-done((bf16[1,4,2,96,128]{4,3,2,1,0:T(8,128)(2,1)S(1)}, bf16[1,4,2,96,128]{4,3,2,1,0:T(8,128)(2,1)S(1)}, u32[]{:S(2)}, u32[]{:S(2)}) %collective-permute-start.3) | collective-permute-done | bytes 196640 | tf_op jit(solution)/shard_map/ppermute | solution.py:200
  15.5 2.3 %shard_map.76 = (bf16[4,2,96,128]{3,2,1,0:T(8,128)(2,1)S(1)}, f32[2,2,96,128]{3,2,1,0:T(8,128)S(1)}, bf16[2,2,96,128]{3,2,1,0:T(8,128)(2,1)S(1)}, bf16[4,2,96,128]{3,2,1,0:T(8,128)(2,1)S(1)}) custom-call(f32[5,8,128]{2,1,0:T(8,128)S(1)} %shard_map.73.valid, bf16[1,4,2,96,128]{4,3,2,1,0:T(8,128)(2,1)S(1)} %collective-permute-done.2.two, ...), custom_call_target="tpu_custom_call" | custom-call | flops 1000000000 | bytes 1000000 | tf_op jit(solution)/shard_map/pallas_call | solution.py:263
  17.7 0.0 collective-permute-done.1.prior_two
  17.7 2.6 %shard_map.77 = bf16[1,4,2,96,128]{4,3,2,1,0:T(8,128)(2,1)} custom-call(f32[5,8,128]{2,1,0:T(8,128)S(1)} %shard_map.73.valid, bf16[1,4,2,96,128]{4,3,2,1,0:T(8,128)(2,1)S(1)} %copy-done.2, bf16[1,4,2,96,128]{4,3,2,1,0:T(8,128)(2,1)S(1)} %collective-permute-done.1.prior_two, bf16[4,2,96,128]{3,2,1,0:T(8,128)(2,1)S(1)} %get-tuple-element.19.inner, ...), custom_call_target="tpu_custom_call" | custom-call | flops 1000000000 | bytes 1000000 | tf_op jit(solution)/shard_map/pallas_call | solution.py:272
  (1 shorter events, 0.0 us)
Async XLA Ops:
  0.0 11.0 %copy-start.2 = (bf16[1,4,2,96,128]{4,3,2,1,0:T(8,128)(2,1)S(1)}, bf16[1,4,2,96,128]{4,3,2,1,0:T(8,128)(2,1)}, u32[]{:S(2)}) copy-start(bf16[1,4,2,96,128]{4,3,2,1,0:T(8,128)(2,1)} %video.3) | copy-start | bytes 589828
  0.0 11.0 %copy-start.4 = (f32[96]{0:T(128)S(1)}, f32[96]{0:T(128)}, u32[]{:S(2)}) copy-start(f32[96]{0:T(128)} %bias_first.1) | copy-start | bytes 1156
  0.0 11.0 %copy-start.5 = (f32[96]{0:T(128)S(1)}, f32[96]{0:T(128)}, u32[]{:S(2)}) copy-start(f32[96]{0:T(128)} %gamma_second.1) | copy-start | bytes 1156
  0.0 11.0 %copy-start.6 = (f32[96]{0:T(128)S(1)}, f32[96]{0:T(128)}, u32[]{:S(2)}) copy-start(f32[96]{0:T(128)} %bias_second.1) | copy-start | bytes 1156
  0.0 11.0 %copy-start.3 = (f32[96]{0:T(128)S(1)}, f32[96]{0:T(128)}, u32[]{:S(2)}) copy-start(f32[96]{0:T(128)} %gamma_first.1) | copy-start | bytes 1156
  0.0 5.7 %collective-permute-start = (bf16[1,4,2,96,128]{4,3,2,1,0:T(8,128)(2,1)}, bf16[1,4,2,96,128]{4,3,2,1,0:T(8,128)(2,1)S(1)}, u32[]{:S(2)}, u32[]{:S(2)}) collective-permute-start(bf16[1,4,2,96,128]{4,3,2,1,0:T(8,128)(2,1)} %video.3), channel_id=1, source_target_pairs={{0,1},{1,2},{2,3},{4,5},{5,6},{6,7},{8,9},{9,10},{10,11},{12,13},{... | collective-permute-start | bytes 589832 | tf_op jit(solution)/shard_map/ppermute | solution.py:200
  2.5 8.6 %collective-permute-start.4 = (bf16[1,4,2,96,128]{4,3,2,1,0:T(8,128)(2,1)}, bf16[1,4,2,96,128]{4,3,2,1,0:T(8,128)(2,1)S(1)}, u32[]{:S(2)}, u32[]{:S(2)}) collective-permute-start(bf16[1,4,2,96,128]{4,3,2,1,0:T(8,128)(2,1)} %video.3), channel_id=1, source_target_pairs={{0,4},{1,5},{2,6},{3,7},{4,0},{5,1},{6,2},{7,3},{8,12},{9,13},{10,... | collective-permute-start | bytes 589832 | tf_op jit(solution)/shard_map/ppermute | solution.py:200
  5.0 7.7 %collective-permute-start.2 = (bf16[1,4,2,96,128]{4,3,2,1,0:T(8,128)(2,1)}, bf16[1,4,2,96,128]{4,3,2,1,0:T(8,128)(2,1)S(1)}, u32[]{:S(2)}, u32[]{:S(2)}) collective-permute-start(bf16[1,4,2,96,128]{4,3,2,1,0:T(8,128)(2,1)} %video.3), channel_id=1, source_target_pairs={{4,8},{5,9},{6,10},{7,11},{8,4},{9,5},{10,6},{11,7},{20,24},{21,25... | collective-permute-start | bytes 589832 | tf_op jit(solution)/shard_map/ppermute | solution.py:200
  5.7 9.8 %collective-permute-start.3 = (bf16[1,4,2,96,128]{4,3,2,1,0:T(8,128)(2,1)S(1)}, bf16[1,4,2,96,128]{4,3,2,1,0:T(8,128)(2,1)S(1)}, u32[]{:S(2)}, u32[]{:S(2)}) collective-permute-start(bf16[1,4,2,96,128]{4,3,2,1,0:T(8,128)(2,1)S(1)} %collective-permute-done.prior), channel_id=1, source_target_pairs={{0,4},{1,5},{2,6},{3,7},{4,0},{5,1},{6,2},{7,3},{8,12},{9,13},{10,... | collective-permute-start | bytes 589832 | tf_op jit(solution)/shard_map/ppermute | solution.py:200
  10.1 1.0 %copy-start = (bf16[96,2592]{1,0:T(8,128)(2,1)S(1)}, bf16[96,2592]{1,0:T(8,128)(2,1)}, u32[]{:S(2)}) copy-start(bf16[96,2592]{1,0:T(8,128)(2,1)} %kernel_first.1) | copy-start | bytes 1492996
  10.1 1.2 %copy-start.1 = (bf16[96,2592]{1,0:T(8,128)(2,1)S(1)}, bf16[96,2592]{1,0:T(8,128)(2,1)}, u32[]{:S(2)}) copy-start(bf16[96,2592]{1,0:T(8,128)(2,1)} %kernel_second.1) | copy-start | bytes 1492996
  10.2 7.6 %collective-permute-start.1 = (bf16[1,4,2,96,128]{4,3,2,1,0:T(8,128)(2,1)S(1)}, bf16[1,4,2,96,128]{4,3,2,1,0:T(8,128)(2,1)S(1)}, u32[]{:S(2)}, u32[]{:S(2)}) collective-permute-start(bf16[1,4,2,96,128]{4,3,2,1,0:T(8,128)(2,1)S(1)} %collective-permute-done.prior), channel_id=1, source_target_pairs={{4,8},{5,9},{6,10},{7,11},{8,4},{9,5},{10,6},{11,7},{20,24},{21,25... | collective-permute-start | bytes 589832 | tf_op jit(solution)/shard_map/ppermute | solution.py:200

commit v3 on v2

--- a/solution.py
+++ b/solution.py
@@ -93,12 +93,19 @@
     one_below = even_partner_below()
     has_above = row_part > 0
     has_below = row_part < lax.axis_size("rows") - 1
+    later = lax.axis_index("tm") > 0
+    has_one = (one_below & has_below) | (~one_below & has_above)
+    has_two = (one_below & has_above) | (~one_below & has_below)
     inside = (
         has_above | one_below,
         has_below | ~one_below,
         has_above | ~one_below,
         has_below | one_below,
-        lax.axis_index("tm") > 0,
+        later,
+        has_one,
+        has_two,
+        later & has_one,
+        later & has_two,
     )
     for index, flag in enumerate(inside):
         valid[index] = jnp.broadcast_to(jnp.where(flag, 1.0, 0.0), valid.shape[1:])
@@ -139,7 +146,7 @@
     first, second, partial, late, active,
 ):
     one_below = even_partner_below()
-    activate(one, active, columns[0])
+    activate(one, active, columns[0] * valid[5, 0:1])
     restack(kernel_first[...], first, True)
     restack(kernel_second[...], second, False)
     either_way(
@@ -147,20 +154,20 @@
     )
 
 
-def two_kernel(
-    valid, two, prior, prior_one, own, first, columns, partial_one,
-    inner, partial, late, early, active, active_prior,
-):
-    one_below = even_partner_below()
-    activate(two, active, columns[0])
+def two_kernel(valid, two, prior, own, first, columns, inner, partial, late, active):
+    one_below = even_partner_below()
+    activate(two, active, columns[0] * valid[6, 0:1])
+    activate(prior, inner, columns[0] * valid[4, 0:1])
     either_way(
         ~one_below, active, own, lambda rows: present_frames(rows, first, columns, valid, 2, partial, late)
     )
-    activate(prior, inner, columns[0])
-    activate(prior_one, active_prior, columns[0])
+
+
+def prior_kernel(valid, prior_one, inner, first, columns, partial, early, active):
+    one_below = even_partner_below()
+    activate(prior_one, active, columns[0] * valid[7, 0:1])
     either_way(
-        one_below, active_prior, inner,
-        lambda rows: earlier_frames(rows, first, columns, valid, 0, partial_one, early),
+        one_below, active, inner, lambda rows: earlier_frames(rows, first, columns, valid, 0, partial, early)
     )
 
 
@@ -169,7 +176,7 @@
     encoded, active, near_one, near_two,
 ):
     one_below = even_partner_below()
-    activate(prior_two, active, columns[0])
+    activate(prior_two, active, columns[0] * valid[8, 0:1])
     near_one[0:4] = early_one[...]
     near_one[4:] = late_one[...]
     near_two[4:] = late_two[...]
@@ -190,26 +197,31 @@
 
 
 def routed(block, goal):
-    frame_parts, row_parts = lax.axis_size("tm"), lax.axis_size("rows")
+    row_parts, frame_parts = lax.axis_size("rows"), lax.axis_size("tm")
     route = []
     for row in range(row_parts):
         for part in range(frame_parts):
-            row_to, part_to = goal(row, part)
-            if 0 <= row_to < row_parts and 0 <= part_to < frame_parts:
-                route.append((row * frame_parts + part, row_to * frame_parts + part_to))
+            row_to, part_to = goal(row, part, row_parts, frame_parts)
+            route.append((row * frame_parts + part, row_to * frame_parts + part_to))
     return lax.ppermute(block, ("rows", "tm"), route)
 
 
-def later(row, part):
-    return row, part + 1
-
-
-def even_pair(row, part):
-    return row + 1 - 2 * (row % 2), part
-
-
-def odd_pair(row, part):
-    return row - 1 + 2 * (row % 2), part
+def later(row, part, row_parts, frame_parts):
+    return row, (part + 1) % frame_parts
+
+
+def paired(row, part, partner, row_parts, frame_parts):
+    if 0 <= partner < row_parts:
+        return partner, part
+    return row, min(part ^ 1, frame_parts - 1)
+
+
+def even_pair(row, part, row_parts, frame_parts):
+    return paired(row, part, row + 1 - 2 * (row % 2), row_parts, frame_parts)
+
+
+def odd_pair(row, part, row_parts, frame_parts):
+    return paired(row, part, row - 1 + 2 * (row % 2), row_parts, frame_parts)
 
 
 def exchange(video):
@@ -238,7 +250,7 @@
     in_vmem = pltpu.VMEM(block.shape, bf16)
     valid = pl.pallas_call(
         edge_kernel,
-        out_shape=shape((5, 8, width), f32),
+        out_shape=shape((9, 8, width), f32),
         out_specs=VMEM,
         compiler_params=params,
         cost_estimate=cost(2000),
@@ -260,15 +272,24 @@
         compiler_params=params,
         cost_estimate=cost(1000),
     )(valid, one, own, kernel_first, kernel_second, columns)
-    inner, partial_two, late_two, early_one = pl.pallas_call(
+    inner, partial_two, late_two = pl.pallas_call(
         two_kernel,
-        out_shape=(block, pair, late, early),
-        in_specs=[VMEM] * 8,
-        out_specs=[VMEM] * 4,
-        scratch_shapes=[in_vmem, in_vmem],
-        compiler_params=params,
-        cost_estimate=cost(1000),
-    )(valid, two, prior, prior_one, own, first, columns, partial_one)
+        out_shape=(block, pair, late),
+        in_specs=[VMEM] * 6,
+        out_specs=[VMEM] * 3,
+        scratch_shapes=[in_vmem],
+        compiler_params=params,
+        cost_estimate=cost(1000),
+    )(valid, two, prior, own, first, columns)
+    early_one = pl.pallas_call(
+        prior_kernel,
+        out_shape=early,
+        in_specs=[VMEM] * 6,
+        out_specs=VMEM,
+        scratch_shapes=[in_vmem],
+        compiler_params=params,
+        cost_estimate=cost(1000),
+    )(valid, prior_one, inner, first, columns, partial_one)
     return pl.pallas_call(
         last_kernel,
         out_shape=shape(video.shape, bf16),

time: 20.5 us -> 17.2 us (0.84)
  starting transfers between devices: 10.9 us -> 6.87 us
  waiting for transfers between devices: 2.71 us -> 3.58 us
    ppermute x5, starting transfers between devices: 10.9 us -> 6.87 us  [routed(): return lax.ppermute(block, ('rows', 'tm'), route)]
    ppermute x5, waiting for transfers between devices: 2.71 us -> 3.58 us  [routed(): return lax.ppermute(block, ('rows', 'tm'), route)]
    pallas_call x2 -> x3, Pallas kernels: 2.27 us -> 2.29 us  [the longest x1 1.23 us: local(): pl.pallas_call(two_kernel, out_shape=(block, pair, late), in_specs=[VMEM]...]
  transfers between devices with their start and end apart: 5 -> 5, of which waited for: 1 -> 2; matrix products, arithmetic and copies ran while one was open for 0% -> 0% of each run, Pallas kernels for 19% -> 22%
where the time goes in v3:
time: 17.2 us; the launch traced here: 17.1 us
  starting transfers between devices  6.87 us (40%)
  Pallas kernels  6.49 us (38%)
  waiting for transfers between devices  3.58 us (21%)
    ppermute x5, starting transfers between devices, routed(): return lax.ppermute(block, ('rows', 'tm'), route)  6.87 us
    ppermute x5, waiting for transfers between devices, routed(): return lax.ppermute(block, ('rows', 'tm'), route)  3.58 us
    pallas_call x1, Pallas kernels, local(): pl.pallas_call(last_kernel, out_shape=shape(video.shape, bf16), in_specs=...  2.64 us
    pallas_call x1, Pallas kernels, local(): pl.pallas_call(one_kernel, out_shape=(shape((3 * chans, 12 * chans), bf16...  1.4 us
    pallas_call x1, Pallas kernels, local(): pl.pallas_call(two_kernel, out_shape=(block, pair, late), in_specs=[VMEM]...  1.23 us
    pallas_call x1, Pallas kernels, local(): pl.pallas_call(prior_kernel, out_shape=early, in_specs=[VMEM] * 6, out_sp...  1.06 us
  transfers between devices with their start and end apart: 5, of which 2 were waited for; matrix products, arithmetic and copies ran while one was open for 0% of the time, Pallas kernels for 22%

profile of v3, /device:TPU:0, one launch (start us, length us, event | category | flops | bytes accessed | tf_op | source)
XLA Modules:
  0.0 17.1 jit_solution(1525607628168897357)
XLA Ops:
  0.0 0.0 copy-start.2
  0.0 0.0 copy-start.4
  0.0 0.0 copy-start.5
  0.0 0.0 copy-start.6
  0.0 0.0 copy-start.3
  0.0 0.5 %collective-permute-start = (bf16[1,4,2,96,128]{4,3,2,1,0:T(8,128)(2,1)}, bf16[1,4,2,96,128]{4,3,2,1,0:T(8,128)(2,1)S(1)}, u32[]{:S(2)}, u32[]{:S(2)}) collective-permute-start(bf16[1,4,2,96,128]{4,3,2,1,0:T(8,128)(2,1)} %video.3), channel_id=1, source_target_pairs={{0,1},{1,2},{2,3},{3,0},{4,5},{5,6},{6,7},{7,4},{8,9},{9,10},{10,1... | collective-permute-start | bytes 589832 | tf_op jit(solution)/shard_map/ppermute | solution.py:206
  0.5 2.6 %collective-permute-start.3 = (bf16[1,4,2,96,128]{4,3,2,1,0:T(8,128)(2,1)}, bf16[1,4,2,96,128]{4,3,2,1,0:T(8,128)(2,1)S(1)}, u32[]{:S(2)}, u32[]{:S(2)}) collective-permute-start(bf16[1,4,2,96,128]{4,3,2,1,0:T(8,128)(2,1)} %video.3), channel_id=1, source_target_pairs={{0,4},{1,5},{2,6},{3,7},{4,0},{5,1},{6,2},{7,3},{8,12},{9,13},{10,... | collective-permute-start | bytes 589832 | tf_op jit(solution)/shard_map/ppermute | solution.py:206
  3.2 1.2 %collective-permute-start.2 = (bf16[1,4,2,96,128]{4,3,2,1,0:T(8,128)(2,1)}, bf16[1,4,2,96,128]{4,3,2,1,0:T(8,128)(2,1)S(1)}, u32[]{:S(2)}, u32[]{:S(2)}) collective-permute-start(bf16[1,4,2,96,128]{4,3,2,1,0:T(8,128)(2,1)} %video.3), channel_id=1, source_target_pairs={{0,1},{1,0},{2,3},{3,2},{4,8},{5,9},{6,10},{7,11},{8,4},{9,5},{10,... | collective-permute-start | bytes 589832 | tf_op jit(solution)/shard_map/ppermute | solution.py:206
  4.4 0.0 copy-start
  4.4 0.0 copy-start.1
  4.5 1.6 %collective-permute-done.prior = bf16[1,4,2,96,128]{4,3,2,1,0:T(8,128)(2,1)S(1)} collective-permute-done((bf16[1,4,2,96,128]{4,3,2,1,0:T(8,128)(2,1)}, bf16[1,4,2,96,128]{4,3,2,1,0:T(8,128)(2,1)S(1)}, u32[]{:S(2)}, u32[]{:S(2)}) %collective-permute-start) | collective-permute-done | bytes 196640 | tf_op jit(solution)/shard_map/ppermute | solution.py:206
  6.0 2.4 %collective-permute-start.4 = (bf16[1,4,2,96,128]{4,3,2,1,0:T(8,128)(2,1)S(1)}, bf16[1,4,2,96,128]{4,3,2,1,0:T(8,128)(2,1)S(1)}, u32[]{:S(2)}, u32[]{:S(2)}) collective-permute-start(bf16[1,4,2,96,128]{4,3,2,1,0:T(8,128)(2,1)S(1)} %collective-permute-done.prior), channel_id=1, source_target_pairs={{0,4},{1,5},{2,6},{3,7},{4,0},{5,1},{6,2},{7,3},{8,12},{9,13},{10,... | collective-permute-start | bytes 589832 | tf_op jit(solution)/shard_map/ppermute | solution.py:206
  8.4 0.0 copy-done.2
  8.4 0.0 copy-done.4
  8.4 0.0 copy-done.5
  8.4 0.0 copy-done.6
  8.4 0.0 copy-done.3
  8.4 0.2 shard_map.74
  8.6 0.1 collective-permute-start.1
  8.7 0.0 collective-permute-done.3.one
  8.7 0.0 copy-done
  8.7 0.0 copy-done.1
  8.7 1.4 %shard_map.75 = (bf16[288,1152]{1,0:T(8,128)(2,1)S(1)}, bf16[288,864]{1,0:T(8,128)(2,1)S(1)}, f32[2,2,96,128]{3,2,1,0:T(8,128)S(1)}, bf16[2,2,96,128]{3,2,1,0:T(8,128)(2,1)S(1)}) custom-call(f32[9,8,128]{2,1,0:T(8,128)S(1)} %shard_map.73.valid, bf16[1,4,2,96,128]{4,3,2,1,0:T(8,128)(2,1)S(1)} %collective-permute-done.3.one, ...), custom_call_target="tpu_custom_call" | custom-call | flops 1000000000 | bytes 1000000 | tf_op jit(solution)/shard_map/pallas_call | solution.py:266
  10.1 0.0 collective-permute-done.2.two
  10.1 1.2 %shard_map.76 = (bf16[4,2,96,128]{3,2,1,0:T(8,128)(2,1)S(1)}, f32[2,2,96,128]{3,2,1,0:T(8,128)S(1)}, bf16[2,2,96,128]{3,2,1,0:T(8,128)(2,1)S(1)}) custom-call(f32[9,8,128]{2,1,0:T(8,128)S(1)} %shard_map.73.valid, bf16[1,4,2,96,128]{4,3,2,1,0:T(8,128)(2,1)S(1)} %collective-permute-done.2.two, bf16[1,4,2,96,128]{4,3,2,1,0:T(8,128)(2,1)S(1)} %collective-permute-done.prior, ...), custom_call_target="tpu_custom_call" | custom-call | flops 1000000000 | bytes 1000000 | tf_op jit(solution)/shard_map/pallas_call | solution.py:275
  11.4 2.0 %collective-permute-done.4.prior_one = bf16[1,4,2,96,128]{4,3,2,1,0:T(8,128)(2,1)S(1)} collective-permute-done((bf16[1,4,2,96,128]{4,3,2,1,0:T(8,128)(2,1)S(1)}, bf16[1,4,2,96,128]{4,3,2,1,0:T(8,128)(2,1)S(1)}, u32[]{:S(2)}, u32[]{:S(2)}) %collective-permute-start.4) | collective-permute-done | bytes 196640 | tf_op jit(solution)/shard_map/ppermute | solution.py:206
  13.4 1.1 %shard_map.77.early_one = bf16[4,2,96,128]{3,2,1,0:T(8,128)(2,1)S(1)} custom-call(f32[9,8,128]{2,1,0:T(8,128)S(1)} %shard_map.73.valid, bf16[1,4,2,96,128]{4,3,2,1,0:T(8,128)(2,1)S(1)} %collective-permute-done.4.prior_one, bf16[4,2,96,128]{3,2,1,0:T(8,128)(2,1)S(1)} %get-tuple-element.17.inner, bf16[288,1152]{1,0:T(8,128)(2,1)S(1)} %get-tuple-element.16.first, ...), custom_call_target="tpu_custom_call" | custom-call | flops 1000000000 | bytes 1000000 | tf_op jit(solution)/shard_map/pallas_call | solution.py:284
  14.4 0.0 collective-permute-done.1.prior_two
  14.4 2.6 %shard_map.78 = bf16[1,4,2,96,128]{4,3,2,1,0:T(8,128)(2,1)} custom-call(f32[9,8,128]{2,1,0:T(8,128)S(1)} %shard_map.73.valid, bf16[1,4,2,96,128]{4,3,2,1,0:T(8,128)(2,1)S(1)} %copy-done.2, bf16[1,4,2,96,128]{4,3,2,1,0:T(8,128)(2,1)S(1)} %collective-permute-done.1.prior_two, bf16[4,2,96,128]{3,2,1,0:T(8,128)(2,1)S(1)} %get-tuple-element.17.inner, ...), custom_call_target="tpu_custom_call" | custom-call | flops 1000000000 | bytes 1000000 | tf_op jit(solution)/shard_map/pallas_call | solution.py:293
  (1 shorter events, 0.0 us)
Async XLA Ops:
  0.0 8.4 %copy-start.2 = (bf16[1,4,2,96,128]{4,3,2,1,0:T(8,128)(2,1)S(1)}, bf16[1,4,2,96,128]{4,3,2,1,0:T(8,128)(2,1)}, u32[]{:S(2)}) copy-start(bf16[1,4,2,96,128]{4,3,2,1,0:T(8,128)(2,1)} %video.3) | copy-start | bytes 589828
  0.0 8.4 %copy-start.4 = (f32[96]{0:T(128)S(1)}, f32[96]{0:T(128)}, u32[]{:S(2)}) copy-start(f32[96]{0:T(128)} %bias_first.1) | copy-start | bytes 1156
  0.0 8.4 %copy-start.5 = (f32[96]{0:T(128)S(1)}, f32[96]{0:T(128)}, u32[]{:S(2)}) copy-start(f32[96]{0:T(128)} %gamma_second.1) | copy-start | bytes 1156
  0.0 8.4 %copy-start.6 = (f32[96]{0:T(128)S(1)}, f32[96]{0:T(128)}, u32[]{:S(2)}) copy-start(f32[96]{0:T(128)} %bias_second.1) | copy-start | bytes 1156
  0.0 8.4 %copy-start.3 = (f32[96]{0:T(128)S(1)}, f32[96]{0:T(128)}, u32[]{:S(2)}) copy-start(f32[96]{0:T(128)} %gamma_first.1) | copy-start | bytes 1156
  0.0 6.0 %collective-permute-start = (bf16[1,4,2,96,128]{4,3,2,1,0:T(8,128)(2,1)}, bf16[1,4,2,96,128]{4,3,2,1,0:T(8,128)(2,1)S(1)}, u32[]{:S(2)}, u32[]{:S(2)}) collective-permute-start(bf16[1,4,2,96,128]{4,3,2,1,0:T(8,128)(2,1)} %video.3), channel_id=1, source_target_pairs={{0,1},{1,2},{2,3},{3,0},{4,5},{5,6},{6,7},{7,4},{8,9},{9,10},{10,1... | collective-permute-start | bytes 589832 | tf_op jit(solution)/shard_map/ppermute | solution.py:206
  0.5 8.1 %collective-permute-start.3 = (bf16[1,4,2,96,128]{4,3,2,1,0:T(8,128)(2,1)}, bf16[1,4,2,96,128]{4,3,2,1,0:T(8,128)(2,1)S(1)}, u32[]{:S(2)}, u32[]{:S(2)}) collective-permute-start(bf16[1,4,2,96,128]{4,3,2,1,0:T(8,128)(2,1)} %video.3), channel_id=1, source_target_pairs={{0,4},{1,5},{2,6},{3,7},{4,0},{5,1},{6,2},{7,3},{8,12},{9,13},{10,... | collective-permute-start | bytes 589832 | tf_op jit(solution)/shard_map/ppermute | solution.py:206
  3.2 6.9 %collective-permute-start.2 = (bf16[1,4,2,96,128]{4,3,2,1,0:T(8,128)(2,1)}, bf16[1,4,2,96,128]{4,3,2,1,0:T(8,128)(2,1)S(1)}, u32[]{:S(2)}, u32[]{:S(2)}) collective-permute-start(bf16[1,4,2,96,128]{4,3,2,1,0:T(8,128)(2,1)} %video.3), channel_id=1, source_target_pairs={{0,1},{1,0},{2,3},{3,2},{4,8},{5,9},{6,10},{7,11},{8,4},{9,5},{10,... | collective-permute-start | bytes 589832 | tf_op jit(solution)/shard_map/ppermute | solution.py:206
  4.4 4.2 %copy-start = (bf16[96,2592]{1,0:T(8,128)(2,1)S(1)}, bf16[96,2592]{1,0:T(8,128)(2,1)}, u32[]{:S(2)}) copy-start(bf16[96,2592]{1,0:T(8,128)(2,1)} %kernel_first.1) | copy-start | bytes 1492996
  4.4 4.2 %copy-start.1 = (bf16[96,2592]{1,0:T(8,128)(2,1)S(1)}, bf16[96,2592]{1,0:T(8,128)(2,1)}, u32[]{:S(2)}) copy-start(bf16[96,2592]{1,0:T(8,128)(2,1)} %kernel_second.1) | copy-start | bytes 1492996
  6.0 7.3 %collective-permute-start.4 = (bf16[1,4,2,96,128]{4,3,2,1,0:T(8,128)(2,1)S(1)}, bf16[1,4,2,96,128]{4,3,2,1,0:T(8,128)(2,1)S(1)}, u32[]{:S(2)}, u32[]{:S(2)}) collective-permute-start(bf16[1,4,2,96,128]{4,3,2,1,0:T(8,128)(2,1)S(1)} %collective-permute-done.prior), channel_id=1, source_target_pairs={{0,4},{1,5},{2,6},{3,7},{4,0},{5,1},{6,2},{7,3},{8,12},{9,13},{10,... | collective-permute-start | bytes 589832 | tf_op jit(solution)/shard_map/ppermute | solution.py:206
  8.6 5.8 %collective-permute-start.1 = (bf16[1,4,2,96,128]{4,3,2,1,0:T(8,128)(2,1)S(1)}, bf16[1,4,2,96,128]{4,3,2,1,0:T(8,128)(2,1)S(1)}, u32[]{:S(2)}, u32[]{:S(2)}) collective-permute-start(bf16[1,4,2,96,128]{4,3,2,1,0:T(8,128)(2,1)S(1)} %collective-permute-done.prior), channel_id=1, source_target_pairs={{0,1},{1,0},{2,3},{3,2},{4,8},{5,9},{6,10},{7,11},{8,4},{9,5},{10,... | collective-permute-start | bytes 589832 | tf_op jit(solution)/shard_map/ppermute | solution.py:206

commit v4 on v0

v4 whole, which is shorter than its diff:
```python
import jax
import jax.numpy as jnp
from jax import lax
from jax.experimental import pallas as pl
from jax.experimental.pallas import tpu as pltpu
from jax.sharding import PartitionSpec as P

epsilon = 1e-06
VMEM = pl.BlockSpec(memory_space=pltpu.VMEM)


def column(vector_ref):
    row = vector_ref[...].reshape(1, -1)
    count = row.shape[1]
    down = lax.broadcasted_iota(jnp.int32, (count, count), 0)
    across = lax.broadcasted_iota(jnp.int32, (count, count), 1)
    return jnp.sum(jnp.where(down == across, row, 0.0), axis=1, keepdims=True)


def norm_silu(values, gain):
    meansq = jnp.mean(values * values, axis=-2, keepdims=True)
    half = values * lax.rsqrt(meansq + epsilon) * (0.5 * gain)
    return half + half * jnp.tanh(half)


def activate(block, out, gain):
    for frame in range(block.shape[1]):
        for row in range(block.shape[2]):
            values = block[0, frame, row].astype(jnp.float32)
            out[frame, row] = norm_silu(values, gain).astype(jnp.bfloat16)


def restack(weights, offsets, out, lead=()):
    chans = weights.shape[0]
    blank = jnp.zeros((chans, chans), weights.dtype)
    for k in range(3):
        pieces = []
        for offset in offsets:
            if offset is None:
                pieces.append(blank)
            else:
                start = ((offset[0] * 3 + offset[1]) * 3 + k) * chans
                pieces.append(weights[:, start : start + chans])
        out[(*lead, slice(k * chans, (k + 1) * chans), slice(None))] = jnp.concatenate(pieces, axis=1)


def conv(weights, windows):
    columns = [jnp.concatenate(window, axis=0) for window in windows]
    stacked = jnp.dot(weights, jnp.concatenate(columns, axis=1), preferred_element_type=jnp.float32)
    chans, width = windows[0][0].shape
    lane = lax.broadcasted_iota(jnp.int32, (chans, width), 1)
    sums = []
    for index in range(len(windows)):
        part = stacked[:, index * width : (index + 1) * width]
        left = jnp.where(lane == 0, 0.0, pltpu.roll(part[:chans], 1, 1))
        right = jnp.where(lane == width - 1, 0.0, pltpu.roll(part[2 * chans :], width - 1, 1))
        sums.append(part[chans : 2 * chans] + left + right)
    return sums


def four_rows(top):
    return [(top, 0), (top, 1), (1 - top, 0), (1 - top, 1)]


def side_of_one():
    return 1 - lax.rem(lax.axis_index("rows"), 2)


def edge_kernel(valid):
    row_part = lax.axis_index("rows")
    one_below = lax.rem(row_part, 2) == 0
    has_above = row_part > 0
    has_below = row_part < lax.axis_size("rows") - 1
    later = lax.axis_index("tm") > 0
    has_one = (one_below & has_below) | (~one_below & has_above)
    has_two = (one_below & has_above) | (~one_below & has_below)
    for index, flag in enumerate((has_one, has_two, later, later & has_one, later & has_two)):
        valid[index] = jnp.broadcast_to(jnp.where(flag, 1.0, 0.0), valid.shape[1:])


def weights_kernel(kernel_first, kernel_second, first, double, single, second, second_12, second_2):
    weights = kernel_first[...]
    restack(weights, [(i, j) if j < 3 else None for i in range(3) for j in range(4)], first)
    restack(weights, [(i, j) for i in range(3) for j in (0, 1)], double, (0,))
    restack(weights, [(i, j) for i in range(3) for j in (1, 2)], double, (1,))
    restack(weights, [(i, 0) for i in range(3)], single, (0,))
    restack(weights, [(i, 2) for i in range(3)], single, (1,))
    weights = kernel_second[...]
    restack(weights, [(i, j) for i in range(3) for j in range(3)], second)
    restack(weights, [(i, j) for i in (1, 2) for j in range(3)], second_12)
    restack(weights, [(2, j) for j in range(3)], second_2)


def own_kernel(video, gamma_first, bias_first, gamma_second, bias_second, own, columns):
    for index, vector in enumerate((gamma_first, bias_first, gamma_second, bias_second)):
        columns[index] = jnp.broadcast_to(column(vector), columns.shape[1:])
    activate(video, own, columns[0])


def present_frames(cells, side, exists, first, columns, partial, late):
    bias, gain = columns[1], columns[2]
    depth = first.shape[1] // 3
    frames = cells.shape[1]
    rows = four_rows(side)
    for frame in range(frames):
        count = min(frame + 1, 3)
        windows = []
        for row in range(2):
            chosen = rows[row : row + 3] + rows[row + 1 : row + 2]
            windows.append([cells[a, f, r] for f in range(frame + 1 - count, frame + 1) for a, r in chosen])
        sums = conv(first[:, (3 - count) * depth :], windows)
        for row in range(2):
            hidden = sums[row] + bias
            if frame < 2:
                partial[frame, row] = hidden
            else:
                mask = jnp.where(side == row, exists, 1.0)
                late[frame - 2, row] = (norm_silu(hidden, gain) * mask).astype(jnp.bfloat16)


def earlier_sums(double, single, pair, row):
    frames = pair.shape[0]
    both, alone = [None] * 4, [None] * 4
    for group in ((0, 1), (2,), (3,)):
        count = min(3, 4 - group[0])
        span = {frame: range(frames - 4 + frame, frames - 4 + frame + count) for frame in group}
        depth = 2 * count * pair.shape[2]
        sums = conv(double[:, :depth], [[pair[f, r] for f in span[frame] for r in range(2)] for frame in group])
        for frame, value in zip(group, sums):
            both[frame] = value
        sums = conv(single[:, : depth // 2], [[pair[f, row] for f in span[frame]] for frame in group])
        for frame, value in zip(group, sums):
            alone[frame] = value
    return both, alone


def earlier_rest(double, single, inner, side, partial, bias, rest):
    both, alone = earlier_sums(double.at[1 - side], single.at[1 - side], inner, side)
    for frame in range(4):
        for index, (value, row) in enumerate(((alone[frame], side), (both[frame], 1 - side))):
            rest[frame, index] = value + (bias if frame < 2 else partial[frame - 2, row])


def earlier_frames(double, single, near, side, rest, exists, later, gain, early, lead=()):
    both, alone = earlier_sums(double.at[side], single.at[side], near, 1 - side)
    for frame in range(4):
        for index, (value, row) in enumerate(((both[frame], side), (alone[frame], 1 - side))):
            value = norm_silu(value + rest[frame, index], gain)
            if index == 0:
                value = value * exists
            if frame < 2:
                value = value * later
            early[(*lead, frame, row)] = value.astype(jnp.bfloat16)


def one_kernel(valid, one, own, first, columns, partial, late, cells):
    activate(one, cells.at[0], columns[0] * valid[0, 0:1])
    cells[1] = own[...]
    present_frames(cells, side_of_one(), valid[0, 0:1], first, columns, partial, late)


def two_kernel(
    valid, two, prior, own, first, double, single, second_12, second_2, columns, partial_one, late_one,
    rest_one, rest_two, late_sums, cells, inner, partial, late,
):
    side = side_of_one()
    activate(two, cells.at[0], columns[0] * valid[1, 0:1])
    cells[1] = own[...]
    activate(prior, inner, columns[0] * valid[2, 0:1])
    late[0] = late_one[...]
    present_frames(cells, 1 - side, valid[1, 0:1], first, columns, partial, late.at[1])
    earlier_rest(double, single, inner, side, partial_one, columns[1], rest_one)
    earlier_rest(double, single, inner, 1 - side, partial, columns[1], rest_two)
    rows = four_rows(side)
    for frame, weights in ((0, second_2), (1, second_12)):
        windows = [[late[a, f, r] for f in range(frame + 1) for a, r in rows[row : row + 3]] for row in range(2)]
        for row, value in enumerate(conv(weights[...], windows)):
            late_sums[frame, row] = value + columns[3]


def prior_kernel(valid, prior_one, double, single, columns, rest, early, near):
    activate(prior_one, near, columns[0] * valid[3, 0:1])
    earlier_frames(
        double, single, near, side_of_one(), rest, valid[0, 0:1], valid[2, 0:1], columns[2], early
    )


def last_kernel(
    valid, video, prior_two, double, single, second, columns, rest, early_one, late_sums,
    encoded, near, early,
):
    side = side_of_one()
    activate(prior_two, near, columns[0] * valid[4, 0:1])
    early[0] = early_one[...]
    earlier_frames(
        double, single, near, 1 - side, rest, valid[1, 0:1], valid[2, 0:1], columns[2], early, (1,)
    )
    rows = four_rows(side)
    for frame in range(4):
        count = min(3, 4 - frame)
        windows = [
            [early[a, f, r] for f in range(frame, frame + count) for a, r in rows[row : row + 3]]
            for row in range(2)
        ]
        sums = conv(second[:, : 3 * count * near.shape[2]], windows)
        for row in range(2):
            rest_of_sum = columns[3] if frame < 2 else late_sums[frame - 2, row]
            value = video[0, frame, row].astype(jnp.float32) + (sums[row] + rest_of_sum)
            encoded[0, frame, row] = value.astype(jnp.bfloat16)


def routed(block, goal):
    row_parts, frame_parts = lax.axis_size("rows"), lax.axis_size("tm")
    route = []
    for row in range(row_parts):
        for part in range(frame_parts):
            row_to, part_to = goal(row, part, row_parts, frame_parts)
            route.append((row * frame_parts + part, row_to * frame_parts + part_to))
    return lax.ppermute(block, ("rows", "tm"), route)


def later(row, part, row_parts, frame_parts):
    return row, (part + 1) % frame_parts


def paired(row, part, partner, row_parts, frame_parts):
    if 0 <= partner < row_parts:
        return partner, part
    return row, min(part ^ 1, frame_parts - 1)


def even_pair(row, part, row_parts, frame_parts):
    return paired(row, part, row + 1 - 2 * (row % 2), row_parts, frame_parts)


def odd_pair(row, part, row_parts, frame_parts):
    return paired(row, part, row - 1 + 2 * (row % 2), row_parts, frame_parts)


def exchange(video):
    prior = routed(video, later)
    two = routed(video, odd_pair)
    one = routed(video, even_pair)
    prior_two = routed(prior, odd_pair)
    prior_one = routed(prior, even_pair)
    return one, two, prior, prior_one, prior_two


def local(video, gamma_first, kernel_first, bias_first, gamma_second, kernel_second, bias_second):
    _, frames, rows, chans, width = video.shape
    assert frames == 4 and rows == 2
    one, two, prior, prior_one, prior_two = exchange(video)
    bf16, f32 = jnp.bfloat16, jnp.float32
    shape = jax.ShapeDtypeStruct
    params = pltpu.CompilerParams(vmem_limit_bytes=24 * 2**20)

    def run(kernel, out_shape, operands, scratch=(), millions=1000):
        single_out = not isinstance(out_shape, tuple)
        return pl.pallas_call(
            kernel,
            out_shape=out_shape,
            in_specs=[VMEM] * len(operands),
            out_specs=VMEM if single_out else [VMEM] * len(out_shape),
            scratch_shapes=[pltpu.VMEM(*one_scratch) for one_scratch in scratch],
            compiler_params=params,
            cost_estimate=pl.CostEstimate(flops=millions * 10**6, bytes_accessed=10**6, transcendentals=10**5),
        )(*operands)

    def stacked(*lead_and_taps):
        *lead, taps = lead_and_taps
        return shape((*lead, 3 * chans, taps * chans), bf16)

    block = (frames, rows, chans, width)
    cells = ((2, *block), bf16)
    pair = shape((2, 2, chans, width), f32)
    late = shape((2, 2, chans, width), bf16)
    rest = shape((4, 2, chans, width), f32)
    early = shape((4, 2, chans, width), bf16)
    valid = run(edge_kernel, shape((5, 8, width), f32), (), millions=2000)
    first, double, single, second, second_12, second_2 = run(
        weights_kernel,
        (stacked(12), stacked(2, 6), stacked(2, 3), stacked(9), stacked(6), stacked(3)),
        (kernel_first, kernel_second),
        millions=2000,
    )
    own, columns = run(
        own_kernel,
        (shape(block, bf16), shape((4, chans, width), f32)),
        (video, gamma_first, bias_first, gamma_second, bias_second),
        millions=1000,
    )
    partial_one, late_one = run(one_kernel, (pair, late), (valid, one, own, first, columns), (cells,), 10)
    rest_one, rest_two, late_sums = run(
        two_kernel,
        (rest, rest, pair),
        (valid, two, prior, own, first, double, single, second_12, second_2, columns, partial_one, late_one),
        (cells, (block, bf16), (pair.shape, f32), ((2, *late.shape), bf16)),
        10,
    )
    early_one = run(prior_kernel, early, (valid, prior_one, double, single, columns, rest_one), ((block, bf16),), 1000)
    return run(
        last_kernel,
        shape(video.shape, bf16),
        (valid, video, prior_two, double, single, second, columns, rest_two, early_one, late_sums),
        ((block, bf16), ((2, *early.shape), bf16)),
        1000,
    )


def solution(mesh):
    in_specs = (P("groups", "tm", "rows", None, None), P(), P(), P(), P(), P(), P())
    out_specs = P("groups", "tm", "rows", None, None)
    return jax.shard_map(local, mesh=mesh, in_specs=in_specs, out_specs=out_specs, check_vma=False)
```

time: 39.9 us -> 16.6 us (0.42)
  the two profiles are of different devices: /device:TPU:1 before, /device:TPU:0 now
where the time goes in v4:
time: 16.6 us; the launch traced here: 16.4 us
  Pallas kernels  6.91 us (42%)
  starting transfers between devices  6.74 us (41%)
  waiting for transfers between devices  2.59 us (16%)
    pallas_call x7, Pallas kernels, run(): pl.pallas_call(kernel, out_shape=out_shape, in_specs=[VMEM] * len(operand...  6.91 us
    ppermute x5, starting transfers between devices, routed(): return lax.ppermute(block, ('rows', 'tm'), route)  6.74 us
    ppermute x5, waiting for transfers between devices, routed(): return lax.ppermute(block, ('rows', 'tm'), route)  2.59 us
  transfers between devices with their start and end apart: 5, of which 2 were waited for; matrix products, arithmetic and copies ran while one was open for 0% of the time, Pallas kernels for 28%

profile of v4, /device:TPU:0, one launch (start us, length us, event | category | flops | bytes accessed | tf_op | source)
XLA Modules:
  0.0 16.4 jit_solution(10464044125657267869)
XLA Ops:
  0.0 0.0 copy-start.1
  0.0 0.0 copy-start
  0.0 0.5 %collective-permute-start = (bf16[1,4,2,96,128]{4,3,2,1,0:T(8,128)(2,1)}, bf16[1,4,2,96,128]{4,3,2,1,0:T(8,128)(2,1)S(1)}, u32[]{:S(2)}, u32[]{:S(2)}) collective-permute-start(bf16[1,4,2,96,128]{4,3,2,1,0:T(8,128)(2,1)} %video.3), channel_id=1, source_target_pairs={{0,1},{1,2},{2,3},{3,0},{4,5},{5,6},{6,7},{7,4},{8,9},{9,10},{10,1... | collective-permute-start | bytes 589832 | tf_op jit(solution)/shard_map/ppermute | solution.py:219
  0.5 2.6 %collective-permute-start.3 = (bf16[1,4,2,96,128]{4,3,2,1,0:T(8,128)(2,1)}, bf16[1,4,2,96,128]{4,3,2,1,0:T(8,128)(2,1)S(1)}, u32[]{:S(2)}, u32[]{:S(2)}) collective-permute-start(bf16[1,4,2,96,128]{4,3,2,1,0:T(8,128)(2,1)} %video.3), channel_id=1, source_target_pairs={{0,4},{1,5},{2,6},{3,7},{4,0},{5,1},{6,2},{7,3},{8,12},{9,13},{10,... | collective-permute-start | bytes 589832 | tf_op jit(solution)/shard_map/ppermute | solution.py:219
  3.1 1.3 %collective-permute-start.2 = (bf16[1,4,2,96,128]{4,3,2,1,0:T(8,128)(2,1)}, bf16[1,4,2,96,128]{4,3,2,1,0:T(8,128)(2,1)S(1)}, u32[]{:S(2)}, u32[]{:S(2)}) collective-permute-start(bf16[1,4,2,96,128]{4,3,2,1,0:T(8,128)(2,1)} %video.3), channel_id=1, source_target_pairs={{0,1},{1,0},{2,3},{3,2},{4,8},{5,9},{6,10},{7,11},{8,4},{9,5},{10,... | collective-permute-start | bytes 589832 | tf_op jit(solution)/shard_map/ppermute | solution.py:219
  4.4 0.0 copy-start.2
  4.4 0.0 copy-start.3
  4.4 0.0 copy-start.4
  4.4 0.0 copy-start.5
  4.4 0.0 copy-start.6
  4.4 1.5 %collective-permute-done.prior = bf16[1,4,2,96,128]{4,3,2,1,0:T(8,128)(2,1)S(1)} collective-permute-done((bf16[1,4,2,96,128]{4,3,2,1,0:T(8,128)(2,1)}, bf16[1,4,2,96,128]{4,3,2,1,0:T(8,128)(2,1)S(1)}, u32[]{:S(2)}, u32[]{:S(2)}) %collective-permute-start) | collective-permute-done | bytes 196640 | tf_op jit(solution)/shard_map/ppermute | solution.py:219
  5.9 2.4 %collective-permute-start.4 = (bf16[1,4,2,96,128]{4,3,2,1,0:T(8,128)(2,1)S(1)}, bf16[1,4,2,96,128]{4,3,2,1,0:T(8,128)(2,1)S(1)}, u32[]{:S(2)}, u32[]{:S(2)}) collective-permute-start(bf16[1,4,2,96,128]{4,3,2,1,0:T(8,128)(2,1)S(1)} %collective-permute-done.prior), channel_id=1, source_target_pairs={{0,4},{1,5},{2,6},{3,7},{4,0},{5,1},{6,2},{7,3},{8,12},{9,13},{10,... | collective-permute-start | bytes 589832 | tf_op jit(solution)/shard_map/ppermute | solution.py:219
  8.3 0.0 collective-permute-start.1
  8.3 0.0 copy-done.1
  8.3 0.0 copy-done
  8.3 0.7 %shard_map.74 = (bf16[288,1152]{1,0:T(8,128)(2,1)S(1)}, bf16[2,288,576]{2,1,0:T(8,128)(2,1)S(1)}, bf16[2,288,288]{2,1,0:T(8,128)(2,1)S(1)}, bf16[288,864]{1,0:T(...) custom-call(bf16[96,2592]{1,0:T(8,128)(2,1)S(1)} %copy-done, bf16[96,2592]{1,0:T(8,128)(2,1)S(1)} %copy-done.1), custom_call_target="tpu_custom_call" | custom-call | flops 2000000000 | bytes 1000000 | tf_op jit(solution)/shard_map/pallas_call | solution.py:259
  9.0 0.0 copy-done.2
  9.0 0.0 copy-done.3
  9.0 0.0 copy-done.4
  9.0 0.0 copy-done.5
  9.1 0.0 copy-done.6
  9.1 0.2 shard_map.75
  9.2 0.0 collective-permute-done.3.one
  9.2 1.0 %shard_map.76 = (f32[2,2,96,128]{3,2,1,0:T(8,128)S(1)}, bf16[2,2,96,128]{3,2,1,0:T(8,128)(2,1)S(1)}) custom-call(f32[5,8,128]{2,1,0:T(8,128)S(1)} %shard_map.73.valid, bf16[1,4,2,96,128]{4,3,2,1,0:T(8,128)(2,1)S(1)} %collective-permute-done.3.one, bf16[4,2,96,128]{3,2,1,0:T(8,128)(2,1)S(1)} %get-tuple-element.22.own, ...), custom_call_target="tpu_custom_call" | custom-call | flops 10000000 | bytes 1000000 | tf_op jit(solution)/shard_map/pallas_call | solution.py:259
  10.3 0.0 collective-permute-done.2.two
  10.3 2.0 %shard_map.77 = (f32[4,2,96,128]{3,2,1,0:T(8,128)S(1)}, f32[4,2,96,128]{3,2,1,0:T(8,128)S(1)}, f32[2,2,96,128]{3,2,1,0:T(8,128)S(1)}) custom-call(f32[5,8,128]{2,1,0:T(8,128)S(1)} %shard_map.73.valid, bf16[1,4,2,96,128]{4,3,2,1,0:T(8,128)(2,1)S(1)} %collective-permute-done.2.two, bf16[1,4,2,96,128]{4,3,2,1,0:T(8,128)(2,1)S(1)} %collective-permute-done.prior, ...), custom_call_target="tpu_custom_call" | custom-call | flops 10000000 | bytes 1000000 | tf_op jit(solution)/shard_map/pallas_call | solution.py:259
  12.2 1.0 %collective-permute-done.4.prior_one = bf16[1,4,2,96,128]{4,3,2,1,0:T(8,128)(2,1)S(1)} collective-permute-done((bf16[1,4,2,96,128]{4,3,2,1,0:T(8,128)(2,1)S(1)}, bf16[1,4,2,96,128]{4,3,2,1,0:T(8,128)(2,1)S(1)}, u32[]{:S(2)}, u32[]{:S(2)}) %collective-permute-start.4) | collective-permute-done | bytes 196640 | tf_op jit(solution)/shard_map/ppermute | solution.py:219
  13.3 0.8 %shard_map.78.early_one = bf16[4,2,96,128]{3,2,1,0:T(8,128)(2,1)S(1)} custom-call(f32[5,8,128]{2,1,0:T(8,128)S(1)} %shard_map.73.valid, bf16[1,4,2,96,128]{4,3,2,1,0:T(8,128)(2,1)S(1)} %collective-permute-done.4.prior_one, bf16[2,288,576]{2,1,0:T(8,128)(2,1)S(1)} %get-tuple-element.18.double, bf16[2,288,288]{2,1,0:T(8,128)(2,1)S(1)} %get-tuple-element.19.single, ...), custom_call_target="tpu_custom_call" | custom-call | flops 1000000000 | bytes 1000000 | tf_op jit(solution)/shard_map/pallas_call | solution.py:259
  14.1 0.0 collective-permute-done.1.prior_two
  14.1 2.3 %shard_map.79 = bf16[1,4,2,96,128]{4,3,2,1,0:T(8,128)(2,1)} custom-call(f32[5,8,128]{2,1,0:T(8,128)S(1)} %shard_map.73.valid, bf16[1,4,2,96,128]{4,3,2,1,0:T(8,128)(2,1)S(1)} %copy-done.2, bf16[1,4,2,96,128]{4,3,2,1,0:T(8,128)(2,1)S(1)} %collective-permute-done.1.prior_two, bf16[2,288,576]{2,1,0:T(8,128)(2,1)S(1)} %get-tuple-element.18.double, ...), custom_call_target="tpu_custom_call" | custom-call | flops 1000000000 | bytes 1000000 | tf_op jit(solution)/shard_map/pallas_call | solution.py:259
  (1 shorter events, 0.0 us)
Async XLA Ops:
  0.0 8.3 %copy-start.1 = (bf16[96,2592]{1,0:T(8,128)(2,1)S(1)}, bf16[96,2592]{1,0:T(8,128)(2,1)}, u32[]{:S(2)}) copy-start(bf16[96,2592]{1,0:T(8,128)(2,1)} %kernel_second.1) | copy-start | bytes 1492996
  0.0 8.3 %copy-start = (bf16[96,2592]{1,0:T(8,128)(2,1)S(1)}, bf16[96,2592]{1,0:T(8,128)(2,1)}, u32[]{:S(2)}) copy-start(bf16[96,2592]{1,0:T(8,128)(2,1)} %kernel_first.1) | copy-start | bytes 1492996
  0.0 5.9 %collective-permute-start = (bf16[1,4,2,96,128]{4,3,2,1,0:T(8,128)(2,1)}, bf16[1,4,2,96,128]{4,3,2,1,0:T(8,128)(2,1)S(1)}, u32[]{:S(2)}, u32[]{:S(2)}) collective-permute-start(bf16[1,4,2,96,128]{4,3,2,1,0:T(8,128)(2,1)} %video.3), channel_id=1, source_target_pairs={{0,1},{1,2},{2,3},{3,0},{4,5},{5,6},{6,7},{7,4},{8,9},{9,10},{10,1... | collective-permute-start | bytes 589832 | tf_op jit(solution)/shard_map/ppermute | solution.py:219
  0.5 8.8 %collective-permute-start.3 = (bf16[1,4,2,96,128]{4,3,2,1,0:T(8,128)(2,1)}, bf16[1,4,2,96,128]{4,3,2,1,0:T(8,128)(2,1)S(1)}, u32[]{:S(2)}, u32[]{:S(2)}) collective-permute-start(bf16[1,4,2,96,128]{4,3,2,1,0:T(8,128)(2,1)} %video.3), channel_id=1, source_target_pairs={{0,4},{1,5},{2,6},{3,7},{4,0},{5,1},{6,2},{7,3},{8,12},{9,13},{10,... | collective-permute-start | bytes 589832 | tf_op jit(solution)/shard_map/ppermute | solution.py:219
  3.1 7.2 %collective-permute-start.2 = (bf16[1,4,2,96,128]{4,3,2,1,0:T(8,128)(2,1)}, bf16[1,4,2,96,128]{4,3,2,1,0:T(8,128)(2,1)S(1)}, u32[]{:S(2)}, u32[]{:S(2)}) collective-permute-start(bf16[1,4,2,96,128]{4,3,2,1,0:T(8,128)(2,1)} %video.3), channel_id=1, source_target_pairs={{0,1},{1,0},{2,3},{3,2},{4,8},{5,9},{6,10},{7,11},{8,4},{9,5},{10,... | collective-permute-start | bytes 589832 | tf_op jit(solution)/shard_map/ppermute | solution.py:219
  4.4 4.7 %copy-start.2 = (bf16[1,4,2,96,128]{4,3,2,1,0:T(8,128)(2,1)S(1)}, bf16[1,4,2,96,128]{4,3,2,1,0:T(8,128)(2,1)}, u32[]{:S(2)}) copy-start(bf16[1,4,2,96,128]{4,3,2,1,0:T(8,128)(2,1)} %video.3) | copy-start | bytes 589828
  4.4 4.7 %copy-start.3 = (f32[96]{0:T(128)S(1)}, f32[96]{0:T(128)}, u32[]{:S(2)}) copy-start(f32[96]{0:T(128)} %gamma_first.1) | copy-start | bytes 1156
  4.4 4.7 %copy-start.4 = (f32[96]{0:T(128)S(1)}, f32[96]{0:T(128)}, u32[]{:S(2)}) copy-start(f32[96]{0:T(128)} %bias_first.1) | copy-start | bytes 1156
  4.4 4.7 %copy-start.5 = (f32[96]{0:T(128)S(1)}, f32[96]{0:T(128)}, u32[]{:S(2)}) copy-start(f32[96]{0:T(128)} %gamma_second.1) | copy-start | bytes 1156
  4.4 4.7 %copy-start.6 = (f32[96]{0:T(128)S(1)}, f32[96]{0:T(128)}, u32[]{:S(2)}) copy-start(f32[96]{0:T(128)} %bias_second.1) | copy-start | bytes 1156
  5.9 7.3 %collective-permute-start.4 = (bf16[1,4,2,96,128]{4,3,2,1,0:T(8,128)(2,1)S(1)}, bf16[1,4,2,96,128]{4,3,2,1,0:T(8,128)(2,1)S(1)}, u32[]{:S(2)}, u32[]{:S(2)}) collective-permute-start(bf16[1,4,2,96,128]{4,3,2,1,0:T(8,128)(2,1)S(1)} %collective-permute-done.prior), channel_id=1, source_target_pairs={{0,4},{1,5},{2,6},{3,7},{4,0},{5,1},{6,2},{7,3},{8,12},{9,13},{10,... | collective-permute-start | bytes 589832 | tf_op jit(solution)/shard_map/ppermute | solution.py:219
  8.3 5.8 %collective-permute-start.1 = (bf16[1,4,2,96,128]{4,3,2,1,0:T(8,128)(2,1)S(1)}, bf16[1,4,2,96,128]{4,3,2,1,0:T(8,128)(2,1)S(1)}, u32[]{:S(2)}, u32[]{:S(2)}) collective-permute-start(bf16[1,4,2,96,128]{4,3,2,1,0:T(8,128)(2,1)S(1)} %collective-permute-done.prior), channel_id=1, source_target_pairs={{0,1},{1,0},{2,3},{3,2},{4,8},{5,9},{6,10},{7,11},{8,4},{9,5},{10,... | collective-permute-start | bytes 589832 | tf_op jit(solution)/shard_map/ppermute | solution.py:219

commit v5 on v4

--- a/solution.py
+++ b/solution.py
@@ -1,3 +1,5 @@
+import itertools
+
 import jax
 import jax.numpy as jnp
 from jax import lax
@@ -210,39 +212,48 @@
 
 
 def routed(block, goal):
-    row_parts, frame_parts = lax.axis_size("rows"), lax.axis_size("tm")
-    route = []
-    for row in range(row_parts):
-        for part in range(frame_parts):
-            row_to, part_to = goal(row, part, row_parts, frame_parts)
-            route.append((row * frame_parts + part, row_to * frame_parts + part_to))
-    return lax.ppermute(block, ("rows", "tm"), route)
-
-
-def later(row, part, row_parts, frame_parts):
-    return row, (part + 1) % frame_parts
-
-
-def paired(row, part, partner, row_parts, frame_parts):
-    if 0 <= partner < row_parts:
-        return partner, part
-    return row, min(part ^ 1, frame_parts - 1)
-
-
-def even_pair(row, part, row_parts, frame_parts):
-    return paired(row, part, row + 1 - 2 * (row % 2), row_parts, frame_parts)
-
-
-def odd_pair(row, part, row_parts, frame_parts):
-    return paired(row, part, row - 1 + 2 * (row % 2), row_parts, frame_parts)
+    sizes = [lax.axis_size(axis) for axis in ("groups", "rows", "tm")]
+    places = list(itertools.product(*map(range, sizes)))
+    route = [(index, places.index(goal(place, sizes))) for index, place in enumerate(places)]
+    return lax.ppermute(block, ("groups", "rows", "tm"), route)
+
+
+def later(place, sizes):
+    group, row, part = place
+    return group, row, (part + 1) % sizes[2]
+
+
+def paired(place, sizes, partner):
+    group, row, part = place
+    if 0 <= partner < sizes[1]:
+        return group, partner, part
+    return group, row, min(part ^ 1, sizes[2] - 1)
+
+
+def even_pair(place, sizes):
+    return paired(place, sizes, place[1] + 1 - 2 * (place[1] % 2))
+
+
+def odd_pair(place, sizes):
+    return paired(place, sizes, place[1] - 1 + 2 * (place[1] % 2))
+
+
+def if_earlier(pair):
+    def goal(place, sizes):
+        group, row, part = place
+        if part == 0 and pair(place, sizes)[1] != row and group ^ 1 < sizes[0]:
+            return group ^ 1, row, part
+        return pair(place, sizes)
+
+    return goal
 
 
 def exchange(video):
     prior = routed(video, later)
     two = routed(video, odd_pair)
     one = routed(video, even_pair)
-    prior_two = routed(prior, odd_pair)
-    prior_one = routed(prior, even_pair)
+    prior_two = routed(prior, if_earlier(odd_pair))
+    prior_one = routed(prior, if_earlier(even_pair))
     return one, two, prior, prior_one, prior_two
 
 

time: 16.6 us -> 15.6 us (0.940)
  the two profiles are of different devices: /device:TPU:0 before, /device:TPU:18 now
where the time goes in v5:
time: 15.6 us; the launch traced here: 15.5 us
  Pallas kernels  6.91 us (44%)
  waiting for transfers between devices  5.17 us (33%)
  starting transfers between devices  3.23 us (21%)
    pallas_call x7, Pallas kernels, run(): pl.pallas_call(kernel, out_shape=out_shape, in_specs=[VMEM] * len(operand...  6.91 us
    ppermute x5, waiting for transfers between devices, routed(): return lax.ppermute(block, ('groups', 'rows', 'tm'), route)  5.17 us
    ppermute x5, starting transfers between devices, routed(): return lax.ppermute(block, ('groups', 'rows', 'tm'), route)  3.23 us
  transfers between devices with their start and end apart: 5, of which 5 were waited for; matrix products, arithmetic and copies ran while one was open for 0% of the time, Pallas kernels for 30%

profile of v5, /device:TPU:18, one launch (start us, length us, event | category | flops | bytes accessed | tf_op | source)
XLA Modules:
  0.0 15.5 jit_solution(8575042827414734690)
XLA Ops:
  0.0 0.0 copy-start.1
  0.0 0.0 copy-start
  0.0 0.0 collective-permute-start
  0.0 1.6 %collective-permute-start.3 = (bf16[1,4,2,96,128]{4,3,2,1,0:T(8,128)(2,1)}, bf16[1,4,2,96,128]{4,3,2,1,0:T(8,128)(2,1)S(1)}, u32[]{:S(2)}, u32[]{:S(2)}) collective-permute-start(bf16[1,4,2,96,128]{4,3,2,1,0:T(8,128)(2,1)} %video.3), channel_id=1, source_target_pairs={{0,4},{1,5},{2,6},{3,7},{4,0},{5,1},{6,2},{7,3},{8,12},{9,13},{10,... | collective-permute-start | bytes 589832 | tf_op jit(solution)/shard_map/ppermute | solution.py:218
  1.7 0.0 collective-permute-start.2
  1.7 0.0 copy-start.2
  1.7 0.0 copy-start.3
  1.7 0.0 copy-start.4
  1.7 0.0 copy-start.5
  1.7 0.0 copy-start.6
  1.7 3.6 %collective-permute-done.prior = bf16[1,4,2,96,128]{4,3,2,1,0:T(8,128)(2,1)S(1)} collective-permute-done((bf16[1,4,2,96,128]{4,3,2,1,0:T(8,128)(2,1)}, bf16[1,4,2,96,128]{4,3,2,1,0:T(8,128)(2,1)S(1)}, u32[]{:S(2)}, u32[]{:S(2)}) %collective-permute-start) | collective-permute-done | bytes 196640 | tf_op jit(solution)/shard_map/ppermute | solution.py:218
  5.3 1.6 %collective-permute-start.4 = (bf16[1,4,2,96,128]{4,3,2,1,0:T(8,128)(2,1)S(1)}, bf16[1,4,2,96,128]{4,3,2,1,0:T(8,128)(2,1)S(1)}, u32[]{:S(2)}, u32[]{:S(2)}) collective-permute-start(bf16[1,4,2,96,128]{4,3,2,1,0:T(8,128)(2,1)S(1)} %collective-permute-done.prior), channel_id=1, source_target_pairs={{0,16},{1,5},{2,6},{3,7},{4,20},{5,1},{6,2},{7,3},{8,24},{9,13},{1... | collective-permute-start | bytes 589832 | tf_op jit(solution)/shard_map/ppermute | solution.py:218
  6.9 0.0 collective-permute-start.1
  6.9 0.0 copy-done.1
  6.9 0.0 copy-done
  6.9 0.7 %shard_map.74 = (bf16[288,1152]{1,0:T(8,128)(2,1)S(1)}, bf16[2,288,576]{2,1,0:T(8,128)(2,1)S(1)}, bf16[2,288,288]{2,1,0:T(8,128)(2,1)S(1)}, bf16[288,864]{1,0:T(...) custom-call(bf16[96,2592]{1,0:T(8,128)(2,1)S(1)} %copy-done, bf16[96,2592]{1,0:T(8,128)(2,1)S(1)} %copy-done.1), custom_call_target="tpu_custom_call" | custom-call | flops 2000000000 | bytes 1000000 | tf_op jit(solution)/shard_map/pallas_call | solution.py:270
  7.6 0.0 copy-done.2
  7.6 0.0 copy-done.3
  7.6 0.0 copy-done.4
  7.6 0.0 copy-done.5
  7.6 0.0 copy-done.6
  7.6 0.2 shard_map.75
  7.8 0.2 %collective-permute-done.3.one = bf16[1,4,2,96,128]{4,3,2,1,0:T(8,128)(2,1)S(1)} collective-permute-done((bf16[1,4,2,96,128]{4,3,2,1,0:T(8,128)(2,1)}, bf16[1,4,2,96,128]{4,3,2,1,0:T(8,128)(2,1)S(1)}, u32[]{:S(2)}, u32[]{:S(2)}) %collective-permute-start.3) | collective-permute-done | bytes 196640 | tf_op jit(solution)/shard_map/ppermute | solution.py:218
  8.0 1.0 %shard_map.76 = (f32[2,2,96,128]{3,2,1,0:T(8,128)S(1)}, bf16[2,2,96,128]{3,2,1,0:T(8,128)(2,1)S(1)}) custom-call(f32[5,8,128]{2,1,0:T(8,128)S(1)} %shard_map.73.valid, bf16[1,4,2,96,128]{4,3,2,1,0:T(8,128)(2,1)S(1)} %collective-permute-done.3.one, bf16[4,2,96,128]{3,2,1,0:T(8,128)(2,1)S(1)} %get-tuple-element.22.own, ...), custom_call_target="tpu_custom_call" | custom-call | flops 10000000 | bytes 1000000 | tf_op jit(solution)/shard_map/pallas_call | solution.py:270
  9.0 0.6 %collective-permute-done.2.two = bf16[1,4,2,96,128]{4,3,2,1,0:T(8,128)(2,1)S(1)} collective-permute-done((bf16[1,4,2,96,128]{4,3,2,1,0:T(8,128)(2,1)}, bf16[1,4,2,96,128]{4,3,2,1,0:T(8,128)(2,1)S(1)}, u32[]{:S(2)}, u32[]{:S(2)}) %collective-permute-start.2) | collective-permute-done | bytes 196640 | tf_op jit(solution)/shard_map/ppermute | solution.py:218
  9.6 2.0 %shard_map.77 = (f32[4,2,96,128]{3,2,1,0:T(8,128)S(1)}, f32[4,2,96,128]{3,2,1,0:T(8,128)S(1)}, f32[2,2,96,128]{3,2,1,0:T(8,128)S(1)}) custom-call(f32[5,8,128]{2,1,0:T(8,128)S(1)} %shard_map.73.valid, bf16[1,4,2,96,128]{4,3,2,1,0:T(8,128)(2,1)S(1)} %collective-permute-done.2.two, bf16[1,4,2,96,128]{4,3,2,1,0:T(8,128)(2,1)S(1)} %collective-permute-done.prior, ...), custom_call_target="tpu_custom_call" | custom-call | flops 10000000 | bytes 1000000 | tf_op jit(solution)/shard_map/pallas_call | solution.py:270
  11.6 0.3 %collective-permute-done.4.prior_one = bf16[1,4,2,96,128]{4,3,2,1,0:T(8,128)(2,1)S(1)} collective-permute-done((bf16[1,4,2,96,128]{4,3,2,1,0:T(8,128)(2,1)S(1)}, bf16[1,4,2,96,128]{4,3,2,1,0:T(8,128)(2,1)S(1)}, u32[]{:S(2)}, u32[]{:S(2)}) %collective-permute-start.4) | collective-permute-done | bytes 196640 | tf_op jit(solution)/shard_map/ppermute | solution.py:218
  11.9 0.8 %shard_map.78.early_one = bf16[4,2,96,128]{3,2,1,0:T(8,128)(2,1)S(1)} custom-call(f32[5,8,128]{2,1,0:T(8,128)S(1)} %shard_map.73.valid, bf16[1,4,2,96,128]{4,3,2,1,0:T(8,128)(2,1)S(1)} %collective-permute-done.4.prior_one, bf16[2,288,576]{2,1,0:T(8,128)(2,1)S(1)} %get-tuple-element.18.double, bf16[2,288,288]{2,1,0:T(8,128)(2,1)S(1)} %get-tuple-element.19.single, ...), custom_call_target="tpu_custom_call" | custom-call | flops 1000000000 | bytes 1000000 | tf_op jit(solution)/shard_map/pallas_call | solution.py:270
  12.7 0.5 %collective-permute-done.1.prior_two = bf16[1,4,2,96,128]{4,3,2,1,0:T(8,128)(2,1)S(1)} collective-permute-done((bf16[1,4,2,96,128]{4,3,2,1,0:T(8,128)(2,1)S(1)}, bf16[1,4,2,96,128]{4,3,2,1,0:T(8,128)(2,1)S(1)}, u32[]{:S(2)}, u32[]{:S(2)}) %collective-permute-start.1) | collective-permute-done | bytes 196640 | tf_op jit(solution)/shard_map/ppermute | solution.py:218
  13.2 2.3 %shard_map.79 = bf16[1,4,2,96,128]{4,3,2,1,0:T(8,128)(2,1)} custom-call(f32[5,8,128]{2,1,0:T(8,128)S(1)} %shard_map.73.valid, bf16[1,4,2,96,128]{4,3,2,1,0:T(8,128)(2,1)S(1)} %copy-done.2, bf16[1,4,2,96,128]{4,3,2,1,0:T(8,128)(2,1)S(1)} %collective-permute-done.1.prior_two, bf16[2,288,576]{2,1,0:T(8,128)(2,1)S(1)} %get-tuple-element.18.double, ...), custom_call_target="tpu_custom_call" | custom-call | flops 1000000000 | bytes 1000000 | tf_op jit(solution)/shard_map/pallas_call | solution.py:270
  (1 shorter events, 0.0 us)
Async XLA Ops:
  0.0 6.9 %copy-start.1 = (bf16[96,2592]{1,0:T(8,128)(2,1)S(1)}, bf16[96,2592]{1,0:T(8,128)(2,1)}, u32[]{:S(2)}) copy-start(bf16[96,2592]{1,0:T(8,128)(2,1)} %kernel_second.1) | copy-start | bytes 1492996
  0.0 6.9 %copy-start = (bf16[96,2592]{1,0:T(8,128)(2,1)S(1)}, bf16[96,2592]{1,0:T(8,128)(2,1)}, u32[]{:S(2)}) copy-start(bf16[96,2592]{1,0:T(8,128)(2,1)} %kernel_first.1) | copy-start | bytes 1492996
  0.0 5.3 %collective-permute-start = (bf16[1,4,2,96,128]{4,3,2,1,0:T(8,128)(2,1)}, bf16[1,4,2,96,128]{4,3,2,1,0:T(8,128)(2,1)S(1)}, u32[]{:S(2)}, u32[]{:S(2)}) collective-permute-start(bf16[1,4,2,96,128]{4,3,2,1,0:T(8,128)(2,1)} %video.3), channel_id=1, source_target_pairs={{0,1},{1,2},{2,3},{3,0},{4,5},{5,6},{6,7},{7,4},{8,9},{9,10},{10,1... | collective-permute-start | bytes 589832 | tf_op jit(solution)/shard_map/ppermute | solution.py:218
  0.0 8.0 %collective-permute-start.3 = (bf16[1,4,2,96,128]{4,3,2,1,0:T(8,128)(2,1)}, bf16[1,4,2,96,128]{4,3,2,1,0:T(8,128)(2,1)S(1)}, u32[]{:S(2)}, u32[]{:S(2)}) collective-permute-start(bf16[1,4,2,96,128]{4,3,2,1,0:T(8,128)(2,1)} %video.3), channel_id=1, source_target_pairs={{0,4},{1,5},{2,6},{3,7},{4,0},{5,1},{6,2},{7,3},{8,12},{9,13},{10,... | collective-permute-start | bytes 589832 | tf_op jit(solution)/shard_map/ppermute | solution.py:218
  1.7 7.9 %collective-permute-start.2 = (bf16[1,4,2,96,128]{4,3,2,1,0:T(8,128)(2,1)}, bf16[1,4,2,96,128]{4,3,2,1,0:T(8,128)(2,1)S(1)}, u32[]{:S(2)}, u32[]{:S(2)}) collective-permute-start(bf16[1,4,2,96,128]{4,3,2,1,0:T(8,128)(2,1)} %video.3), channel_id=1, source_target_pairs={{0,1},{1,0},{2,3},{3,2},{4,8},{5,9},{6,10},{7,11},{8,4},{9,5},{10,... | collective-permute-start | bytes 589832 | tf_op jit(solution)/shard_map/ppermute | solution.py:218
  1.7 5.9 %copy-start.2 = (bf16[1,4,2,96,128]{4,3,2,1,0:T(8,128)(2,1)S(1)}, bf16[1,4,2,96,128]{4,3,2,1,0:T(8,128)(2,1)}, u32[]{:S(2)}) copy-start(bf16[1,4,2,96,128]{4,3,2,1,0:T(8,128)(2,1)} %video.3) | copy-start | bytes 589828
  1.7 5.9 %copy-start.3 = (f32[96]{0:T(128)S(1)}, f32[96]{0:T(128)}, u32[]{:S(2)}) copy-start(f32[96]{0:T(128)} %gamma_first.1) | copy-start | bytes 1156
  1.7 5.9 %copy-start.4 = (f32[96]{0:T(128)S(1)}, f32[96]{0:T(128)}, u32[]{:S(2)}) copy-start(f32[96]{0:T(128)} %bias_first.1) | copy-start | bytes 1156
  1.7 5.9 %copy-start.5 = (f32[96]{0:T(128)S(1)}, f32[96]{0:T(128)}, u32[]{:S(2)}) copy-start(f32[96]{0:T(128)} %gamma_second.1) | copy-start | bytes 1156
  1.7 5.9 %copy-start.6 = (f32[96]{0:T(128)S(1)}, f32[96]{0:T(128)}, u32[]{:S(2)}) copy-start(f32[96]{0:T(128)} %bias_second.1) | copy-start | bytes 1156
  5.3 6.6 %collective-permute-start.4 = (bf16[1,4,2,96,128]{4,3,2,1,0:T(8,128)(2,1)S(1)}, bf16[1,4,2,96,128]{4,3,2,1,0:T(8,128)(2,1)S(1)}, u32[]{:S(2)}, u32[]{:S(2)}) collective-permute-start(bf16[1,4,2,96,128]{4,3,2,1,0:T(8,128)(2,1)S(1)} %collective-permute-done.prior), channel_id=1, source_target_pairs={{0,16},{1,5},{2,6},{3,7},{4,20},{5,1},{6,2},{7,3},{8,24},{9,13},{1... | collective-permute-start | bytes 589832 | tf_op jit(solution)/shard_map/ppermute | solution.py:218
  6.9 6.3 %collective-permute-start.1 = (bf16[1,4,2,96,128]{4,3,2,1,0:T(8,128)(2,1)S(1)}, bf16[1,4,2,96,128]{4,3,2,1,0:T(8,128)(2,1)S(1)}, u32[]{:S(2)}, u32[]{:S(2)}) collective-permute-start(bf16[1,4,2,96,128]{4,3,2,1,0:T(8,128)(2,1)S(1)} %collective-permute-done.prior), channel_id=1, source_target_pairs={{0,1},{1,0},{2,3},{3,2},{4,20},{5,9},{6,10},{7,11},{8,24},{9,5},{1... | collective-permute-start | bytes 589832 | tf_op jit(solution)/shard_map/ppermute | solution.py:218

commit v6 on v5

--- a/solution.py
+++ b/solution.py
@@ -76,7 +76,7 @@
     later = lax.axis_index("tm") > 0
     has_one = (one_below & has_below) | (~one_below & has_above)
     has_two = (one_below & has_above) | (~one_below & has_below)
-    for index, flag in enumerate((has_one, has_two, later, later & has_one, later & has_two)):
+    for index, flag in enumerate((has_one, has_two, later)):
         valid[index] = jnp.broadcast_to(jnp.where(flag, 1.0, 0.0), valid.shape[1:])
 
 
@@ -121,16 +121,17 @@
 
 
 def earlier_sums(double, single, pair, row):
-    frames = pair.shape[0]
+    frames, _, chans, width = pair.shape
+    blank = jnp.zeros((chans, width), pair.dtype)
     both, alone = [None] * 4, [None] * 4
-    for group in ((0, 1), (2,), (3,)):
-        count = min(3, 4 - group[0])
+    for group, count in (((0, 1), 3), ((2, 3), 2)):
         span = {frame: range(frames - 4 + frame, frames - 4 + frame + count) for frame in group}
-        depth = 2 * count * pair.shape[2]
-        sums = conv(double[:, :depth], [[pair[f, r] for f in span[frame] for r in range(2)] for frame in group])
+        depth = 2 * count * chans
+        read = lambda f, r: pair[f, r] if f < frames else blank
+        sums = conv(double[:, :depth], [[read(f, r) for f in span[frame] for r in range(2)] for frame in group])
         for frame, value in zip(group, sums):
             both[frame] = value
-        sums = conv(single[:, : depth // 2], [[pair[f, row] for f in span[frame]] for frame in group])
+        sums = conv(single[:, : depth // 2], [[read(f, row) for f in span[frame]] for frame in group])
         for frame, value in zip(group, sums):
             alone[frame] = value
     return both, alone
@@ -147,7 +148,7 @@
     both, alone = earlier_sums(double.at[side], single.at[side], near, 1 - side)
     for frame in range(4):
         for index, (value, row) in enumerate(((both[frame], side), (alone[frame], 1 - side))):
-            value = norm_silu(value + rest[frame, index], gain)
+            value = norm_silu(value * exists + rest[frame, index], gain)
             if index == 0:
                 value = value * exists
             if frame < 2:
@@ -162,13 +163,12 @@
 
 
 def two_kernel(
-    valid, two, prior, own, first, double, single, second_12, second_2, columns, partial_one, late_one,
-    rest_one, rest_two, late_sums, cells, inner, partial, late,
+    valid, two, inner, own, first, double, single, second_12, second_2, columns, partial_one, late_one,
+    rest_one, rest_two, late_sums, cells, partial, late,
 ):
     side = side_of_one()
     activate(two, cells.at[0], columns[0] * valid[1, 0:1])
     cells[1] = own[...]
-    activate(prior, inner, columns[0] * valid[2, 0:1])
     late[0] = late_one[...]
     present_frames(cells, 1 - side, valid[1, 0:1], first, columns, partial, late.at[1])
     earlier_rest(double, single, inner, side, partial_one, columns[1], rest_one)
@@ -180,19 +180,21 @@
             late_sums[frame, row] = value + columns[3]
 
 
-def prior_kernel(valid, prior_one, double, single, columns, rest, early, near):
-    activate(prior_one, near, columns[0] * valid[3, 0:1])
+def inner_kernel(valid, prior, columns, inner):
+    activate(prior, inner, columns[0] * valid[2, 0:1])
+
+
+def prior_kernel(valid, near, double, single, columns, rest, early):
     earlier_frames(
         double, single, near, side_of_one(), rest, valid[0, 0:1], valid[2, 0:1], columns[2], early
     )
 
 
 def last_kernel(
-    valid, video, prior_two, double, single, second, columns, rest, early_one, late_sums,
-    encoded, near, early,
+    valid, video, near, double, single, second, columns, rest, early_one, late_sums,
+    encoded, early,
 ):
     side = side_of_one()
-    activate(prior_two, near, columns[0] * valid[4, 0:1])
     early[0] = early_one[...]
     earlier_frames(
         double, single, near, 1 - side, rest, valid[1, 0:1], valid[2, 0:1], columns[2], early, (1,)
@@ -248,19 +250,12 @@
     return goal
 
 
-def exchange(video):
+def local(video, gamma_first, kernel_first, bias_first, gamma_second, kernel_second, bias_second):
+    _, frames, rows, chans, width = video.shape
+    assert frames == 4 and rows == 2
     prior = routed(video, later)
     two = routed(video, odd_pair)
     one = routed(video, even_pair)
-    prior_two = routed(prior, if_earlier(odd_pair))
-    prior_one = routed(prior, if_earlier(even_pair))
-    return one, two, prior, prior_one, prior_two
-
-
-def local(video, gamma_first, kernel_first, bias_first, gamma_second, kernel_second, bias_second):
-    _, frames, rows, chans, width = video.shape
-    assert frames == 4 and rows == 2
-    one, two, prior, prior_one, prior_two = exchange(video)
     bf16, f32 = jnp.bfloat16, jnp.float32
     shape = jax.ShapeDtypeStruct
     params = pltpu.CompilerParams(vmem_limit_bytes=24 * 2**20)
@@ -287,33 +282,36 @@
     late = shape((2, 2, chans, width), bf16)
     rest = shape((4, 2, chans, width), f32)
     early = shape((4, 2, chans, width), bf16)
-    valid = run(edge_kernel, shape((5, 8, width), f32), (), millions=2000)
+    valid = run(edge_kernel, shape((3, 8, width), f32), (), millions=2000)
     first, double, single, second, second_12, second_2 = run(
         weights_kernel,
         (stacked(12), stacked(2, 6), stacked(2, 3), stacked(9), stacked(6), stacked(3)),
         (kernel_first, kernel_second),
-        millions=2000,
+        millions=10,
     )
     own, columns = run(
         own_kernel,
         (shape(block, bf16), shape((4, chans, width), f32)),
         (video, gamma_first, bias_first, gamma_second, bias_second),
-        millions=1000,
-    )
+        millions=10,
+    )
+    inner = run(inner_kernel, shape(block, bf16), (valid, prior, columns), millions=10)
+    prior_two = routed(inner, if_earlier(odd_pair))
+    prior_one = routed(inner, if_earlier(even_pair))
     partial_one, late_one = run(one_kernel, (pair, late), (valid, one, own, first, columns), (cells,), 10)
     rest_one, rest_two, late_sums = run(
         two_kernel,
         (rest, rest, pair),
-        (valid, two, prior, own, first, double, single, second_12, second_2, columns, partial_one, late_one),
-        (cells, (block, bf16), (pair.shape, f32), ((2, *late.shape), bf16)),
+        (valid, two, inner, own, first, double, single, second_12, second_2, columns, partial_one, late_one),
+        (cells, (pair.shape, f32), ((2, *late.shape), bf16)),
         10,
     )
-    early_one = run(prior_kernel, early, (valid, prior_one, double, single, columns, rest_one), ((block, bf16),), 1000)
+    early_one = run(prior_kernel, early, (valid, prior_one, double, single, columns, rest_one), (), 1000)
     return run(
         last_kernel,
         shape(video.shape, bf16),
         (valid, video, prior_two, double, single, second, columns, rest_two, early_one, late_sums),
-        ((block, bf16), ((2, *early.shape), bf16)),
+        (((2, *early.shape), bf16),),
         1000,
     )
 

time: 15.6 us -> 15.6 us (level)
  Pallas kernels: 6.91 us -> 6.49 us
  waiting for transfers between devices: 5.17 us -> 5.36 us
    pallas_call x7 -> x8, Pallas kernels: 6.91 us -> 6.49 us  [run(): pl.pallas_call(kernel, out_shape=out_shape, in_specs=[VMEM] * len(operand...]
    ppermute x5, waiting for transfers between devices: 5.17 us -> 5.36 us  [routed(): return lax.ppermute(block, ('groups', 'rows', 'tm'), route)]
  transfers between devices with their start and end apart: 5 -> 5, of which waited for: 5 -> 5; matrix products, arithmetic and copies ran while one was open for 0% -> 0% of each run, Pallas kernels for 30% -> 29%
where the time goes in v6:
time: 15.6 us; the launch traced here: 15.4 us
  Pallas kernels  6.49 us (42%)
  waiting for transfers between devices  5.36 us (34%)
  starting transfers between devices  3.35 us (21%)
    pallas_call x8, Pallas kernels, run(): pl.pallas_call(kernel, out_shape=out_shape, in_specs=[VMEM] * len(operand...  6.49 us
    ppermute x5, waiting for transfers between devices, routed(): return lax.ppermute(block, ('groups', 'rows', 'tm'), route)  5.36 us
    ppermute x5, starting transfers between devices, routed(): return lax.ppermute(block, ('groups', 'rows', 'tm'), route)  3.35 us
  transfers between devices with their start and end apart: 5, of which 5 were waited for; matrix products, arithmetic and copies ran while one was open for 0% of the time, Pallas kernels for 29%

profile of v6, /device:TPU:18, one launch (start us, length us, event | category | flops | bytes accessed | tf_op | source)
XLA Modules:
  0.0 15.4 jit_solution(10544164072092956808)
XLA Ops:
  0.0 0.0 copy-start.2
  0.0 0.0 copy-start.4
  0.0 0.0 copy-start.5
  0.0 0.0 copy-start.6
  0.0 0.0 copy-start.3
  0.0 0.1 collective-permute-start
  0.1 1.6 %collective-permute-start.3 = (bf16[1,4,2,96,128]{4,3,2,1,0:T(8,128)(2,1)}, bf16[1,4,2,96,128]{4,3,2,1,0:T(8,128)(2,1)S(1)}, u32[]{:S(2)}, u32[]{:S(2)}) collective-permute-start(bf16[1,4,2,96,128]{4,3,2,1,0:T(8,128)(2,1)} %video.3), channel_id=1, source_target_pairs={{0,4},{1,5},{2,6},{3,7},{4,0},{5,1},{6,2},{7,3},{8,12},{9,13},{10,... | collective-permute-start | bytes 589832 | tf_op jit(solution)/shard_map/ppermute | solution.py:220
  1.7 0.0 collective-permute-start.2
  1.7 0.0 copy-start.1
  1.7 0.0 copy-done.2
  1.8 0.0 copy-done.4
  1.8 0.0 copy-done.5
  1.8 0.0 copy-done.6
  1.8 0.0 copy-done.3
  1.8 0.0 copy-start
  1.8 0.2 shard_map.74
  2.0 3.4 %collective-permute-done.prior = bf16[1,4,2,96,128]{4,3,2,1,0:T(8,128)(2,1)S(1)} collective-permute-done((bf16[1,4,2,96,128]{4,3,2,1,0:T(8,128)(2,1)}, bf16[1,4,2,96,128]{4,3,2,1,0:T(8,128)(2,1)S(1)}, u32[]{:S(2)}, u32[]{:S(2)}) %collective-permute-start) | collective-permute-done | bytes 196640 | tf_op jit(solution)/shard_map/ppermute | solution.py:220
  5.4 0.2 shard_map.75.inner
  5.5 1.6 %collective-permute-start.4 = (bf16[4,2,96,128]{3,2,1,0:T(8,128)(2,1)S(1)}, bf16[4,2,96,128]{3,2,1,0:T(8,128)(2,1)S(1)}, u32[]{:S(2)}, u32[]{:S(2)}) collective-permute-start(bf16[4,2,96,128]{3,2,1,0:T(8,128)(2,1)S(1)} %shard_map.75.inner), channel_id=1, source_target_pairs={{0,16},{1,5},{2,6},{3,7},{4,20},{5,1},{6,2},{7,3},{8,24},{9,13},{1... | collective-permute-start | bytes 589832 | tf_op jit(solution)/shard_map/ppermute | solution.py:220
  7.2 0.0 collective-permute-start.1
  7.2 0.0 copy-done.1
  7.2 0.0 copy-done
  7.2 0.7 %shard_map.76 = (bf16[288,1152]{1,0:T(8,128)(2,1)S(1)}, bf16[2,288,576]{2,1,0:T(8,128)(2,1)S(1)}, bf16[2,288,288]{2,1,0:T(8,128)(2,1)S(1)}, bf16[288,864]{1,0:T(...) custom-call(bf16[96,2592]{1,0:T(8,128)(2,1)S(1)} %copy-done, bf16[96,2592]{1,0:T(8,128)(2,1)S(1)} %copy-done.1), custom_call_target="tpu_custom_call" | custom-call | flops 10000000 | bytes 1000000 | tf_op jit(solution)/shard_map/pallas_call | solution.py:265
  7.9 0.2 %collective-permute-done.3.one = bf16[1,4,2,96,128]{4,3,2,1,0:T(8,128)(2,1)S(1)} collective-permute-done((bf16[1,4,2,96,128]{4,3,2,1,0:T(8,128)(2,1)}, bf16[1,4,2,96,128]{4,3,2,1,0:T(8,128)(2,1)S(1)}, u32[]{:S(2)}, u32[]{:S(2)}) %collective-permute-start.3) | collective-permute-done | bytes 196640 | tf_op jit(solution)/shard_map/ppermute | solution.py:220
  8.1 1.0 %shard_map.77 = (f32[2,2,96,128]{3,2,1,0:T(8,128)S(1)}, bf16[2,2,96,128]{3,2,1,0:T(8,128)(2,1)S(1)}) custom-call(f32[3,8,128]{2,1,0:T(8,128)S(1)} %shard_map.73.valid, bf16[1,4,2,96,128]{4,3,2,1,0:T(8,128)(2,1)S(1)} %collective-permute-done.3.one, bf16[4,2,96,128]{3,2,1,0:T(8,128)(2,1)S(1)} %get-tuple-element.22.own, ...), custom_call_target="tpu_custom_call" | custom-call | flops 10000000 | bytes 1000000 | tf_op jit(solution)/shard_map/pallas_call | solution.py:265
  9.1 0.6 %collective-permute-done.2.two = bf16[1,4,2,96,128]{4,3,2,1,0:T(8,128)(2,1)S(1)} collective-permute-done((bf16[1,4,2,96,128]{4,3,2,1,0:T(8,128)(2,1)}, bf16[1,4,2,96,128]{4,3,2,1,0:T(8,128)(2,1)S(1)}, u32[]{:S(2)}, u32[]{:S(2)}) %collective-permute-start.2) | collective-permute-done | bytes 196640 | tf_op jit(solution)/shard_map/ppermute | solution.py:220
  9.7 1.7 %shard_map.78 = (f32[4,2,96,128]{3,2,1,0:T(8,128)S(1)}, f32[4,2,96,128]{3,2,1,0:T(8,128)S(1)}, f32[2,2,96,128]{3,2,1,0:T(8,128)S(1)}) custom-call(f32[3,8,128]{2,1,0:T(8,128)S(1)} %shard_map.73.valid, bf16[1,4,2,96,128]{4,3,2,1,0:T(8,128)(2,1)S(1)} %collective-permute-done.2.two, bf16[4,2,96,128]{3,2,1,0:T(8,128)(2,1)S(1)} %shard_map.75.inner, ...), custom_call_target="tpu_custom_call" | custom-call | flops 10000000 | bytes 1000000 | tf_op jit(solution)/shard_map/pallas_call | solution.py:265
  11.4 0.6 %collective-permute-done.4.near = bf16[4,2,96,128]{3,2,1,0:T(8,128)(2,1)S(1)} collective-permute-done((bf16[4,2,96,128]{3,2,1,0:T(8,128)(2,1)S(1)}, bf16[4,2,96,128]{3,2,1,0:T(8,128)(2,1)S(1)}, u32[]{:S(2)}, u32[]{:S(2)}) %collective-permute-start.4) | collective-permute-done | bytes 196640 | tf_op jit(solution)/shard_map/ppermute | solution.py:220
  12.0 0.7 %shard_map.79.early_one = bf16[4,2,96,128]{3,2,1,0:T(8,128)(2,1)S(1)} custom-call(f32[3,8,128]{2,1,0:T(8,128)S(1)} %shard_map.73.valid, bf16[4,2,96,128]{3,2,1,0:T(8,128)(2,1)S(1)} %collective-permute-done.4.near, bf16[2,288,576]{2,1,0:T(8,128)(2,1)S(1)} %get-tuple-element.19.double, bf16[2,288,288]{2,1,0:T(8,128)(2,1)S(1)} %get-tuple-element.20.single, ...), custom_call_target="tpu_custom_call" | custom-call | flops 1000000000 | bytes 1000000 | tf_op jit(solution)/shard_map/pallas_call | solution.py:265
  12.6 0.6 %collective-permute-done.1.near = bf16[4,2,96,128]{3,2,1,0:T(8,128)(2,1)S(1)} collective-permute-done((bf16[4,2,96,128]{3,2,1,0:T(8,128)(2,1)S(1)}, bf16[4,2,96,128]{3,2,1,0:T(8,128)(2,1)S(1)}, u32[]{:S(2)}, u32[]{:S(2)}) %collective-permute-start.1) | collective-permute-done | bytes 196640 | tf_op jit(solution)/shard_map/ppermute | solution.py:220
  13.3 2.1 %shard_map.80 = bf16[1,4,2,96,128]{4,3,2,1,0:T(8,128)(2,1)} custom-call(f32[3,8,128]{2,1,0:T(8,128)S(1)} %shard_map.73.valid, bf16[1,4,2,96,128]{4,3,2,1,0:T(8,128)(2,1)S(1)} %copy-done.2, bf16[4,2,96,128]{3,2,1,0:T(8,128)(2,1)S(1)} %collective-permute-done.1.near, bf16[2,288,576]{2,1,0:T(8,128)(2,1)S(1)} %get-tuple-element.19.double, ...), custom_call_target="tpu_custom_call" | custom-call | flops 1000000000 | bytes 1000000 | tf_op jit(solution)/shard_map/pallas_call | solution.py:265
  (1 shorter events, 0.0 us)
Async XLA Ops:
  0.0 1.8 %copy-start.2 = (bf16[1,4,2,96,128]{4,3,2,1,0:T(8,128)(2,1)S(1)}, bf16[1,4,2,96,128]{4,3,2,1,0:T(8,128)(2,1)}, u32[]{:S(2)}) copy-start(bf16[1,4,2,96,128]{4,3,2,1,0:T(8,128)(2,1)} %video.3) | copy-start | bytes 589828
  0.0 1.8 %copy-start.4 = (f32[96]{0:T(128)S(1)}, f32[96]{0:T(128)}, u32[]{:S(2)}) copy-start(f32[96]{0:T(128)} %bias_first.1) | copy-start | bytes 1156
  0.0 1.8 %copy-start.5 = (f32[96]{0:T(128)S(1)}, f32[96]{0:T(128)}, u32[]{:S(2)}) copy-start(f32[96]{0:T(128)} %gamma_second.1) | copy-start | bytes 1156
  0.0 1.8 %copy-start.6 = (f32[96]{0:T(128)S(1)}, f32[96]{0:T(128)}, u32[]{:S(2)}) copy-start(f32[96]{0:T(128)} %bias_second.1) | copy-start | bytes 1156
  0.0 1.8 %copy-start.3 = (f32[96]{0:T(128)S(1)}, f32[96]{0:T(128)}, u32[]{:S(2)}) copy-start(f32[96]{0:T(128)} %gamma_first.1) | copy-start | bytes 1156
  0.0 5.4 %collective-permute-start = (bf16[1,4,2,96,128]{4,3,2,1,0:T(8,128)(2,1)}, bf16[1,4,2,96,128]{4,3,2,1,0:T(8,128)(2,1)S(1)}, u32[]{:S(2)}, u32[]{:S(2)}) collective-permute-start(bf16[1,4,2,96,128]{4,3,2,1,0:T(8,128)(2,1)} %video.3), channel_id=1, source_target_pairs={{0,1},{1,2},{2,3},{3,0},{4,5},{5,6},{6,7},{7,4},{8,9},{9,10},{10,1... | collective-permute-start | bytes 589832 | tf_op jit(solution)/shard_map/ppermute | solution.py:220
  0.1 8.0 %collective-permute-start.3 = (bf16[1,4,2,96,128]{4,3,2,1,0:T(8,128)(2,1)}, bf16[1,4,2,96,128]{4,3,2,1,0:T(8,128)(2,1)S(1)}, u32[]{:S(2)}, u32[]{:S(2)}) collective-permute-start(bf16[1,4,2,96,128]{4,3,2,1,0:T(8,128)(2,1)} %video.3), channel_id=1, source_target_pairs={{0,4},{1,5},{2,6},{3,7},{4,0},{5,1},{6,2},{7,3},{8,12},{9,13},{10,... | collective-permute-start | bytes 589832 | tf_op jit(solution)/shard_map/ppermute | solution.py:220
  1.7 7.9 %collective-permute-start.2 = (bf16[1,4,2,96,128]{4,3,2,1,0:T(8,128)(2,1)}, bf16[1,4,2,96,128]{4,3,2,1,0:T(8,128)(2,1)S(1)}, u32[]{:S(2)}, u32[]{:S(2)}) collective-permute-start(bf16[1,4,2,96,128]{4,3,2,1,0:T(8,128)(2,1)} %video.3), channel_id=1, source_target_pairs={{0,1},{1,0},{2,3},{3,2},{4,8},{5,9},{6,10},{7,11},{8,4},{9,5},{10,... | collective-permute-start | bytes 589832 | tf_op jit(solution)/shard_map/ppermute | solution.py:220
  1.7 5.5 %copy-start.1 = (bf16[96,2592]{1,0:T(8,128)(2,1)S(1)}, bf16[96,2592]{1,0:T(8,128)(2,1)}, u32[]{:S(2)}) copy-start(bf16[96,2592]{1,0:T(8,128)(2,1)} %kernel_second.1) | copy-start | bytes 1492996
  1.8 5.4 %copy-start = (bf16[96,2592]{1,0:T(8,128)(2,1)S(1)}, bf16[96,2592]{1,0:T(8,128)(2,1)}, u32[]{:S(2)}) copy-start(bf16[96,2592]{1,0:T(8,128)(2,1)} %kernel_first.1) | copy-start | bytes 1492996
  5.5 6.4 %collective-permute-start.4 = (bf16[4,2,96,128]{3,2,1,0:T(8,128)(2,1)S(1)}, bf16[4,2,96,128]{3,2,1,0:T(8,128)(2,1)S(1)}, u32[]{:S(2)}, u32[]{:S(2)}) collective-permute-start(bf16[4,2,96,128]{3,2,1,0:T(8,128)(2,1)S(1)} %shard_map.75.inner), channel_id=1, source_target_pairs={{0,16},{1,5},{2,6},{3,7},{4,20},{5,1},{6,2},{7,3},{8,24},{9,13},{1... | collective-permute-start | bytes 589832 | tf_op jit(solution)/shard_map/ppermute | solution.py:220
  7.2 6.1 %collective-permute-start.1 = (bf16[4,2,96,128]{3,2,1,0:T(8,128)(2,1)S(1)}, bf16[4,2,96,128]{3,2,1,0:T(8,128)(2,1)S(1)}, u32[]{:S(2)}, u32[]{:S(2)}) collective-permute-start(bf16[4,2,96,128]{3,2,1,0:T(8,128)(2,1)S(1)} %shard_map.75.inner), channel_id=1, source_target_pairs={{0,1},{1,0},{2,3},{3,2},{4,20},{5,9},{6,10},{7,11},{8,24},{9,5},{1... | collective-permute-start | bytes 589832 | tf_op jit(solution)/shard_map/ppermute | solution.py:220

commit v7 on v6

--- a/solution.py
+++ b/solution.py
@@ -80,23 +80,27 @@
         valid[index] = jnp.broadcast_to(jnp.where(flag, 1.0, 0.0), valid.shape[1:])
 
 
-def weights_kernel(kernel_first, kernel_second, first, double, single, second, second_12, second_2):
-    weights = kernel_first[...]
-    restack(weights, [(i, j) if j < 3 else None for i in range(3) for j in range(4)], first)
+def restack_sides(weights, double, single):
     restack(weights, [(i, j) for i in range(3) for j in (0, 1)], double, (0,))
     restack(weights, [(i, j) for i in range(3) for j in (1, 2)], double, (1,))
     restack(weights, [(i, 0) for i in range(3)], single, (0,))
     restack(weights, [(i, 2) for i in range(3)], single, (1,))
-    weights = kernel_second[...]
-    restack(weights, [(i, j) for i in range(3) for j in range(3)], second)
-    restack(weights, [(i, j) for i in (1, 2) for j in range(3)], second_12)
-    restack(weights, [(2, j) for j in range(3)], second_2)
-
-
-def own_kernel(video, gamma_first, bias_first, gamma_second, bias_second, own, columns):
+
+
+def own_kernel(
+    valid, video, gamma_first, kernel_first, bias_first, gamma_second, kernel_second, bias_second,
+    own, columns, first, double, single, second_double, second_single, second_12, second_2,
+):
     for index, vector in enumerate((gamma_first, bias_first, gamma_second, bias_second)):
         columns[index] = jnp.broadcast_to(column(vector), columns.shape[1:])
     activate(video, own, columns[0])
+    weights = kernel_first[...]
+    restack(weights, [(i, j) if j < 3 else None for i in range(3) for j in range(4)], first)
+    restack_sides(weights, double, single)
+    weights = kernel_second[...]
+    restack_sides(weights, second_double, second_single)
+    restack(weights, [(i, j) for i in (1, 2) for j in range(3)], second_12)
+    restack(weights, [(2, j) for j in range(3)], second_2)
 
 
 def present_frames(cells, side, exists, first, columns, partial, late):
@@ -163,7 +167,7 @@
 
 
 def two_kernel(
-    valid, two, inner, own, first, double, single, second_12, second_2, columns, partial_one, late_one,
+    partial_one, late_one, valid, two, inner, own, first, double, single, second_12, second_2, columns,
     rest_one, rest_two, late_sums, cells, partial, late,
 ):
     side = side_of_one()
@@ -184,33 +188,25 @@
     activate(prior, inner, columns[0] * valid[2, 0:1])
 
 
-def prior_kernel(valid, near, double, single, columns, rest, early):
-    earlier_frames(
-        double, single, near, side_of_one(), rest, valid[0, 0:1], valid[2, 0:1], columns[2], early
-    )
-
-
-def last_kernel(
-    valid, video, near, double, single, second, columns, rest, early_one, late_sums,
-    encoded, early,
+def prior_kernel(
+    valid, video, near, double, single, second_double, second_single, columns, rest, late_sums, sums, early
 ):
     side = side_of_one()
-    early[0] = early_one[...]
-    earlier_frames(
-        double, single, near, 1 - side, rest, valid[1, 0:1], valid[2, 0:1], columns[2], early, (1,)
-    )
-    rows = four_rows(side)
+    earlier_frames(double, single, near, side, rest, valid[0, 0:1], valid[2, 0:1], columns[2], early)
+    both, alone = earlier_sums(second_double.at[side], second_single.at[side], early, 1 - side)
     for frame in range(4):
-        count = min(3, 4 - frame)
-        windows = [
-            [early[a, f, r] for f in range(frame, frame + count) for a, r in rows[row : row + 3]]
-            for row in range(2)
-        ]
-        sums = conv(second[:, : 3 * count * near.shape[2]], windows)
-        for row in range(2):
+        for value, row in ((both[frame], side), (alone[frame], 1 - side)):
             rest_of_sum = columns[3] if frame < 2 else late_sums[frame - 2, row]
-            value = video[0, frame, row].astype(jnp.float32) + (sums[row] + rest_of_sum)
-            encoded[0, frame, row] = value.astype(jnp.bfloat16)
+            sums[frame, row] = video[0, frame, row].astype(jnp.float32) + (value + rest_of_sum)
+
+
+def last_kernel(valid, near, double, single, second_double, second_single, columns, rest, sums, encoded, early):
+    side = 1 - side_of_one()
+    earlier_frames(double, single, near, side, rest, valid[1, 0:1], valid[2, 0:1], columns[2], early)
+    both, alone = earlier_sums(second_double.at[side], second_single.at[side], early, 1 - side)
+    for frame in range(4):
+        for value, row in ((both[frame], side), (alone[frame], 1 - side)):
+            encoded[0, frame, row] = (sums[frame, row] + value).astype(jnp.bfloat16)
 
 
 def routed(block, goal):
@@ -283,16 +279,14 @@
     rest = shape((4, 2, chans, width), f32)
     early = shape((4, 2, chans, width), bf16)
     valid = run(edge_kernel, shape((3, 8, width), f32), (), millions=2000)
-    first, double, single, second, second_12, second_2 = run(
-        weights_kernel,
-        (stacked(12), stacked(2, 6), stacked(2, 3), stacked(9), stacked(6), stacked(3)),
-        (kernel_first, kernel_second),
-        millions=10,
-    )
-    own, columns = run(
+    own, columns, first, double, single, second_double, second_single, second_12, second_2 = run(
         own_kernel,
-        (shape(block, bf16), shape((4, chans, width), f32)),
-        (video, gamma_first, bias_first, gamma_second, bias_second),
+        (
+            shape(block, bf16),
+            shape((4, chans, width), f32),
+            *(stacked(12), stacked(2, 6), stacked(2, 3), stacked(2, 6), stacked(2, 3), stacked(6), stacked(3)),
+        ),
+        (valid, video, gamma_first, kernel_first, bias_first, gamma_second, kernel_second, bias_second),
         millions=10,
     )
     inner = run(inner_kernel, shape(block, bf16), (valid, prior, columns), millions=10)
@@ -302,16 +296,22 @@
     rest_one, rest_two, late_sums = run(
         two_kernel,
         (rest, rest, pair),
-        (valid, two, inner, own, first, double, single, second_12, second_2, columns, partial_one, late_one),
+        (partial_one, late_one, valid, two, inner, own, first, double, single, second_12, second_2, columns),
         (cells, (pair.shape, f32), ((2, *late.shape), bf16)),
         10,
     )
-    early_one = run(prior_kernel, early, (valid, prior_one, double, single, columns, rest_one), (), 1000)
+    sums = run(
+        prior_kernel,
+        rest,
+        (valid, video, prior_one, double, single, second_double, second_single, columns, rest_one, late_sums),
+        ((early.shape, bf16),),
+        1000,
+    )
     return run(
         last_kernel,
         shape(video.shape, bf16),
-        (valid, video, prior_two, double, single, second, columns, rest_two, early_one, late_sums),
-        (((2, *early.shape), bf16),),
+        (valid, prior_two, double, single, second_double, second_single, columns, rest_two, sums),
+        ((early.shape, bf16),),
         1000,
     )
 

time: 15.6 us -> 15.5 us (level)
  the two profiles are of different devices: /device:TPU:18 before, /device:TPU:0 now
where the time goes in v7:
time: 15.5 us; the launch traced here: 15.4 us
  Pallas kernels  6.84 us (44%)
  starting transfers between devices  6.81 us (44%)
  waiting for transfers between devices  1.57 us (10%)
    pallas_call x7, Pallas kernels, run(): pl.pallas_call(kernel, out_shape=out_shape, in_specs=[VMEM] * len(operand...  6.84 us
    ppermute x5, starting transfers between devices, routed(): return lax.ppermute(block, ('groups', 'rows', 'tm'), route)  6.81 us
    ppermute x5, waiting for transfers between devices, routed(): return lax.ppermute(block, ('groups', 'rows', 'tm'), route)  1.57 us
  transfers between devices with their start and end apart: 5, of which 2 were waited for; matrix products, arithmetic and copies ran while one was open for 0% of the time, Pallas kernels for 32%

profile of v7, /device:TPU:0, one launch (start us, length us, event | category | flops | bytes accessed | tf_op | source)
XLA Modules:
  0.0 15.4 jit_solution(14954823981161064082)
XLA Ops:
  0.0 0.0 copy-start
  0.0 0.0 copy-start.6
  0.0 0.0 copy-start.2
  0.0 0.0 copy-start.5
  0.0 0.0 copy-start.4
  0.0 0.0 copy-start.1
  0.0 0.0 copy-start.3
  0.0 0.5 %collective-permute-start = (bf16[1,4,2,96,128]{4,3,2,1,0:T(8,128)(2,1)}, bf16[1,4,2,96,128]{4,3,2,1,0:T(8,128)(2,1)S(1)}, u32[]{:S(2)}, u32[]{:S(2)}) collective-permute-start(bf16[1,4,2,96,128]{4,3,2,1,0:T(8,128)(2,1)} %video.3), channel_id=1, source_target_pairs={{0,1},{1,2},{2,3},{3,0},{4,5},{5,6},{6,7},{7,4},{8,9},{9,10},{10,1... | collective-permute-start | bytes 589832 | tf_op jit(solution)/shard_map/ppermute | solution.py:216
  0.6 2.6 %collective-permute-start.2 = (bf16[1,4,2,96,128]{4,3,2,1,0:T(8,128)(2,1)}, bf16[1,4,2,96,128]{4,3,2,1,0:T(8,128)(2,1)S(1)}, u32[]{:S(2)}, u32[]{:S(2)}) collective-permute-start(bf16[1,4,2,96,128]{4,3,2,1,0:T(8,128)(2,1)} %video.3), channel_id=1, source_target_pairs={{0,4},{1,5},{2,6},{3,7},{4,0},{5,1},{6,2},{7,3},{8,12},{9,13},{10,... | collective-permute-start | bytes 589832 | tf_op jit(solution)/shard_map/ppermute | solution.py:216
  3.2 1.2 %collective-permute-start.3 = (bf16[1,4,2,96,128]{4,3,2,1,0:T(8,128)(2,1)}, bf16[1,4,2,96,128]{4,3,2,1,0:T(8,128)(2,1)S(1)}, u32[]{:S(2)}, u32[]{:S(2)}) collective-permute-start(bf16[1,4,2,96,128]{4,3,2,1,0:T(8,128)(2,1)} %video.3), channel_id=1, source_target_pairs={{0,1},{1,0},{2,3},{3,2},{4,8},{5,9},{6,10},{7,11},{8,4},{9,5},{10,... | collective-permute-start | bytes 589832 | tf_op jit(solution)/shard_map/ppermute | solution.py:216
  4.5 0.0 copy-done
  4.5 0.0 copy-done.6
  4.5 0.0 copy-done.2
  4.5 0.0 copy-done.5
  4.5 0.0 copy-done.4
  4.5 0.0 copy-done.1
  4.5 0.0 copy-done.3
  4.5 0.8 %shard_map.74 = (bf16[4,2,96,128]{3,2,1,0:T(8,128)(2,1)S(1)}, f32[4,96,128]{2,1,0:T(8,128)S(1)}, bf16[288,1152]{1,0:T(8,128)(2,1)S(1)}, bf16[2,288,576]{2,1,0:T(...) custom-call(f32[3,8,128]{2,1,0:T(8,128)S(1)} %shard_map.73.valid, ...), custom_call_target="tpu_custom_call" | custom-call | flops 10000000 | bytes 1000000 | tf_op jit(solution)/shard_map/pallas_call | solution.py:261
  5.3 0.7 %collective-permute-done.prior = bf16[1,4,2,96,128]{4,3,2,1,0:T(8,128)(2,1)S(1)} collective-permute-done((bf16[1,4,2,96,128]{4,3,2,1,0:T(8,128)(2,1)}, bf16[1,4,2,96,128]{4,3,2,1,0:T(8,128)(2,1)S(1)}, u32[]{:S(2)}, u32[]{:S(2)}) %collective-permute-start) | collective-permute-done | bytes 196640 | tf_op jit(solution)/shard_map/ppermute | solution.py:216
  6.0 0.2 shard_map.75.inner
  6.2 2.4 %collective-permute-start.4 = (bf16[4,2,96,128]{3,2,1,0:T(8,128)(2,1)S(1)}, bf16[4,2,96,128]{3,2,1,0:T(8,128)(2,1)S(1)}, u32[]{:S(2)}, u32[]{:S(2)}) collective-permute-start(bf16[4,2,96,128]{3,2,1,0:T(8,128)(2,1)S(1)} %shard_map.75.inner), channel_id=1, source_target_pairs={{0,16},{1,5},{2,6},{3,7},{4,20},{5,1},{6,2},{7,3},{8,24},{9,13},{1... | collective-permute-start | bytes 589832 | tf_op jit(solution)/shard_map/ppermute | solution.py:216
  8.6 0.0 collective-permute-start.1
  8.6 0.0 collective-permute-done.2.one
  8.6 1.0 %shard_map.76 = (f32[2,2,96,128]{3,2,1,0:T(8,128)S(1)}, bf16[2,2,96,128]{3,2,1,0:T(8,128)(2,1)S(1)}) custom-call(f32[3,8,128]{2,1,0:T(8,128)S(1)} %shard_map.73.valid, bf16[1,4,2,96,128]{4,3,2,1,0:T(8,128)(2,1)S(1)} %collective-permute-done.2.one, bf16[4,2,96,128]{3,2,1,0:T(8,128)(2,1)S(1)} %get-tuple-element.24.own, ...), custom_call_target="tpu_custom_call" | custom-call | flops 10000000 | bytes 1000000 | tf_op jit(solution)/shard_map/pallas_call | solution.py:261
  9.7 0.0 collective-permute-done.3.two
  9.7 1.7 %shard_map.77 = (f32[4,2,96,128]{3,2,1,0:T(8,128)S(1)}, f32[4,2,96,128]{3,2,1,0:T(8,128)S(1)}, f32[2,2,96,128]{3,2,1,0:T(8,128)S(1)}) custom-call(f32[2,2,96,128]{3,2,1,0:T(8,128)S(1)} %get-tuple-element.26.partial_one, bf16[2,2,96,128]{3,2,1,0:T(8,128)(2,1)S(1)} %get-tuple-element.27.late_one, f32[3,8,128]{2,1,0:T(8,128)S(1)} %shard_map.73.valid, ...), custom_call_target="tpu_custom_call" | custom-call | flops 10000000 | bytes 1000000 | tf_op jit(solution)/shard_map/pallas_call | solution.py:261
  11.4 0.9 %collective-permute-done.4.near = bf16[4,2,96,128]{3,2,1,0:T(8,128)(2,1)S(1)} collective-permute-done((bf16[4,2,96,128]{3,2,1,0:T(8,128)(2,1)S(1)}, bf16[4,2,96,128]{3,2,1,0:T(8,128)(2,1)S(1)}, u32[]{:S(2)}, u32[]{:S(2)}) %collective-permute-start.4) | collective-permute-done | bytes 196640 | tf_op jit(solution)/shard_map/ppermute | solution.py:216
  12.2 1.2 %shard_map.78.sums = f32[4,2,96,128]{3,2,1,0:T(8,128)S(1)} custom-call(f32[3,8,128]{2,1,0:T(8,128)S(1)} %shard_map.73.valid, bf16[1,4,2,96,128]{4,3,2,1,0:T(8,128)(2,1)S(1)} %copy-done, bf16[4,2,96,128]{3,2,1,0:T(8,128)(2,1)S(1)} %collective-permute-done.4.near, bf16[2,288,576]{2,1,0:T(8,128)(2,1)S(1)} %get-tuple-element.20.double, ...), custom_call_target="tpu_custom_call" | custom-call | flops 1000000000 | bytes 1000000 | tf_op jit(solution)/shard_map/pallas_call | solution.py:261
  13.5 0.0 collective-permute-done.1.near
  13.5 1.9 %shard_map.79 = bf16[1,4,2,96,128]{4,3,2,1,0:T(8,128)(2,1)} custom-call(f32[3,8,128]{2,1,0:T(8,128)S(1)} %shard_map.73.valid, bf16[4,2,96,128]{3,2,1,0:T(8,128)(2,1)S(1)} %collective-permute-done.1.near, bf16[2,288,576]{2,1,0:T(8,128)(2,1)S(1)} %get-tuple-element.20.double, bf16[2,288,288]{2,1,0:T(8,128)(2,1)S(1)} %get-tuple-element.21.single, ...), custom_call_target="tpu_custom_call" | custom-call | flops 1000000000 | bytes 1000000 | tf_op jit(solution)/shard_map/pallas_call | solution.py:261
  (1 shorter events, 0.0 us)
Async XLA Ops:
  0.0 4.5 %copy-start = (bf16[1,4,2,96,128]{4,3,2,1,0:T(8,128)(2,1)S(1)}, bf16[1,4,2,96,128]{4,3,2,1,0:T(8,128)(2,1)}, u32[]{:S(2)}) copy-start(bf16[1,4,2,96,128]{4,3,2,1,0:T(8,128)(2,1)} %video.3) | copy-start | bytes 589828
  0.0 4.5 %copy-start.6 = (f32[96]{0:T(128)S(1)}, f32[96]{0:T(128)}, u32[]{:S(2)}) copy-start(f32[96]{0:T(128)} %bias_second.1) | copy-start | bytes 1156
  0.0 4.5 %copy-start.2 = (bf16[96,2592]{1,0:T(8,128)(2,1)S(1)}, bf16[96,2592]{1,0:T(8,128)(2,1)}, u32[]{:S(2)}) copy-start(bf16[96,2592]{1,0:T(8,128)(2,1)} %kernel_second.1) | copy-start | bytes 1492996
  0.0 4.5 %copy-start.5 = (f32[96]{0:T(128)S(1)}, f32[96]{0:T(128)}, u32[]{:S(2)}) copy-start(f32[96]{0:T(128)} %gamma_second.1) | copy-start | bytes 1156
  0.0 4.5 %copy-start.4 = (f32[96]{0:T(128)S(1)}, f32[96]{0:T(128)}, u32[]{:S(2)}) copy-start(f32[96]{0:T(128)} %bias_first.1) | copy-start | bytes 1156
  0.0 4.5 %copy-start.1 = (bf16[96,2592]{1,0:T(8,128)(2,1)S(1)}, bf16[96,2592]{1,0:T(8,128)(2,1)}, u32[]{:S(2)}) copy-start(bf16[96,2592]{1,0:T(8,128)(2,1)} %kernel_first.1) | copy-start | bytes 1492996
  0.0 4.5 %copy-start.3 = (f32[96]{0:T(128)S(1)}, f32[96]{0:T(128)}, u32[]{:S(2)}) copy-start(f32[96]{0:T(128)} %gamma_first.1) | copy-start | bytes 1156
  0.0 6.0 %collective-permute-start = (bf16[1,4,2,96,128]{4,3,2,1,0:T(8,128)(2,1)}, bf16[1,4,2,96,128]{4,3,2,1,0:T(8,128)(2,1)S(1)}, u32[]{:S(2)}, u32[]{:S(2)}) collective-permute-start(bf16[1,4,2,96,128]{4,3,2,1,0:T(8,128)(2,1)} %video.3), channel_id=1, source_target_pairs={{0,1},{1,2},{2,3},{3,0},{4,5},{5,6},{6,7},{7,4},{8,9},{9,10},{10,1... | collective-permute-start | bytes 589832 | tf_op jit(solution)/shard_map/ppermute | solution.py:216
  0.6 8.0 %collective-permute-start.2 = (bf16[1,4,2,96,128]{4,3,2,1,0:T(8,128)(2,1)}, bf16[1,4,2,96,128]{4,3,2,1,0:T(8,128)(2,1)S(1)}, u32[]{:S(2)}, u32[]{:S(2)}) collective-permute-start(bf16[1,4,2,96,128]{4,3,2,1,0:T(8,128)(2,1)} %video.3), channel_id=1, source_target_pairs={{0,4},{1,5},{2,6},{3,7},{4,0},{5,1},{6,2},{7,3},{8,12},{9,13},{10,... | collective-permute-start | bytes 589832 | tf_op jit(solution)/shard_map/ppermute | solution.py:216
  3.2 6.5 %collective-permute-start.3 = (bf16[1,4,2,96,128]{4,3,2,1,0:T(8,128)(2,1)}, bf16[1,4,2,96,128]{4,3,2,1,0:T(8,128)(2,1)S(1)}, u32[]{:S(2)}, u32[]{:S(2)}) collective-permute-start(bf16[1,4,2,96,128]{4,3,2,1,0:T(8,128)(2,1)} %video.3), channel_id=1, source_target_pairs={{0,1},{1,0},{2,3},{3,2},{4,8},{5,9},{6,10},{7,11},{8,4},{9,5},{10,... | collective-permute-start | bytes 589832 | tf_op jit(solution)/shard_map/ppermute | solution.py:216
  6.2 6.0 %collective-permute-start.4 = (bf16[4,2,96,128]{3,2,1,0:T(8,128)(2,1)S(1)}, bf16[4,2,96,128]{3,2,1,0:T(8,128)(2,1)S(1)}, u32[]{:S(2)}, u32[]{:S(2)}) collective-permute-start(bf16[4,2,96,128]{3,2,1,0:T(8,128)(2,1)S(1)} %shard_map.75.inner), channel_id=1, source_target_pairs={{0,16},{1,5},{2,6},{3,7},{4,20},{5,1},{6,2},{7,3},{8,24},{9,13},{1... | collective-permute-start | bytes 589832 | tf_op jit(solution)/shard_map/ppermute | solution.py:216
  8.6 4.9 %collective-permute-start.1 = (bf16[4,2,96,128]{3,2,1,0:T(8,128)(2,1)S(1)}, bf16[4,2,96,128]{3,2,1,0:T(8,128)(2,1)S(1)}, u32[]{:S(2)}, u32[]{:S(2)}) collective-permute-start(bf16[4,2,96,128]{3,2,1,0:T(8,128)(2,1)S(1)} %shard_map.75.inner), channel_id=1, source_target_pairs={{0,1},{1,0},{2,3},{3,2},{4,20},{5,9},{6,10},{7,11},{8,24},{9,5},{1... | collective-permute-start | bytes 589832 | tf_op jit(solution)/shard_map/ppermute | solution.py:216

commit v8 on v7

--- a/solution.py
+++ b/solution.py
@@ -9,6 +9,7 @@
 
 epsilon = 1e-06
 VMEM = pl.BlockSpec(memory_space=pltpu.VMEM)
+FIRST, LAST = ((0, 1), 3), ((2, 3), 2)
 
 
 def column(vector_ref):
@@ -124,40 +125,45 @@
                 late[frame - 2, row] = (norm_silu(hidden, gain) * mask).astype(jnp.bfloat16)
 
 
-def earlier_sums(double, single, pair, row):
+def earlier_sums(double, single, pair, row, group, count):
     frames, _, chans, width = pair.shape
     blank = jnp.zeros((chans, width), pair.dtype)
-    both, alone = [None] * 4, [None] * 4
-    for group, count in (((0, 1), 3), ((2, 3), 2)):
-        span = {frame: range(frames - 4 + frame, frames - 4 + frame + count) for frame in group}
-        depth = 2 * count * chans
-        read = lambda f, r: pair[f, r] if f < frames else blank
-        sums = conv(double[:, :depth], [[read(f, r) for f in span[frame] for r in range(2)] for frame in group])
-        for frame, value in zip(group, sums):
-            both[frame] = value
-        sums = conv(single[:, : depth // 2], [[read(f, row) for f in span[frame]] for frame in group])
-        for frame, value in zip(group, sums):
-            alone[frame] = value
-    return both, alone
+    depth = 2 * count * chans
+    spans = [range(frames - 4 + frame, frames - 4 + frame + count) for frame in group]
+
+    def read(frame, at):
+        return pair[frame, at] if frame < frames else blank
+
+    both = conv(double[:, :depth], [[read(f, r) for f in span for r in range(2)] for span in spans])
+    alone = conv(single[:, : depth // 2], [[read(f, row) for f in span] for span in spans])
+    return list(zip(group, both, alone))
 
 
 def earlier_rest(double, single, inner, side, partial, bias, rest):
-    both, alone = earlier_sums(double.at[1 - side], single.at[1 - side], inner, side)
-    for frame in range(4):
-        for index, (value, row) in enumerate(((alone[frame], side), (both[frame], 1 - side))):
-            rest[frame, index] = value + (bias if frame < 2 else partial[frame - 2, row])
-
-
-def earlier_frames(double, single, near, side, rest, exists, later, gain, early, lead=()):
-    both, alone = earlier_sums(double.at[side], single.at[side], near, 1 - side)
-    for frame in range(4):
-        for index, (value, row) in enumerate(((both[frame], side), (alone[frame], 1 - side))):
+    for group, count in (FIRST, LAST):
+        for frame, both, alone in earlier_sums(double.at[1 - side], single.at[1 - side], inner, side, group, count):
+            for index, (value, row) in enumerate(((alone, side), (both, 1 - side))):
+                rest[frame, index] = value + (bias if frame < 2 else partial[frame - 2, row])
+
+
+def earlier_frames(sums, side, rest, exists, later, gain, early):
+    for frame, both, alone in sums:
+        for index, (value, row) in enumerate(((both, side), (alone, 1 - side))):
             value = norm_silu(value * exists + rest[frame, index], gain)
             if index == 0:
                 value = value * exists
             if frame < 2:
                 value = value * later
-            early[(*lead, frame, row)] = value.astype(jnp.bfloat16)
+            early[frame, row] = value.astype(jnp.bfloat16)
+
+
+def earlier_result(double, single, near, second_double, second_single, side, rest, exists, later, gain, early):
+    sums = earlier_sums(double.at[side], single.at[side], near, 1 - side, *LAST)
+    earlier_frames(sums, side, rest, exists, later, gain, early)
+    sums = earlier_sums(double.at[side], single.at[side], near, 1 - side, *FIRST)
+    result = earlier_sums(second_double.at[side], second_single.at[side], early, 1 - side, *LAST)
+    earlier_frames(sums, side, rest, exists, later, gain, early)
+    return result + earlier_sums(second_double.at[side], second_single.at[side], early, 1 - side, *FIRST)
 
 
 def one_kernel(valid, one, own, first, columns, partial, late, cells):
@@ -192,20 +198,39 @@
     valid, video, near, double, single, second_double, second_single, columns, rest, late_sums, sums, early
 ):
     side = side_of_one()
-    earlier_frames(double, single, near, side, rest, valid[0, 0:1], valid[2, 0:1], columns[2], early)
-    both, alone = earlier_sums(second_double.at[side], second_single.at[side], early, 1 - side)
-    for frame in range(4):
-        for value, row in ((both[frame], side), (alone[frame], 1 - side)):
+    result = earlier_result(
+        double, single, near, second_double, second_single, side, rest, valid[0, 0:1], valid[2, 0:1], columns[2], early
+    )
+    for frame, both, alone in result:
+        for value, row in ((both, side), (alone, 1 - side)):
             rest_of_sum = columns[3] if frame < 2 else late_sums[frame - 2, row]
             sums[frame, row] = video[0, frame, row].astype(jnp.float32) + (value + rest_of_sum)
 
 
-def last_kernel(valid, near, double, single, second_double, second_single, columns, rest, sums, encoded, early):
+def last_kernel(
+    valid, near, double, single, second_double, second_single, columns, rest, sums, encoded, early, near_sums
+):
     side = 1 - side_of_one()
-    earlier_frames(double, single, near, side, rest, valid[1, 0:1], valid[2, 0:1], columns[2], early)
-    both, alone = earlier_sums(second_double.at[side], second_single.at[side], early, 1 - side)
-    for frame in range(4):
-        for value, row in ((both[frame], side), (alone[frame], 1 - side)):
+    has_earlier = lax.axis_index("tm") > 0
+
+    @pl.when(has_earlier)
+    def _():
+        for group, count in (LAST, FIRST):
+            for frame, both, alone in earlier_sums(double.at[side], single.at[side], near, 1 - side, group, count):
+                near_sums[frame, 0] = both
+                near_sums[frame, 1] = alone
+
+    @pl.when(~has_earlier)
+    def _():
+        near_sums[...] = jnp.zeros_like(near_sums)
+
+    result = []
+    for group, count in (LAST, FIRST):
+        parts = [(frame, near_sums[frame, 0], near_sums[frame, 1]) for frame in group]
+        earlier_frames(parts, side, rest, valid[1, 0:1], valid[2, 0:1], columns[2], early)
+        result += earlier_sums(second_double.at[side], second_single.at[side], early, 1 - side, group, count)
+    for frame, both, alone in result:
+        for value, row in ((both, side), (alone, 1 - side)):
             encoded[0, frame, row] = (sums[frame, row] + value).astype(jnp.bfloat16)
 
 
@@ -311,7 +336,7 @@
         last_kernel,
         shape(video.shape, bf16),
         (valid, prior_two, double, single, second_double, second_single, columns, rest_two, sums),
-        ((early.shape, bf16),),
+        ((early.shape, bf16), (rest.shape, f32)),
         1000,
     )
 

time: 15.5 us -> 15.4 us (level)
  the two profiles are of different devices: /device:TPU:0 before, /device:TPU:18 now
where the time goes in v8:
time: 15.4 us; the launch traced here: 15.2 us
  Pallas kernels  6.79 us (44%)
  waiting for transfers between devices  4.92 us (32%)
  starting transfers between devices  3.35 us (22%)
    pallas_call x7, Pallas kernels, run(): pl.pallas_call(kernel, out_shape=out_shape, in_specs=[VMEM] * len(operand...  6.79 us
    ppermute x5, waiting for transfers between devices, routed(): return lax.ppermute(block, ('groups', 'rows', 'tm'), route)  4.92 us
    ppermute x5, starting transfers between devices, routed(): return lax.ppermute(block, ('groups', 'rows', 'tm'), route)  3.35 us
  transfers between devices with their start and end apart: 5, of which 5 were waited for; matrix products, arithmetic and copies ran while one was open for 0% of the time, Pallas kernels for 32%

profile of v8, /device:TPU:18, one launch (start us, length us, event | category | flops | bytes accessed | tf_op | source)
XLA Modules:
  0.0 15.2 jit_solution(11299051508658927751)
XLA Ops:
  0.0 0.0 copy-start
  0.0 0.0 copy-start.6
  0.0 0.0 copy-start.2
  0.0 0.0 copy-start.5
  0.0 0.0 copy-start.4
  0.0 0.0 copy-start.1
  0.0 0.0 copy-start.3
  0.0 0.1 collective-permute-start
  0.1 1.6 %collective-permute-start.2 = (bf16[1,4,2,96,128]{4,3,2,1,0:T(8,128)(2,1)}, bf16[1,4,2,96,128]{4,3,2,1,0:T(8,128)(2,1)S(1)}, u32[]{:S(2)}, u32[]{:S(2)}) collective-permute-start(bf16[1,4,2,96,128]{4,3,2,1,0:T(8,128)(2,1)} %video.3), channel_id=1, source_target_pairs={{0,4},{1,5},{2,6},{3,7},{4,0},{5,1},{6,2},{7,3},{8,12},{9,13},{10,... | collective-permute-start | bytes 589832 | tf_op jit(solution)/shard_map/ppermute | solution.py:241
  1.8 0.0 collective-permute-start.3
  1.8 0.0 copy-done
  1.8 0.0 copy-done.6
  1.8 0.0 copy-done.2
  1.8 0.0 copy-done.5
  1.8 0.0 copy-done.4
  1.8 0.0 copy-done.1
  1.8 0.0 copy-done.3
  1.8 0.8 %shard_map.74 = (bf16[4,2,96,128]{3,2,1,0:T(8,128)(2,1)S(1)}, f32[4,96,128]{2,1,0:T(8,128)S(1)}, bf16[288,1152]{1,0:T(8,128)(2,1)S(1)}, bf16[2,288,576]{2,1,0:T(...) custom-call(f32[3,8,128]{2,1,0:T(8,128)S(1)} %shard_map.73.valid, ...), custom_call_target="tpu_custom_call" | custom-call | flops 10000000 | bytes 1000000 | tf_op jit(solution)/shard_map/pallas_call | solution.py:286
  2.6 2.8 %collective-permute-done.prior = bf16[1,4,2,96,128]{4,3,2,1,0:T(8,128)(2,1)S(1)} collective-permute-done((bf16[1,4,2,96,128]{4,3,2,1,0:T(8,128)(2,1)}, bf16[1,4,2,96,128]{4,3,2,1,0:T(8,128)(2,1)S(1)}, u32[]{:S(2)}, u32[]{:S(2)}) %collective-permute-start) | collective-permute-done | bytes 196640 | tf_op jit(solution)/shard_map/ppermute | solution.py:241
  5.4 0.2 %shard_map.75.inner = bf16[4,2,96,128]{3,2,1,0:T(8,128)(2,1)S(1)} custom-call(f32[3,8,128]{2,1,0:T(8,128)S(1)} %shard_map.73.valid, bf16[1,4,2,96,128]{4,3,2,1,0:T(8,128)(2,1)S(1)} %collective-permute-done.prior, f32[4,96,128]{2,1,0:T(8,128)S(1)} %get-tuple-element.19.columns), custom_call_target="tpu_custom_call" | custom-call | flops 10000000 | bytes 1000000 | tf_op jit(solution)/shard_map/pallas_call | solution.py:286
  5.6 1.6 %collective-permute-start.4 = (bf16[4,2,96,128]{3,2,1,0:T(8,128)(2,1)S(1)}, bf16[4,2,96,128]{3,2,1,0:T(8,128)(2,1)S(1)}, u32[]{:S(2)}, u32[]{:S(2)}) collective-permute-start(bf16[4,2,96,128]{3,2,1,0:T(8,128)(2,1)S(1)} %shard_map.75.inner), channel_id=1, source_target_pairs={{0,16},{1,5},{2,6},{3,7},{4,20},{5,1},{6,2},{7,3},{8,24},{9,13},{1... | collective-permute-start | bytes 589832 | tf_op jit(solution)/shard_map/ppermute | solution.py:241
  7.2 0.0 collective-permute-start.1
  7.2 0.9 %collective-permute-done.2.one = bf16[1,4,2,96,128]{4,3,2,1,0:T(8,128)(2,1)S(1)} collective-permute-done((bf16[1,4,2,96,128]{4,3,2,1,0:T(8,128)(2,1)}, bf16[1,4,2,96,128]{4,3,2,1,0:T(8,128)(2,1)S(1)}, u32[]{:S(2)}, u32[]{:S(2)}) %collective-permute-start.2) | collective-permute-done | bytes 196640 | tf_op jit(solution)/shard_map/ppermute | solution.py:241
  8.1 1.0 %shard_map.76 = (f32[2,2,96,128]{3,2,1,0:T(8,128)S(1)}, bf16[2,2,96,128]{3,2,1,0:T(8,128)(2,1)S(1)}) custom-call(f32[3,8,128]{2,1,0:T(8,128)S(1)} %shard_map.73.valid, bf16[1,4,2,96,128]{4,3,2,1,0:T(8,128)(2,1)S(1)} %collective-permute-done.2.one, bf16[4,2,96,128]{3,2,1,0:T(8,128)(2,1)S(1)} %get-tuple-element.24.own, ...), custom_call_target="tpu_custom_call" | custom-call | flops 10000000 | bytes 1000000 | tf_op jit(solution)/shard_map/pallas_call | solution.py:286
  9.1 0.6 %collective-permute-done.3.two = bf16[1,4,2,96,128]{4,3,2,1,0:T(8,128)(2,1)S(1)} collective-permute-done((bf16[1,4,2,96,128]{4,3,2,1,0:T(8,128)(2,1)}, bf16[1,4,2,96,128]{4,3,2,1,0:T(8,128)(2,1)S(1)}, u32[]{:S(2)}, u32[]{:S(2)}) %collective-permute-start.3) | collective-permute-done | bytes 196640 | tf_op jit(solution)/shard_map/ppermute | solution.py:241
  9.7 1.7 %shard_map.77 = (f32[4,2,96,128]{3,2,1,0:T(8,128)S(1)}, f32[4,2,96,128]{3,2,1,0:T(8,128)S(1)}, f32[2,2,96,128]{3,2,1,0:T(8,128)S(1)}) custom-call(f32[2,2,96,128]{3,2,1,0:T(8,128)S(1)} %get-tuple-element.26.partial_one, bf16[2,2,96,128]{3,2,1,0:T(8,128)(2,1)S(1)} %get-tuple-element.27.late_one, f32[3,8,128]{2,1,0:T(8,128)S(1)} %shard_map.73.valid, ...), custom_call_target="tpu_custom_call" | custom-call | flops 10000000 | bytes 1000000 | tf_op jit(solution)/shard_map/pallas_call | solution.py:286
  11.4 0.6 %collective-permute-done.4.near = bf16[4,2,96,128]{3,2,1,0:T(8,128)(2,1)S(1)} collective-permute-done((bf16[4,2,96,128]{3,2,1,0:T(8,128)(2,1)S(1)}, bf16[4,2,96,128]{3,2,1,0:T(8,128)(2,1)S(1)}, u32[]{:S(2)}, u32[]{:S(2)}) %collective-permute-start.4) | collective-permute-done | bytes 196640 | tf_op jit(solution)/shard_map/ppermute | solution.py:241
  12.0 1.1 %shard_map.78.sums = f32[4,2,96,128]{3,2,1,0:T(8,128)S(1)} custom-call(f32[3,8,128]{2,1,0:T(8,128)S(1)} %shard_map.73.valid, bf16[1,4,2,96,128]{4,3,2,1,0:T(8,128)(2,1)S(1)} %copy-done, bf16[4,2,96,128]{3,2,1,0:T(8,128)(2,1)S(1)} %collective-permute-done.4.near, bf16[2,288,576]{2,1,0:T(8,128)(2,1)S(1)} %get-tuple-element.20.double, ...), custom_call_target="tpu_custom_call" | custom-call | flops 1000000000 | bytes 1000000 | tf_op jit(solution)/shard_map/pallas_call | solution.py:286
  13.1 0.1 collective-permute-done.1.near
  13.3 1.9 %shard_map.79 = bf16[1,4,2,96,128]{4,3,2,1,0:T(8,128)(2,1)} custom-call(f32[3,8,128]{2,1,0:T(8,128)S(1)} %shard_map.73.valid, bf16[4,2,96,128]{3,2,1,0:T(8,128)(2,1)S(1)} %collective-permute-done.1.near, bf16[2,288,576]{2,1,0:T(8,128)(2,1)S(1)} %get-tuple-element.20.double, bf16[2,288,288]{2,1,0:T(8,128)(2,1)S(1)} %get-tuple-element.21.single, ...), custom_call_target="tpu_custom_call" | custom-call | flops 1000000000 | bytes 1000000 | tf_op jit(solution)/shard_map/pallas_call | solution.py:286
  (1 shorter events, 0.0 us)
Async XLA Ops:
  0.0 1.8 %copy-start = (bf16[1,4,2,96,128]{4,3,2,1,0:T(8,128)(2,1)S(1)}, bf16[1,4,2,96,128]{4,3,2,1,0:T(8,128)(2,1)}, u32[]{:S(2)}) copy-start(bf16[1,4,2,96,128]{4,3,2,1,0:T(8,128)(2,1)} %video.3) | copy-start | bytes 589828
  0.0 1.8 %copy-start.6 = (f32[96]{0:T(128)S(1)}, f32[96]{0:T(128)}, u32[]{:S(2)}) copy-start(f32[96]{0:T(128)} %bias_second.1) | copy-start | bytes 1156
  0.0 1.8 %copy-start.2 = (bf16[96,2592]{1,0:T(8,128)(2,1)S(1)}, bf16[96,2592]{1,0:T(8,128)(2,1)}, u32[]{:S(2)}) copy-start(bf16[96,2592]{1,0:T(8,128)(2,1)} %kernel_second.1) | copy-start | bytes 1492996
  0.0 1.8 %copy-start.5 = (f32[96]{0:T(128)S(1)}, f32[96]{0:T(128)}, u32[]{:S(2)}) copy-start(f32[96]{0:T(128)} %gamma_second.1) | copy-start | bytes 1156
  0.0 1.8 %copy-start.4 = (f32[96]{0:T(128)S(1)}, f32[96]{0:T(128)}, u32[]{:S(2)}) copy-start(f32[96]{0:T(128)} %bias_first.1) | copy-start | bytes 1156
  0.0 1.8 %copy-start.1 = (bf16[96,2592]{1,0:T(8,128)(2,1)S(1)}, bf16[96,2592]{1,0:T(8,128)(2,1)}, u32[]{:S(2)}) copy-start(bf16[96,2592]{1,0:T(8,128)(2,1)} %kernel_first.1) | copy-start | bytes 1492996
  0.0 1.8 %copy-start.3 = (f32[96]{0:T(128)S(1)}, f32[96]{0:T(128)}, u32[]{:S(2)}) copy-start(f32[96]{0:T(128)} %gamma_first.1) | copy-start | bytes 1156
  0.0 5.4 %collective-permute-start = (bf16[1,4,2,96,128]{4,3,2,1,0:T(8,128)(2,1)}, bf16[1,4,2,96,128]{4,3,2,1,0:T(8,128)(2,1)S(1)}, u32[]{:S(2)}, u32[]{:S(2)}) collective-permute-start(bf16[1,4,2,96,128]{4,3,2,1,0:T(8,128)(2,1)} %video.3), channel_id=1, source_target_pairs={{0,1},{1,2},{2,3},{3,0},{4,5},{5,6},{6,7},{7,4},{8,9},{9,10},{10,1... | collective-permute-start | bytes 589832 | tf_op jit(solution)/shard_map/ppermute | solution.py:241
  0.1 8.0 %collective-permute-start.2 = (bf16[1,4,2,96,128]{4,3,2,1,0:T(8,128)(2,1)}, bf16[1,4,2,96,128]{4,3,2,1,0:T(8,128)(2,1)S(1)}, u32[]{:S(2)}, u32[]{:S(2)}) collective-permute-start(bf16[1,4,2,96,128]{4,3,2,1,0:T(8,128)(2,1)} %video.3), channel_id=1, source_target_pairs={{0,4},{1,5},{2,6},{3,7},{4,0},{5,1},{6,2},{7,3},{8,12},{9,13},{10,... | collective-permute-start | bytes 589832 | tf_op jit(solution)/shard_map/ppermute | solution.py:241
  1.8 7.9 %collective-permute-start.3 = (bf16[1,4,2,96,128]{4,3,2,1,0:T(8,128)(2,1)}, bf16[1,4,2,96,128]{4,3,2,1,0:T(8,128)(2,1)S(1)}, u32[]{:S(2)}, u32[]{:S(2)}) collective-permute-start(bf16[1,4,2,96,128]{4,3,2,1,0:T(8,128)(2,1)} %video.3), channel_id=1, source_target_pairs={{0,1},{1,0},{2,3},{3,2},{4,8},{5,9},{6,10},{7,11},{8,4},{9,5},{10,... | collective-permute-start | bytes 589832 | tf_op jit(solution)/shard_map/ppermute | solution.py:241
  5.6 6.4 %collective-permute-start.4 = (bf16[4,2,96,128]{3,2,1,0:T(8,128)(2,1)S(1)}, bf16[4,2,96,128]{3,2,1,0:T(8,128)(2,1)S(1)}, u32[]{:S(2)}, u32[]{:S(2)}) collective-permute-start(bf16[4,2,96,128]{3,2,1,0:T(8,128)(2,1)S(1)} %shard_map.75.inner), channel_id=1, source_target_pairs={{0,16},{1,5},{2,6},{3,7},{4,20},{5,1},{6,2},{7,3},{8,24},{9,13},{1... | collective-permute-start | bytes 589832 | tf_op jit(solution)/shard_map/ppermute | solution.py:241
  7.2 6.1 %collective-permute-start.1 = (bf16[4,2,96,128]{3,2,1,0:T(8,128)(2,1)S(1)}, bf16[4,2,96,128]{3,2,1,0:T(8,128)(2,1)S(1)}, u32[]{:S(2)}, u32[]{:S(2)}) collective-permute-start(bf16[4,2,96,128]{3,2,1,0:T(8,128)(2,1)S(1)} %shard_map.75.inner), channel_id=1, source_target_pairs={{0,1},{1,0},{2,3},{3,2},{4,20},{5,9},{6,10},{7,11},{8,24},{9,5},{1... | collective-permute-start | bytes 589832 | tf_op jit(solution)/shard_map/ppermute | solution.py:241

commit v9 on v8

--- a/solution.py
+++ b/solution.py
@@ -208,7 +208,7 @@
 
 
 def last_kernel(
-    valid, near, double, single, second_double, second_single, columns, rest, sums, encoded, early, near_sums
+    valid, near, double, single, second_double, second_single, columns, rest, sums, encoded, early, near_sums, ready, sems
 ):
     side = 1 - side_of_one()
     has_earlier = lax.axis_index("tm") > 0
@@ -224,14 +224,20 @@
     def _():
         near_sums[...] = jnp.zeros_like(near_sums)
 
-    result = []
+    moves = []
     for group, count in (LAST, FIRST):
         parts = [(frame, near_sums[frame, 0], near_sums[frame, 1]) for frame in group]
         earlier_frames(parts, side, rest, valid[1, 0:1], valid[2, 0:1], columns[2], early)
-        result += earlier_sums(second_double.at[side], second_single.at[side], early, 1 - side, group, count)
-    for frame, both, alone in result:
-        for value, row in ((both, side), (alone, 1 - side)):
-            encoded[0, frame, row] = (sums[frame, row] + value).astype(jnp.bfloat16)
+        result = earlier_sums(second_double.at[side], second_single.at[side], early, 1 - side, group, count)
+        for frame, both, alone in result:
+            for value, row in ((both, side), (alone, 1 - side)):
+                ready[0, frame, row] = (sums[frame, row] + value).astype(jnp.bfloat16)
+        chosen = (0, slice(group[0], group[-1] + 1))
+        move = pltpu.make_async_copy(ready.at[chosen], encoded.at[chosen], sems.at[len(moves)])
+        move.start()
+        moves.append(move)
+    for move in moves:
+        move.wait()
 
 
 def routed(block, goal):
@@ -281,14 +287,14 @@
     shape = jax.ShapeDtypeStruct
     params = pltpu.CompilerParams(vmem_limit_bytes=24 * 2**20)
 
-    def run(kernel, out_shape, operands, scratch=(), millions=1000):
+    def run(kernel, out_shape, operands, scratch=(), millions=1000, out_spec=VMEM, sems=()):
         single_out = not isinstance(out_shape, tuple)
         return pl.pallas_call(
             kernel,
             out_shape=out_shape,
             in_specs=[VMEM] * len(operands),
-            out_specs=VMEM if single_out else [VMEM] * len(out_shape),
-            scratch_shapes=[pltpu.VMEM(*one_scratch) for one_scratch in scratch],
+            out_specs=out_spec if single_out else [VMEM] * len(out_shape),
+            scratch_shapes=[pltpu.VMEM(*one_scratch) for one_scratch in scratch] + list(sems),
             compiler_params=params,
             cost_estimate=pl.CostEstimate(flops=millions * 10**6, bytes_accessed=10**6, transcendentals=10**5),
         )(*operands)
@@ -336,8 +342,10 @@
         last_kernel,
         shape(video.shape, bf16),
         (valid, prior_two, double, single, second_double, second_single, columns, rest_two, sums),
-        ((early.shape, bf16), (rest.shape, f32)),
+        ((early.shape, bf16), (rest.shape, f32), (video.shape, bf16)),
         1000,
+        pl.BlockSpec(memory_space=pl.ANY),
+        [pltpu.SemaphoreType.DMA((2,))],
     )
 
 

time: 15.4 us -> 15.3 us (level)
  no operation moved by 1% of the time
where the time goes in v9:
time: 15.3 us; the launch traced here: 15.2 us
  Pallas kernels  6.78 us (44%)
  waiting for transfers between devices  4.92 us (32%)
  starting transfers between devices  3.35 us (22%)
    pallas_call x7, Pallas kernels, run(): pl.pallas_call(kernel, out_shape=out_shape, in_specs=[VMEM] * len(operand...  6.78 us
    ppermute x5, waiting for transfers between devices, routed(): return lax.ppermute(block, ('groups', 'rows', 'tm'), route)  4.92 us
    ppermute x5, starting transfers between devices, routed(): return lax.ppermute(block, ('groups', 'rows', 'tm'), route)  3.35 us
  transfers between devices with their start and end apart: 5, of which 5 were waited for; matrix products, arithmetic and copies ran while one was open for 0% of the time, Pallas kernels for 32%

profile of v9, /device:TPU:18, one launch (start us, length us, event | category | flops | bytes accessed | tf_op | source)
XLA Modules:
  0.0 15.2 jit_solution(1619563904827743463)
XLA Ops:
  0.0 0.0 copy-start
  0.0 0.0 copy-start.6
  0.0 0.0 copy-start.2
  0.0 0.0 copy-start.5
  0.0 0.0 copy-start.4
  0.0 0.0 copy-start.1
  0.0 0.0 copy-start.3
  0.0 0.1 collective-permute-start
  0.1 1.6 %collective-permute-start.2 = (bf16[1,4,2,96,128]{4,3,2,1,0:T(8,128)(2,1)}, bf16[1,4,2,96,128]{4,3,2,1,0:T(8,128)(2,1)S(1)}, u32[]{:S(2)}, u32[]{:S(2)}) collective-permute-start(bf16[1,4,2,96,128]{4,3,2,1,0:T(8,128)(2,1)} %video.3), channel_id=1, source_target_pairs={{0,4},{1,5},{2,6},{3,7},{4,0},{5,1},{6,2},{7,3},{8,12},{9,13},{10,... | collective-permute-start | bytes 589832 | tf_op jit(solution)/shard_map/ppermute | solution.py:247
  1.8 0.0 collective-permute-start.3
  1.8 0.0 copy-done
  1.8 0.0 copy-done.6
  1.8 0.0 copy-done.2
  1.8 0.0 copy-done.5
  1.8 0.0 copy-done.4
  1.8 0.0 copy-done.1
  1.8 0.0 copy-done.3
  1.8 0.8 %shard_map.74 = (bf16[4,2,96,128]{3,2,1,0:T(8,128)(2,1)S(1)}, f32[4,96,128]{2,1,0:T(8,128)S(1)}, bf16[288,1152]{1,0:T(8,128)(2,1)S(1)}, bf16[2,288,576]{2,1,0:T(...) custom-call(f32[3,8,128]{2,1,0:T(8,128)S(1)} %shard_map.73.valid, ...), custom_call_target="tpu_custom_call" | custom-call | flops 10000000 | bytes 1000000 | tf_op jit(solution)/shard_map/pallas_call | solution.py:292
  2.6 2.8 %collective-permute-done.prior = bf16[1,4,2,96,128]{4,3,2,1,0:T(8,128)(2,1)S(1)} collective-permute-done((bf16[1,4,2,96,128]{4,3,2,1,0:T(8,128)(2,1)}, bf16[1,4,2,96,128]{4,3,2,1,0:T(8,128)(2,1)S(1)}, u32[]{:S(2)}, u32[]{:S(2)}) %collective-permute-start) | collective-permute-done | bytes 196640 | tf_op jit(solution)/shard_map/ppermute | solution.py:247
  5.4 0.2 %shard_map.75.inner = bf16[4,2,96,128]{3,2,1,0:T(8,128)(2,1)S(1)} custom-call(f32[3,8,128]{2,1,0:T(8,128)S(1)} %shard_map.73.valid, bf16[1,4,2,96,128]{4,3,2,1,0:T(8,128)(2,1)S(1)} %collective-permute-done.prior, f32[4,96,128]{2,1,0:T(8,128)S(1)} %get-tuple-element.19.columns), custom_call_target="tpu_custom_call" | custom-call | flops 10000000 | bytes 1000000 | tf_op jit(solution)/shard_map/pallas_call | solution.py:292
  5.6 1.6 %collective-permute-start.4 = (bf16[4,2,96,128]{3,2,1,0:T(8,128)(2,1)S(1)}, bf16[4,2,96,128]{3,2,1,0:T(8,128)(2,1)S(1)}, u32[]{:S(2)}, u32[]{:S(2)}) collective-permute-start(bf16[4,2,96,128]{3,2,1,0:T(8,128)(2,1)S(1)} %shard_map.75.inner), channel_id=1, source_target_pairs={{0,16},{1,5},{2,6},{3,7},{4,20},{5,1},{6,2},{7,3},{8,24},{9,13},{1... | collective-permute-start | bytes 589832 | tf_op jit(solution)/shard_map/ppermute | solution.py:247
  7.2 0.0 collective-permute-start.1
  7.2 0.9 %collective-permute-done.2.one = bf16[1,4,2,96,128]{4,3,2,1,0:T(8,128)(2,1)S(1)} collective-permute-done((bf16[1,4,2,96,128]{4,3,2,1,0:T(8,128)(2,1)}, bf16[1,4,2,96,128]{4,3,2,1,0:T(8,128)(2,1)S(1)}, u32[]{:S(2)}, u32[]{:S(2)}) %collective-permute-start.2) | collective-permute-done | bytes 196640 | tf_op jit(solution)/shard_map/ppermute | solution.py:247
  8.1 1.0 %shard_map.76 = (f32[2,2,96,128]{3,2,1,0:T(8,128)S(1)}, bf16[2,2,96,128]{3,2,1,0:T(8,128)(2,1)S(1)}) custom-call(f32[3,8,128]{2,1,0:T(8,128)S(1)} %shard_map.73.valid, bf16[1,4,2,96,128]{4,3,2,1,0:T(8,128)(2,1)S(1)} %collective-permute-done.2.one, bf16[4,2,96,128]{3,2,1,0:T(8,128)(2,1)S(1)} %get-tuple-element.24.own, ...), custom_call_target="tpu_custom_call" | custom-call | flops 10000000 | bytes 1000000 | tf_op jit(solution)/shard_map/pallas_call | solution.py:292
  9.1 0.6 %collective-permute-done.3.two = bf16[1,4,2,96,128]{4,3,2,1,0:T(8,128)(2,1)S(1)} collective-permute-done((bf16[1,4,2,96,128]{4,3,2,1,0:T(8,128)(2,1)}, bf16[1,4,2,96,128]{4,3,2,1,0:T(8,128)(2,1)S(1)}, u32[]{:S(2)}, u32[]{:S(2)}) %collective-permute-start.3) | collective-permute-done | bytes 196640 | tf_op jit(solution)/shard_map/ppermute | solution.py:247
  9.7 1.7 %shard_map.77 = (f32[4,2,96,128]{3,2,1,0:T(8,128)S(1)}, f32[4,2,96,128]{3,2,1,0:T(8,128)S(1)}, f32[2,2,96,128]{3,2,1,0:T(8,128)S(1)}) custom-call(f32[2,2,96,128]{3,2,1,0:T(8,128)S(1)} %get-tuple-element.26.partial_one, bf16[2,2,96,128]{3,2,1,0:T(8,128)(2,1)S(1)} %get-tuple-element.27.late_one, f32[3,8,128]{2,1,0:T(8,128)S(1)} %shard_map.73.valid, ...), custom_call_target="tpu_custom_call" | custom-call | flops 10000000 | bytes 1000000 | tf_op jit(solution)/shard_map/pallas_call | solution.py:292
  11.4 0.6 %collective-permute-done.4.near = bf16[4,2,96,128]{3,2,1,0:T(8,128)(2,1)S(1)} collective-permute-done((bf16[4,2,96,128]{3,2,1,0:T(8,128)(2,1)S(1)}, bf16[4,2,96,128]{3,2,1,0:T(8,128)(2,1)S(1)}, u32[]{:S(2)}, u32[]{:S(2)}) %collective-permute-start.4) | collective-permute-done | bytes 196640 | tf_op jit(solution)/shard_map/ppermute | solution.py:247
  12.0 1.1 %shard_map.78.sums = f32[4,2,96,128]{3,2,1,0:T(8,128)S(1)} custom-call(f32[3,8,128]{2,1,0:T(8,128)S(1)} %shard_map.73.valid, bf16[1,4,2,96,128]{4,3,2,1,0:T(8,128)(2,1)S(1)} %copy-done, bf16[4,2,96,128]{3,2,1,0:T(8,128)(2,1)S(1)} %collective-permute-done.4.near, bf16[2,288,576]{2,1,0:T(8,128)(2,1)S(1)} %get-tuple-element.20.double, ...), custom_call_target="tpu_custom_call" | custom-call | flops 1000000000 | bytes 1000000 | tf_op jit(solution)/shard_map/pallas_call | solution.py:292
  13.1 0.1 collective-permute-done.1.near
  13.3 1.9 %shard_map.79 = bf16[1,4,2,96,128]{4,3,2,1,0:T(8,128)(2,1)} custom-call(f32[3,8,128]{2,1,0:T(8,128)S(1)} %shard_map.73.valid, bf16[4,2,96,128]{3,2,1,0:T(8,128)(2,1)S(1)} %collective-permute-done.1.near, bf16[2,288,576]{2,1,0:T(8,128)(2,1)S(1)} %get-tuple-element.20.double, bf16[2,288,288]{2,1,0:T(8,128)(2,1)S(1)} %get-tuple-element.21.single, ...), custom_call_target="tpu_custom_call" | custom-call | flops 1000000000 | bytes 1000000 | tf_op jit(solution)/shard_map/pallas_call | solution.py:292
  (1 shorter events, 0.0 us)
Async XLA Ops:
  0.0 1.8 %copy-start = (bf16[1,4,2,96,128]{4,3,2,1,0:T(8,128)(2,1)S(1)}, bf16[1,4,2,96,128]{4,3,2,1,0:T(8,128)(2,1)}, u32[]{:S(2)}) copy-start(bf16[1,4,2,96,128]{4,3,2,1,0:T(8,128)(2,1)} %video.3) | copy-start | bytes 589828
  0.0 1.8 %copy-start.6 = (f32[96]{0:T(128)S(1)}, f32[96]{0:T(128)}, u32[]{:S(2)}) copy-start(f32[96]{0:T(128)} %bias_second.1) | copy-start | bytes 1156
  0.0 1.8 %copy-start.2 = (bf16[96,2592]{1,0:T(8,128)(2,1)S(1)}, bf16[96,2592]{1,0:T(8,128)(2,1)}, u32[]{:S(2)}) copy-start(bf16[96,2592]{1,0:T(8,128)(2,1)} %kernel_second.1) | copy-start | bytes 1492996
  0.0 1.8 %copy-start.5 = (f32[96]{0:T(128)S(1)}, f32[96]{0:T(128)}, u32[]{:S(2)}) copy-start(f32[96]{0:T(128)} %gamma_second.1) | copy-start | bytes 1156
  0.0 1.8 %copy-start.4 = (f32[96]{0:T(128)S(1)}, f32[96]{0:T(128)}, u32[]{:S(2)}) copy-start(f32[96]{0:T(128)} %bias_first.1) | copy-start | bytes 1156
  0.0 1.8 %copy-start.1 = (bf16[96,2592]{1,0:T(8,128)(2,1)S(1)}, bf16[96,2592]{1,0:T(8,128)(2,1)}, u32[]{:S(2)}) copy-start(bf16[96,2592]{1,0:T(8,128)(2,1)} %kernel_first.1) | copy-start | bytes 1492996
  0.0 1.8 %copy-start.3 = (f32[96]{0:T(128)S(1)}, f32[96]{0:T(128)}, u32[]{:S(2)}) copy-start(f32[96]{0:T(128)} %gamma_first.1) | copy-start | bytes 1156
  0.0 5.4 %collective-permute-start = (bf16[1,4,2,96,128]{4,3,2,1,0:T(8,128)(2,1)}, bf16[1,4,2,96,128]{4,3,2,1,0:T(8,128)(2,1)S(1)}, u32[]{:S(2)}, u32[]{:S(2)}) collective-permute-start(bf16[1,4,2,96,128]{4,3,2,1,0:T(8,128)(2,1)} %video.3), channel_id=1, source_target_pairs={{0,1},{1,2},{2,3},{3,0},{4,5},{5,6},{6,7},{7,4},{8,9},{9,10},{10,1... | collective-permute-start | bytes 589832 | tf_op jit(solution)/shard_map/ppermute | solution.py:247
  0.1 8.0 %collective-permute-start.2 = (bf16[1,4,2,96,128]{4,3,2,1,0:T(8,128)(2,1)}, bf16[1,4,2,96,128]{4,3,2,1,0:T(8,128)(2,1)S(1)}, u32[]{:S(2)}, u32[]{:S(2)}) collective-permute-start(bf16[1,4,2,96,128]{4,3,2,1,0:T(8,128)(2,1)} %video.3), channel_id=1, source_target_pairs={{0,4},{1,5},{2,6},{3,7},{4,0},{5,1},{6,2},{7,3},{8,12},{9,13},{10,... | collective-permute-start | bytes 589832 | tf_op jit(solution)/shard_map/ppermute | solution.py:247
  1.8 7.9 %collective-permute-start.3 = (bf16[1,4,2,96,128]{4,3,2,1,0:T(8,128)(2,1)}, bf16[1,4,2,96,128]{4,3,2,1,0:T(8,128)(2,1)S(1)}, u32[]{:S(2)}, u32[]{:S(2)}) collective-permute-start(bf16[1,4,2,96,128]{4,3,2,1,0:T(8,128)(2,1)} %video.3), channel_id=1, source_target_pairs={{0,1},{1,0},{2,3},{3,2},{4,8},{5,9},{6,10},{7,11},{8,4},{9,5},{10,... | collective-permute-start | bytes 589832 | tf_op jit(solution)/shard_map/ppermute | solution.py:247
  5.6 6.4 %collective-permute-start.4 = (bf16[4,2,96,128]{3,2,1,0:T(8,128)(2,1)S(1)}, bf16[4,2,96,128]{3,2,1,0:T(8,128)(2,1)S(1)}, u32[]{:S(2)}, u32[]{:S(2)}) collective-permute-start(bf16[4,2,96,128]{3,2,1,0:T(8,128)(2,1)S(1)} %shard_map.75.inner), channel_id=1, source_target_pairs={{0,16},{1,5},{2,6},{3,7},{4,20},{5,1},{6,2},{7,3},{8,24},{9,13},{1... | collective-permute-start | bytes 589832 | tf_op jit(solution)/shard_map/ppermute | solution.py:247
  7.2 6.1 %collective-permute-start.1 = (bf16[4,2,96,128]{3,2,1,0:T(8,128)(2,1)S(1)}, bf16[4,2,96,128]{3,2,1,0:T(8,128)(2,1)S(1)}, u32[]{:S(2)}, u32[]{:S(2)}) collective-permute-start(bf16[4,2,96,128]{3,2,1,0:T(8,128)(2,1)S(1)} %shard_map.75.inner), channel_id=1, source_target_pairs={{0,1},{1,0},{2,3},{3,2},{4,20},{5,9},{6,10},{7,11},{8,24},{9,5},{1... | collective-permute-start | bytes 589832 | tf_op jit(solution)/shard_map/ppermute | solution.py:247

commit v10 on v9

--- a/solution.py
+++ b/solution.py
@@ -211,7 +211,9 @@
     valid, near, double, single, second_double, second_single, columns, rest, sums, encoded, early, near_sums, ready, sems
 ):
     side = 1 - side_of_one()
-    has_earlier = lax.axis_index("tm") > 0
+    row_part, row_parts = lax.axis_index("rows"), lax.axis_size("rows")
+    has_two = (row_part > 0) & ((row_part < row_parts - 1) | (row_parts % 2 == 1))
+    has_earlier = (lax.axis_index("tm") > 0) & has_two
 
     @pl.when(has_earlier)
     def _():

time: 15.3 us -> 15.3 us (level)
  no operation moved by 1% of the time
where the time goes in v10:
time: 15.3 us; the launch traced here: 15.2 us
  Pallas kernels  6.78 us (44%)
  waiting for transfers between devices  4.92 us (32%)
  starting transfers between devices  3.35 us (22%)
    pallas_call x7, Pallas kernels, run(): pl.pallas_call(kernel, out_shape=out_shape, in_specs=[VMEM] * len(operand...  6.78 us
    ppermute x5, waiting for transfers between devices, routed(): return lax.ppermute(block, ('groups', 'rows', 'tm'), route)  4.92 us
    ppermute x5, starting transfers between devices, routed(): return lax.ppermute(block, ('groups', 'rows', 'tm'), route)  3.35 us
  transfers between devices with their start and end apart: 5, of which 5 were waited for; matrix products, arithmetic and copies ran while one was open for 0% of the time, Pallas kernels for 32%

profile of v10, /device:TPU:18, one launch (start us, length us, event | category | flops | bytes accessed | tf_op | source)
XLA Modules:
  0.0 15.2 jit_solution(15242880430527281628)
XLA Ops:
  0.0 0.0 copy-start
  0.0 0.0 copy-start.6
  0.0 0.0 copy-start.2
  0.0 0.0 copy-start.5
  0.0 0.0 copy-start.4
  0.0 0.0 copy-start.1
  0.0 0.0 copy-start.3
  0.0 0.1 collective-permute-start
  0.1 1.6 %collective-permute-start.2 = (bf16[1,4,2,96,128]{4,3,2,1,0:T(8,128)(2,1)}, bf16[1,4,2,96,128]{4,3,2,1,0:T(8,128)(2,1)S(1)}, u32[]{:S(2)}, u32[]{:S(2)}) collective-permute-start(bf16[1,4,2,96,128]{4,3,2,1,0:T(8,128)(2,1)} %video.3), channel_id=1, source_target_pairs={{0,4},{1,5},{2,6},{3,7},{4,0},{5,1},{6,2},{7,3},{8,12},{9,13},{10,... | collective-permute-start | bytes 589832 | tf_op jit(solution)/shard_map/ppermute | solution.py:249
  1.8 0.0 collective-permute-start.3
  1.8 0.0 copy-done
  1.8 0.0 copy-done.6
  1.8 0.0 copy-done.2
  1.8 0.0 copy-done.5
  1.8 0.0 copy-done.4
  1.8 0.0 copy-done.1
  1.8 0.0 copy-done.3
  1.8 0.8 %shard_map.74 = (bf16[4,2,96,128]{3,2,1,0:T(8,128)(2,1)S(1)}, f32[4,96,128]{2,1,0:T(8,128)S(1)}, bf16[288,1152]{1,0:T(8,128)(2,1)S(1)}, bf16[2,288,576]{2,1,0:T(...) custom-call(f32[3,8,128]{2,1,0:T(8,128)S(1)} %shard_map.73.valid, ...), custom_call_target="tpu_custom_call" | custom-call | flops 10000000 | bytes 1000000 | tf_op jit(solution)/shard_map/pallas_call | solution.py:294
  2.6 2.8 %collective-permute-done.prior = bf16[1,4,2,96,128]{4,3,2,1,0:T(8,128)(2,1)S(1)} collective-permute-done((bf16[1,4,2,96,128]{4,3,2,1,0:T(8,128)(2,1)}, bf16[1,4,2,96,128]{4,3,2,1,0:T(8,128)(2,1)S(1)}, u32[]{:S(2)}, u32[]{:S(2)}) %collective-permute-start) | collective-permute-done | bytes 196640 | tf_op jit(solution)/shard_map/ppermute | solution.py:249
  5.4 0.2 %shard_map.75.inner = bf16[4,2,96,128]{3,2,1,0:T(8,128)(2,1)S(1)} custom-call(f32[3,8,128]{2,1,0:T(8,128)S(1)} %shard_map.73.valid, bf16[1,4,2,96,128]{4,3,2,1,0:T(8,128)(2,1)S(1)} %collective-permute-done.prior, f32[4,96,128]{2,1,0:T(8,128)S(1)} %get-tuple-element.19.columns), custom_call_target="tpu_custom_call" | custom-call | flops 10000000 | bytes 1000000 | tf_op jit(solution)/shard_map/pallas_call | solution.py:294
  5.6 1.6 %collective-permute-start.4 = (bf16[4,2,96,128]{3,2,1,0:T(8,128)(2,1)S(1)}, bf16[4,2,96,128]{3,2,1,0:T(8,128)(2,1)S(1)}, u32[]{:S(2)}, u32[]{:S(2)}) collective-permute-start(bf16[4,2,96,128]{3,2,1,0:T(8,128)(2,1)S(1)} %shard_map.75.inner), channel_id=1, source_target_pairs={{0,16},{1,5},{2,6},{3,7},{4,20},{5,1},{6,2},{7,3},{8,24},{9,13},{1... | collective-permute-start | bytes 589832 | tf_op jit(solution)/shard_map/ppermute | solution.py:249
  7.2 0.0 collective-permute-start.1
  7.2 0.9 %collective-permute-done.2.one = bf16[1,4,2,96,128]{4,3,2,1,0:T(8,128)(2,1)S(1)} collective-permute-done((bf16[1,4,2,96,128]{4,3,2,1,0:T(8,128)(2,1)}, bf16[1,4,2,96,128]{4,3,2,1,0:T(8,128)(2,1)S(1)}, u32[]{:S(2)}, u32[]{:S(2)}) %collective-permute-start.2) | collective-permute-done | bytes 196640 | tf_op jit(solution)/shard_map/ppermute | solution.py:249
  8.1 1.0 %shard_map.76 = (f32[2,2,96,128]{3,2,1,0:T(8,128)S(1)}, bf16[2,2,96,128]{3,2,1,0:T(8,128)(2,1)S(1)}) custom-call(f32[3,8,128]{2,1,0:T(8,128)S(1)} %shard_map.73.valid, bf16[1,4,2,96,128]{4,3,2,1,0:T(8,128)(2,1)S(1)} %collective-permute-done.2.one, bf16[4,2,96,128]{3,2,1,0:T(8,128)(2,1)S(1)} %get-tuple-element.24.own, ...), custom_call_target="tpu_custom_call" | custom-call | flops 10000000 | bytes 1000000 | tf_op jit(solution)/shard_map/pallas_call | solution.py:294
  9.1 0.6 %collective-permute-done.3.two = bf16[1,4,2,96,128]{4,3,2,1,0:T(8,128)(2,1)S(1)} collective-permute-done((bf16[1,4,2,96,128]{4,3,2,1,0:T(8,128)(2,1)}, bf16[1,4,2,96,128]{4,3,2,1,0:T(8,128)(2,1)S(1)}, u32[]{:S(2)}, u32[]{:S(2)}) %collective-permute-start.3) | collective-permute-done | bytes 196640 | tf_op jit(solution)/shard_map/ppermute | solution.py:249
  9.7 1.7 %shard_map.77 = (f32[4,2,96,128]{3,2,1,0:T(8,128)S(1)}, f32[4,2,96,128]{3,2,1,0:T(8,128)S(1)}, f32[2,2,96,128]{3,2,1,0:T(8,128)S(1)}) custom-call(f32[2,2,96,128]{3,2,1,0:T(8,128)S(1)} %get-tuple-element.26.partial_one, bf16[2,2,96,128]{3,2,1,0:T(8,128)(2,1)S(1)} %get-tuple-element.27.late_one, f32[3,8,128]{2,1,0:T(8,128)S(1)} %shard_map.73.valid, ...), custom_call_target="tpu_custom_call" | custom-call | flops 10000000 | bytes 1000000 | tf_op jit(solution)/shard_map/pallas_call | solution.py:294
  11.4 0.6 %collective-permute-done.4.near = bf16[4,2,96,128]{3,2,1,0:T(8,128)(2,1)S(1)} collective-permute-done((bf16[4,2,96,128]{3,2,1,0:T(8,128)(2,1)S(1)}, bf16[4,2,96,128]{3,2,1,0:T(8,128)(2,1)S(1)}, u32[]{:S(2)}, u32[]{:S(2)}) %collective-permute-start.4) | collective-permute-done | bytes 196640 | tf_op jit(solution)/shard_map/ppermute | solution.py:249
  12.0 1.1 %shard_map.78.sums = f32[4,2,96,128]{3,2,1,0:T(8,128)S(1)} custom-call(f32[3,8,128]{2,1,0:T(8,128)S(1)} %shard_map.73.valid, bf16[1,4,2,96,128]{4,3,2,1,0:T(8,128)(2,1)S(1)} %copy-done, bf16[4,2,96,128]{3,2,1,0:T(8,128)(2,1)S(1)} %collective-permute-done.4.near, bf16[2,288,576]{2,1,0:T(8,128)(2,1)S(1)} %get-tuple-element.20.double, ...), custom_call_target="tpu_custom_call" | custom-call | flops 1000000000 | bytes 1000000 | tf_op jit(solution)/shard_map/pallas_call | solution.py:294
  13.1 0.1 collective-permute-done.1.near
  13.3 1.9 %shard_map.79 = bf16[1,4,2,96,128]{4,3,2,1,0:T(8,128)(2,1)} custom-call(f32[3,8,128]{2,1,0:T(8,128)S(1)} %shard_map.73.valid, bf16[4,2,96,128]{3,2,1,0:T(8,128)(2,1)S(1)} %collective-permute-done.1.near, bf16[2,288,576]{2,1,0:T(8,128)(2,1)S(1)} %get-tuple-element.20.double, bf16[2,288,288]{2,1,0:T(8,128)(2,1)S(1)} %get-tuple-element.21.single, ...), custom_call_target="tpu_custom_call" | custom-call | flops 1000000000 | bytes 1000000 | tf_op jit(solution)/shard_map/pallas_call | solution.py:294
  (1 shorter events, 0.0 us)
Async XLA Ops:
  0.0 1.8 %copy-start = (bf16[1,4,2,96,128]{4,3,2,1,0:T(8,128)(2,1)S(1)}, bf16[1,4,2,96,128]{4,3,2,1,0:T(8,128)(2,1)}, u32[]{:S(2)}) copy-start(bf16[1,4,2,96,128]{4,3,2,1,0:T(8,128)(2,1)} %video.3) | copy-start | bytes 589828
  0.0 1.8 %copy-start.6 = (f32[96]{0:T(128)S(1)}, f32[96]{0:T(128)}, u32[]{:S(2)}) copy-start(f32[96]{0:T(128)} %bias_second.1) | copy-start | bytes 1156
  0.0 1.8 %copy-start.2 = (bf16[96,2592]{1,0:T(8,128)(2,1)S(1)}, bf16[96,2592]{1,0:T(8,128)(2,1)}, u32[]{:S(2)}) copy-start(bf16[96,2592]{1,0:T(8,128)(2,1)} %kernel_second.1) | copy-start | bytes 1492996
  0.0 1.8 %copy-start.5 = (f32[96]{0:T(128)S(1)}, f32[96]{0:T(128)}, u32[]{:S(2)}) copy-start(f32[96]{0:T(128)} %gamma_second.1) | copy-start | bytes 1156
  0.0 1.8 %copy-start.4 = (f32[96]{0:T(128)S(1)}, f32[96]{0:T(128)}, u32[]{:S(2)}) copy-start(f32[96]{0:T(128)} %bias_first.1) | copy-start | bytes 1156
  0.0 1.8 %copy-start.1 = (bf16[96,2592]{1,0:T(8,128)(2,1)S(1)}, bf16[96,2592]{1,0:T(8,128)(2,1)}, u32[]{:S(2)}) copy-start(bf16[96,2592]{1,0:T(8,128)(2,1)} %kernel_first.1) | copy-start | bytes 1492996
  0.0 1.8 %copy-start.3 = (f32[96]{0:T(128)S(1)}, f32[96]{0:T(128)}, u32[]{:S(2)}) copy-start(f32[96]{0:T(128)} %gamma_first.1) | copy-start | bytes 1156
  0.0 5.4 %collective-permute-start = (bf16[1,4,2,96,128]{4,3,2,1,0:T(8,128)(2,1)}, bf16[1,4,2,96,128]{4,3,2,1,0:T(8,128)(2,1)S(1)}, u32[]{:S(2)}, u32[]{:S(2)}) collective-permute-start(bf16[1,4,2,96,128]{4,3,2,1,0:T(8,128)(2,1)} %video.3), channel_id=1, source_target_pairs={{0,1},{1,2},{2,3},{3,0},{4,5},{5,6},{6,7},{7,4},{8,9},{9,10},{10,1... | collective-permute-start | bytes 589832 | tf_op jit(solution)/shard_map/ppermute | solution.py:249
  0.1 8.0 %collective-permute-start.2 = (bf16[1,4,2,96,128]{4,3,2,1,0:T(8,128)(2,1)}, bf16[1,4,2,96,128]{4,3,2,1,0:T(8,128)(2,1)S(1)}, u32[]{:S(2)}, u32[]{:S(2)}) collective-permute-start(bf16[1,4,2,96,128]{4,3,2,1,0:T(8,128)(2,1)} %video.3), channel_id=1, source_target_pairs={{0,4},{1,5},{2,6},{3,7},{4,0},{5,1},{6,2},{7,3},{8,12},{9,13},{10,... | collective-permute-start | bytes 589832 | tf_op jit(solution)/shard_map/ppermute | solution.py:249
  1.8 7.9 %collective-permute-start.3 = (bf16[1,4,2,96,128]{4,3,2,1,0:T(8,128)(2,1)}, bf16[1,4,2,96,128]{4,3,2,1,0:T(8,128)(2,1)S(1)}, u32[]{:S(2)}, u32[]{:S(2)}) collective-permute-start(bf16[1,4,2,96,128]{4,3,2,1,0:T(8,128)(2,1)} %video.3), channel_id=1, source_target_pairs={{0,1},{1,0},{2,3},{3,2},{4,8},{5,9},{6,10},{7,11},{8,4},{9,5},{10,... | collective-permute-start | bytes 589832 | tf_op jit(solution)/shard_map/ppermute | solution.py:249
  5.6 6.4 %collective-permute-start.4 = (bf16[4,2,96,128]{3,2,1,0:T(8,128)(2,1)S(1)}, bf16[4,2,96,128]{3,2,1,0:T(8,128)(2,1)S(1)}, u32[]{:S(2)}, u32[]{:S(2)}) collective-permute-start(bf16[4,2,96,128]{3,2,1,0:T(8,128)(2,1)S(1)} %shard_map.75.inner), channel_id=1, source_target_pairs={{0,16},{1,5},{2,6},{3,7},{4,20},{5,1},{6,2},{7,3},{8,24},{9,13},{1... | collective-permute-start | bytes 589832 | tf_op jit(solution)/shard_map/ppermute | solution.py:249
  7.2 6.1 %collective-permute-start.1 = (bf16[4,2,96,128]{3,2,1,0:T(8,128)(2,1)S(1)}, bf16[4,2,96,128]{3,2,1,0:T(8,128)(2,1)S(1)}, u32[]{:S(2)}, u32[]{:S(2)}) collective-permute-start(bf16[4,2,96,128]{3,2,1,0:T(8,128)(2,1)S(1)} %shard_map.75.inner), channel_id=1, source_target_pairs={{0,1},{1,0},{2,3},{3,2},{4,20},{5,9},{6,10},{7,11},{8,24},{9,5},{1... | collective-permute-start | bytes 589832 | tf_op jit(solution)/shard_map/ppermute | solution.py:249
